TPU v7x, 32 devices: a whole 2x2x4 slice. The times are simulated.
32 devices in a mesh: dp: 8 (over y, x, core), seq: 4 (over z).
Axes of the slice: x: 2, y: 2, z: 4, core: 2. Of those that a mesh axis runs over, the one named last changes fastest.
Arguments:
- tokens: bfloat16 [16, 1024, 1024], P('dp', 'seq'), may hold values from -6 to 6
- cotangent: bfloat16 [16, 1024, 1024], P('dp', 'seq'), may hold values from -6 to 6
- lengths: int32 [16, 4], P('dp'), may hold values from 1 to 1021, as said below
- owners: int32 [192], replicated, may hold values from 0 to 7, as said below
- masters: float32 [256, 131072], P('dp', 'seq'), may hold values from -0.75 to 0.75
- first_moment: float32 [256, 131072], P('dp', 'seq'), may hold values from -320 to 320
- second_moment: float32 [256, 131072], P('dp', 'seq'), may hold values from 204.8 to 819.2
- small_params: float32 [14336], P(('dp', 'seq')), may hold values from -0.8 to 1.4
- small_first: float32 [14336], P(('dp', 'seq')), may hold values from -640 to 640
- small_second: float32 [14336], P(('dp', 'seq')), may hold values from 819.2 to 3276.8
Outputs:
- outputs: bfloat16 [16, 1024, 1024], P('dp', 'seq')
- grad_in: bfloat16 [16, 1024, 1024], P('dp', 'seq')
- new_masters: float32 [256, 131072], P('dp', 'seq')
- new_first: float32 [256, 131072], P('dp', 'seq')
- new_second: float32 [256, 131072], P('dp', 'seq')
- new_low: bfloat16 [256, 131072], P('dp', 'seq')
- small_new: float32 [14336], P(('dp', 'seq'))
- small_first_new: float32 [14336], P(('dp', 'seq'))
- small_second_new: float32 [14336], P(('dp', 'seq'))
Inputs may be any that keep to these rules, and one draw needn't show every extreme that they name: Each row's 4 lengths sum to 1024; all but one, at a place drawn per row, are at most 64; in some row all those others are 1. `owners`: no index owns more than 32 blocks, and some index owns exactly 32.
All inputs are finite; a program needn't handle non-finite values.
Results may differ from a plain program's by a relative error of at most 0.018.
Values may be sent and summed in bfloat16 or wider, within the bound.
No kernel may reach another device: no remote copies, remote signals or barrier semaphores. Data moves between devices by JAX's collectives and lax.ppermute only.
A program may use at most 512 MiB of HBM per device.

v0:
```python
import jax
import jax.numpy as jnp
from jax import lax
from jax.sharding import PartitionSpec as P

HEADS = 16
HD = 64
ROT = 32
FF = 4096
LAYERS = 2
STEP = 10


norm_epsilon = 1e-05
gelu_coeff = 0.7978845608
gelu_cubic = 0.044715
beta_first = 0.9
beta_second = 0.999
learn_rate = 0.05
small_rate = 0.3
decay_rate = 0.1
adam_epsilon = 1e-08


def gelu_tanh(values):
    return (
        0.5
        * values
        * (1.0 + jnp.tanh(gelu_coeff * (values + gelu_cubic * values * values * values)))
    )


def gelu_slope(values):
    tanh_part = jnp.tanh(gelu_coeff * (values + gelu_cubic * values * values * values))
    return 0.5 * (1.0 + tanh_part) + 0.5 * values * (1.0 - tanh_part * tanh_part) * gelu_coeff * (
        1.0 + 3.0 * gelu_cubic * values * values
    )


def token_tables(lengths, length):
    ends = jnp.cumsum(lengths, axis=1)
    starts = ends - lengths
    places = jnp.arange(length, dtype=jnp.int32)
    segment = jnp.sum((places[None, :, None] >= ends[:, None, :]).astype(jnp.int32), axis=2)
    owner_hit = segment[:, :, None] == jnp.arange(lengths.shape[1], dtype=jnp.int32)[None, None, :]
    first = jnp.sum(jnp.where(owner_hit, starts[:, None, :], 0), axis=2)
    return (segment, places[None, :] - first)


def rotate(projected, cosines, sines):
    half = ROT // 2
    pair = projected[:, :, :2]
    first = pair[..., :half]
    second = pair[..., half:ROT]
    cos_b = cosines[:, :, None, None, :]
    sin_b = sines[:, :, None, None, :]
    turned = jnp.concatenate(
        [first * cos_b - second * sin_b, second * cos_b + first * sin_b, pair[..., ROT:]], axis=-1
    )
    return jnp.concatenate([turned, projected[:, :, 2:]], axis=2)


def rotate_back(grads, cosines, sines):
    half = ROT // 2
    pair = grads[:, :, :2]
    first = pair[..., :half]
    second = pair[..., half:ROT]
    cos_b = cosines[:, :, None, None, :]
    sin_b = sines[:, :, None, None, :]
    turned = jnp.concatenate(
        [first * cos_b + second * sin_b, second * cos_b - first * sin_b, pair[..., ROT:]], axis=-1
    )
    return jnp.concatenate([turned, grads[:, :, 2:]], axis=2)


def mask_for(segment_row):
    places = jnp.arange(segment_row.shape[0])
    return (places[None, :] <= places[:, None]) & (segment_row[:, None] == segment_row[None, :])


def split_row(heads_row):
    length = heads_row.shape[0]
    per_dev = heads_row.shape[-1]
    local_heads = per_dev // HD
    queries = heads_row[:, 0, 0].reshape(length, local_heads, HD)
    key_rows = heads_row[:, 1, 0].reshape(length, local_heads, HD)
    value_rows = heads_row[:, 2, 0].reshape(length, local_heads, HD)
    return (queries, key_rows, value_rows)


def masked_scores(queries, key_rows, segment_row):
    scores = jnp.einsum(
        "qhd,khd->hqk", queries, key_rows, preferred_element_type=jnp.float32
    ) * HD ** (-0.5)
    return jnp.where(mask_for(segment_row)[None], scores, -1e30)


def attend_row(packed):
    heads_row, segment_row = packed
    queries, key_rows, value_rows = split_row(heads_row)
    scores = masked_scores(queries, key_rows, segment_row)
    top = jnp.max(scores, axis=-1, keepdims=True)
    log_total = top[..., 0] + jnp.log(jnp.sum(jnp.exp(scores - top), axis=-1))
    probs = jnp.exp(scores - log_total[..., None]).astype(jnp.bfloat16)
    context = jnp.einsum("hqk,khd->qhd", probs, value_rows, preferred_element_type=jnp.float32)
    return (
        context.astype(jnp.bfloat16).reshape(heads_row.shape[0], heads_row.shape[-1]),
        log_total,
    )


def attend_back(packed):
    heads_row, d_row, log_total, segment_row = packed
    length = heads_row.shape[0]
    per_dev = heads_row.shape[-1]
    queries, key_rows, value_rows = split_row(heads_row)
    scores = masked_scores(queries, key_rows, segment_row)
    probs_full = jnp.exp(scores - log_total[..., None])
    probs = probs_full.astype(jnp.bfloat16)
    d_context = d_row[:, 0].reshape(length, per_dev // HD, HD)
    d_values = jnp.einsum(
        "hqk,qhd->khd", probs, d_context, preferred_element_type=jnp.float32
    ).astype(jnp.bfloat16)
    d_probs = jnp.einsum("qhd,khd->hqk", d_context, value_rows, preferred_element_type=jnp.float32)
    weighted = jnp.sum(probs_full * d_probs, axis=-1, keepdims=True)
    d_scores = (probs_full * (d_probs - weighted)).astype(jnp.bfloat16)
    d_queries = (
        jnp.einsum("hqk,khd->qhd", d_scores, key_rows, preferred_element_type=jnp.float32)
        * HD ** (-0.5)
    ).astype(jnp.bfloat16)
    d_keys = (
        jnp.einsum("hqk,qhd->khd", d_scores, queries, preferred_element_type=jnp.float32)
        * HD ** (-0.5)
    ).astype(jnp.bfloat16)
    return jnp.stack([d_queries, d_keys, d_values], axis=1).reshape(length, 3, 1, per_dev)


def layer_weights(blocks, small_all, layer, width):
    per_layer = 4 * width * width + 2 * width * FF
    start = layer * per_layer
    w_qkv = blocks[start : start + 3 * width * width].reshape(width, 3 * width)
    start = start + 3 * width * width
    w_out = blocks[start : start + width * width].reshape(width, width)
    start = start + width * width
    w_in = blocks[start : start + width * FF].reshape(width, FF)
    start = start + width * FF
    w_down = blocks[start : start + width * FF].reshape(FF, width)
    base = layer * (3 * width + FF)
    small_f = small_all[base : base + 3 * width + FF].astype(jnp.float32)
    gain = small_f[:width]
    shift = small_f[width : 2 * width]
    bias_in = small_f[2 * width : 2 * width + FF]
    bias_out = small_f[2 * width + FF :]
    return (w_qkv, w_out, w_in, w_down, gain, shift, bias_in, bias_out)


def adam_update(weights, grads, moment_one, moment_two, rate, decay):
    new_one = beta_first * moment_one + (1.0 - beta_first) * grads
    new_two = beta_second * moment_two + (1.0 - beta_second) * grads * grads
    corrected_one = new_one / (1.0 - beta_first**STEP)
    corrected_two = new_two / (1.0 - beta_second**STEP)
    new_weights = weights - rate * (
        corrected_one / (jnp.sqrt(corrected_two) + adam_epsilon) + decay * weights
    )
    return (new_weights, new_one, new_two)


def body(
    tokens,
    cotangent,
    lengths,
    owners,
    masters,
    first_moment,
    second_moment,
    small_params,
    small_first,
    small_second,
):
    n_data = lax.axis_size("dp")
    n_seq = lax.axis_size("seq")
    capacity, piece = masters.shape
    unit = piece * n_seq
    n_blocks = owners.shape[0]
    rows_here, local, width = tokens.shape
    length = local * n_seq
    per_dev = width // n_seq
    block_index = jnp.arange(n_blocks, dtype=jnp.int32)
    same_owner = owners[:, None] == owners[None, :]
    earlier = block_index[None, :] < block_index[:, None]
    slot_rank = jnp.sum((same_owner & earlier).astype(jnp.int32), axis=1)
    slot_of_block = owners * capacity + slot_rank
    low_masters = masters.astype(jnp.bfloat16)
    low_small = small_params.astype(jnp.bfloat16)
    by_seq, small_seq = (
        lax.all_gather(low_masters, "seq", axis=1, tiled=True),
        lax.all_gather(low_small, "seq", axis=0, tiled=True),
    )
    gathered, small_all = (
        lax.all_gather(by_seq, "dp", axis=0, tiled=True),
        lax.all_gather(small_seq, "dp", axis=0, tiled=True),
    )
    blocks = gathered[slot_of_block].reshape(-1)
    segment, within = token_tables(lengths, length)
    mine = lax.dynamic_slice_in_dim(within, lax.axis_index("seq") * local, local, axis=1)
    inverse = 1.0 / 10000.0 ** (jnp.arange(0, ROT, 2, dtype=jnp.float32) / ROT)
    angle = mine.astype(jnp.float32)[..., None] * inverse
    cosines = jnp.cos(angle)
    sines = jnp.sin(angle)
    state = tokens.astype(jnp.float32)
    stored = []
    for layer in range(LAYERS):
        w_qkv, w_out, w_in, w_down, gain, shift, bias_in, bias_out = layer_weights(
            blocks, small_all, layer, width
        )
        centered = state - jnp.mean(state, axis=-1, keepdims=True)
        inv_std = lax.rsqrt(jnp.mean(centered * centered, axis=-1, keepdims=True) + norm_epsilon)
        normed = centered * inv_std
        hidden = (normed * gain + shift).astype(jnp.bfloat16)
        projected = jnp.dot(hidden, w_qkv, preferred_element_type=jnp.float32).reshape(
            rows_here, local, 3, HEADS, HD
        )
        rotated = (
            rotate(projected, cosines, sines)
            .astype(jnp.bfloat16)
            .reshape(rows_here, local, 3, n_seq, per_dev)
        )
        heads = lax.all_to_all(rotated, "seq", split_axis=3, concat_axis=1, tiled=True)
        context_heads, log_total = lax.map(attend_row, (heads, segment))
        context = lax.all_to_all(context_heads, "seq", split_axis=1, concat_axis=2, tiled=True)
        attended = jnp.dot(context, w_out, preferred_element_type=jnp.float32)
        inner = jnp.dot(hidden, w_in, preferred_element_type=jnp.float32) + bias_in
        activated = gelu_tanh(inner).astype(jnp.bfloat16)
        branch = jnp.dot(activated, w_down, preferred_element_type=jnp.float32) + bias_out
        stored.append((normed, inv_std, hidden, heads, log_total, context, inner, activated))
        state = state + attended + branch
    outputs = state.astype(jnp.bfloat16)
    d_state = cotangent.astype(jnp.float32)
    big_grads = [None] * LAYERS
    small_grads = [None] * LAYERS
    for layer in reversed(range(LAYERS)):
        w_qkv, w_out, w_in, w_down, gain, shift, bias_in, bias_out = layer_weights(
            blocks, small_all, layer, width
        )
        normed, inv_std, hidden, heads, log_total, context, inner, activated = stored[layer]
        d_branch = d_state.astype(jnp.bfloat16)
        flat_branch = d_branch.reshape(-1, width)
        flat_hidden = hidden.reshape(-1, width)
        g_down = jnp.dot(
            activated.reshape(-1, FF).T, flat_branch, preferred_element_type=jnp.float32
        )
        g_out = jnp.dot(
            context.reshape(-1, width).T, flat_branch, preferred_element_type=jnp.float32
        )
        g_bias_out = jnp.sum(d_branch.astype(jnp.float32), axis=(0, 1))
        d_active = jnp.dot(d_branch, w_down.T, preferred_element_type=jnp.float32)
        d_inner = (d_active * gelu_slope(inner)).astype(jnp.bfloat16)
        g_in = jnp.dot(flat_hidden.T, d_inner.reshape(-1, FF), preferred_element_type=jnp.float32)
        g_bias_in = jnp.sum(d_inner.astype(jnp.float32), axis=(0, 1))
        d_context = jnp.dot(d_branch, w_out.T, preferred_element_type=jnp.float32).astype(
            jnp.bfloat16
        )
        d_context = d_context.reshape(rows_here, local, n_seq, per_dev)
        d_heads = lax.all_to_all(d_context, "seq", split_axis=2, concat_axis=1, tiled=True)
        d_qkv_heads = lax.map(attend_back, (heads, d_heads, log_total, segment))
        d_qkv = lax.all_to_all(d_qkv_heads, "seq", split_axis=1, concat_axis=3, tiled=True)
        d_projected = rotate_back(
            d_qkv.astype(jnp.float32).reshape(rows_here, local, 3, HEADS, HD), cosines, sines
        )
        d_projected = d_projected.astype(jnp.bfloat16).reshape(rows_here, local, 3 * width)
        g_qkv = jnp.dot(
            flat_hidden.T, d_projected.reshape(-1, 3 * width), preferred_element_type=jnp.float32
        )
        d_hidden = jnp.dot(d_inner, w_in.T, preferred_element_type=jnp.float32)
        d_hidden = d_hidden + jnp.dot(d_projected, w_qkv.T, preferred_element_type=jnp.float32)
        g_gain = jnp.sum(d_hidden * normed, axis=(0, 1))
        g_shift = jnp.sum(d_hidden, axis=(0, 1))
        d_normed = d_hidden * gain
        d_state = d_state + inv_std * (
            d_normed
            - jnp.mean(d_normed, axis=-1, keepdims=True)
            - normed * jnp.mean(d_normed * normed, axis=-1, keepdims=True)
        )
        big_grads[layer] = jnp.concatenate(
            [g_qkv.reshape(-1), g_out.reshape(-1), g_in.reshape(-1), g_down.reshape(-1)]
        )
        small_grads[layer] = jnp.concatenate([g_gain, g_shift, g_bias_in, g_bias_out])
    grad_in = d_state.astype(jnp.bfloat16)
    flat_grads = jnp.concatenate(big_grads)
    small_flat = jnp.concatenate(small_grads)
    slot_ids = jnp.arange(n_data * capacity, dtype=jnp.int32)
    hit = slot_of_block[None, :] == slot_ids[:, None]
    block_of_slot = jnp.sum(jnp.where(hit, block_index[None, :], 0), axis=1) + jnp.where(
        jnp.any(hit, axis=1), 0, n_blocks
    )
    padded = jnp.concatenate(
        [flat_grads.reshape(n_blocks, unit), jnp.zeros((1, unit), jnp.float32)], axis=0
    )
    term = padded[block_of_slot]
    small_order = small_flat.reshape(n_data, n_seq, -1).transpose(1, 0, 2).reshape(-1)
    part_big, part_small = (
        lax.psum_scatter(term.astype(jnp.bfloat16), "seq", scatter_dimension=1, tiled=True).astype(
            jnp.float32
        ),
        lax.psum_scatter(
            small_order.astype(jnp.bfloat16), "seq", scatter_dimension=0, tiled=True
        ).astype(jnp.float32),
    )
    owned, small_owned = (
        lax.psum_scatter(
            part_big.astype(jnp.bfloat16), "dp", scatter_dimension=0, tiled=True
        ).astype(jnp.float32),
        lax.psum_scatter(
            part_small.astype(jnp.bfloat16), "dp", scatter_dimension=0, tiled=True
        ).astype(jnp.float32),
    )
    new_masters, new_first, new_second = adam_update(
        masters, owned, first_moment, second_moment, learn_rate, decay_rate
    )
    small_new, small_first_new, small_second_new = adam_update(
        small_params, small_owned, small_first, small_second, small_rate, 0.0
    )
    return (
        outputs,
        grad_in,
        new_masters,
        new_first,
        new_second,
        new_masters.astype(jnp.bfloat16),
        small_new,
        small_first_new,
        small_second_new,
    )


def solution(mesh):
    placed = (
        P("dp", "seq", None),
        P("dp", "seq", None),
        P("dp", None),
        P(),
        P("dp", "seq"),
        P("dp", "seq"),
        P("dp", "seq"),
        P(("dp", "seq")),
        P(("dp", "seq")),
        P(("dp", "seq")),
    )
    return jax.shard_map(
        body,
        mesh=mesh,
        in_specs=placed,
        out_specs=(
            P("dp", "seq", None),
            P("dp", "seq", None),
            P("dp", "seq"),
            P("dp", "seq"),
            P("dp", "seq"),
            P("dp", "seq"),
            P(("dp", "seq")),
            P(("dp", "seq")),
            P(("dp", "seq")),
        ),
        check_vma=False,
    )
```

profile of v0, /device:TPU:0, one launch (start us, length us, event | category | flops | bytes accessed | tf_op | source)
XLA Modules:
  0.0 2960.7 jit_solution(2474750659011372110)
XLA Ops:
  11.0 152.4 %all-gather.4.cloned.1.call-done = bf16[32,131072]{1,0:T(8,128)(2,1)} async-done(((bf16[32,32768]{1,0:T(8,128)(2,1)}), bf16[32,131072]{1,0:T(8,128)(2,1)}) %all-gather.4.cloned.1.call-update) | async-done | bytes 8388624 | tf_op jit(solution)/shard_map/all_gather | solution.py:196
  165.1 8.6 all-reduce.1
  173.7 9.4 all-gather
  189.7 276.7 %all-gather.6.cloned.1.call-done = bf16[256,131072]{1,0:T(8,128)(2,1)} async-done(((bf16[32,131072]{1,0:T(8,128)(2,1)}), bf16[256,131072]{1,0:T(8,128)(2,1)}) %all-gather.6.cloned.1.call-update) | async-done | bytes 67108880 | tf_op jit(solution)/shard_map/all_gather | solution.py:200
  466.4 43.9 %fusion.85 = (bf16[256,65536]{1,0:T(8,128)(2,1)}, bf16[256,65536]{1,0:T(8,128)(2,1)}) fusion(bf16[256,131072]{1,0:T(8,128)(2,1)} %all-gather.6.cloned.1.call-done), kind=kLoop, calls=%fused_computation.222 | loop fusion | bytes 134217728 | tf_op jit(solution)/shard_map/gather | solution.py:203
  510.3 46.7 %gather_fusion = bf16[192,65536]{1,0:T(8,128)(2,1)} fusion(bf16[256,65536]{1,0:T(8,128)(2,1)} %get-tuple-element.289, s32[1024]{0:T(1024)S(1)} %pad_clamp_fusion.1), kind=kCustom, calls=%fused_computation | custom fusion | bytes 50332416 | tf_op jit(solution)/shard_map/gather | solution.py:203
  557.0 20.5 constant_dynamic-update-slice_fusion.3
  577.5 47.3 %gather_fusion.1 = bf16[192,65536]{1,0:T(8,128)(2,1)} fusion(bf16[256,65536]{1,0:T(8,128)(2,1)} %get-tuple-element.288, s32[1024]{0:T(1024)S(1)} %pad_clamp_fusion.1), kind=kCustom, calls=%fused_computation.1 | custom fusion | bytes 50332416 | tf_op jit(solution)/shard_map/gather | solution.py:203
  624.7 20.4 constant_dynamic-update-slice_fusion.2
  645.1 22.6 fusion.88
  667.8 10.4 fusion.87
  678.1 14.8 reshape.529
  693.0 8.7 copy.233
  720.4 8.9 reshape.602
  733.2 11.5 fusion.101
  744.7 42.2 %all-to-all-done = bf16[2,256,3,4,256]{1,4,2,0,3:T(8,128)(2,1)S(1)} async-done(((bf16[2,256,3,4,256]{1,4,2,0,3:T(8,128)(2,1)}), bf16[2,256,3,4,256]{1,4,2,0,3:T(8,128)(2,1)S(1)}, u32[]{:S(2)}, u32[]{:S(2)}) %all-to-all-start) | async-done | bytes 3145760 | tf_op jit(solution)/shard_map/all_to_all | solution.py:228
  794.0 27.1 while.44
  833.4 8.9 reshape.603
  846.2 14.7 reshape.533
  860.9 8.9 copy.240
  870.9 12.4 fusion.72
  919.8 14.7 reshape.609
  934.5 8.9 reshape.608
  943.4 9.0 reshape.607
  952.9 35.6 %all-to-all-done.2 = bf16[2,256,3,4,256]{1,4,2,0,3:T(8,128)(2,1)} async-done(((bf16[2,256,3,4,256]{1,4,2,0,3:T(8,128)(2,1)}), bf16[2,256,3,4,256]{1,4,2,0,3:T(8,128)(2,1)}, u32[]{:S(2)}, u32[]{:S(2)}) %all-to-all-start.2) | async-done | bytes 3145760 | tf_op jit(solution)/shard_map/all_to_all | solution.py:228
  997.9 27.9 while.45
  1027.9 85.4 %while.46 = (s32[]{:T(128)}, bf16[2,1024,3,1,256]{1,4,3,2,0:T(8,128)(2,1)}, bf16[2,1024,3,1,256]{1,4,2,3,0:T(8,128)(2,1)}, s32[2,1024]{1,0:T(2,128)S(1)}, f32[2,...) while((s32[]{:T(128)}, bf16[2,1024,3,1,256]{1,4,3,2,0:T(8,128)(2,1)}, ...), condition=%wide.region_18.19_spmd, body=%wide.region_16.18_spmd.sunk | while | flops 2731274240 | bytes 180777328 | solution.py:265
  1036.7 11.2 multiply_reduce_fusion.9
  1047.9 8.5 fusion.250
  1056.4 7.9 multiply_convert_fusion.10
  1079.3 11.2 multiply_reduce_fusion.9
  1090.5 8.5 fusion.250
  1099.0 7.9 multiply_convert_fusion.10
  1113.3 9.1 copy.251
  1135.0 13.8 fusion.98
  1157.6 9.5 copy.299
  1167.1 10.5 fusion.103
  1181.3 15.0 all-to-all-done.5
  1229.7 13.5 convolution_bitcast_fusion
  1243.2 8.8 copy.300
  1260.7 83.3 %while.47 = (s32[]{:T(128)}, bf16[2,1024,3,1,256]{1,4,3,2,0:T(8,128)(2,1)}, bf16[2,1024,3,1,256]{1,4,2,3,0:T(8,128)(2,1)}, s32[2,1024]{1,0:T(2,128)S(1)}, f32[2,...) while((s32[]{:T(128)}, bf16[2,1024,3,1,256]{1,4,3,2,0:T(8,128)(2,1)}, ...), condition=%wide.region_23.24_spmd, body=%wide.region_21.23_spmd.sunk | while | flops 2731274240 | bytes 180646224 | solution.py:265
  1268.5 11.2 multiply_reduce_fusion.10
  1279.7 8.5 fusion.266
  1288.2 7.9 multiply_convert_fusion.11
  1309.9 11.2 multiply_reduce_fusion.10
  1321.2 8.5 fusion.266
  1329.6 7.9 multiply_convert_fusion.11
  1344.0 8.8 copy.259
  1357.7 13.6 fusion.97
  1385.0 9.5 copy.293
  1394.6 13.3 convolution_bitcast_fusion.1
  1407.8 8.9 copy.294
  1478.8 48.5 %reshape.553 = bf16[192,131072]{1,0:T(8,128)(2,1)} reshape(bf16[25165824]{0:T(1024)(128)(2,1)} %constant_dynamic-update-slice_fusion.6) | data formatting | bytes 100663296 | tf_op jit(solution)/shard_map/reshape | solution.py:297
  1527.3 34.0 %pad_slice_fusion = (bf16[193,65536]{1,0:T(8,128)(2,1)}, bf16[193,65536]{1,0:T(8,128)(2,1)}) fusion(bf16[192,131072]{1,0:T(8,128)(2,1)} %reshape.553), kind=kLoop, calls=%fused_computation.71 | loop fusion | bytes 100925440 | tf_op jit(solution)/shard_map/gather | solution.py:299
  1561.3 60.9 %gather_fusion.3 = bf16[256,65536]{1,0:T(8,128)(2,1)} fusion(bf16[193,65536]{1,0:T(8,128)(2,1)} %get-tuple-element.291, s32[1024]{0:T(1024)S(1)} %copy-done.88), kind=kCustom, calls=%fused_computation.3 | custom fusion | bytes 67109888 | tf_op jit(solution)/shard_map/gather | solution.py:299
  1622.2 61.0 %gather_fusion.2 = bf16[256,65536]{1,0:T(8,128)(2,1)} fusion(bf16[193,65536]{1,0:T(8,128)(2,1)} %get-tuple-element.290, s32[1024]{0:T(1024)S(1)} %copy-done.88), kind=kCustom, calls=%fused_computation.2 | custom fusion | bytes 67109888 | tf_op jit(solution)/shard_map/gather | solution.py:299
  1683.2 44.1 %maximum_convert_fusion = bf16[256,131072]{1,0:T(8,128)(2,1)} fusion(bf16[256,65536]{1,0:T(8,128)(2,1)} %gather_fusion.3, bf16[256,65536]{1,0:T(8,128)(2,1)} %gather_fusion.2), kind=kLoop, calls=%fused_computation.70 | loop fusion | flops 134217728 | bytes 134217728 | tf_op jit(solution)/shard_map/convert_element_type | solution.py:302
  1727.8 1093.9 %reduce-scatter.3.cloned.1.call-done = bf16[256,32768]{1,0:T(8,128)(2,1)} async-done(((bf16[256,131072]{1,0:T(8,128)(2,1)}), bf16[256,32768]{1,0:T(8,128)(2,1)}) %reduce-scatter.3.cloned.1.call-update) | async-done | bytes 16777232 | tf_op jit(solution)/shard_map/reduce_scatter | solution.py:302
  2824.3 15.5 reshape.610
  2839.9 15.7 fusion.73
  2875.9 19.5 all-reduce.2
  2895.4 12.9 all-reduce.3
  2913.2 30.4 %reduce-scatter.5.cloned.1.call-done = bf16[32,32768]{1,0:T(8,128)(2,1)} async-done(((bf16[256,32768]{1,0:T(8,128)(2,1)}), bf16[32,32768]{1,0:T(8,128)(2,1)}) %reduce-scatter.5.cloned.1.call-update) | async-done | bytes 2097168 | tf_op jit(solution)/shard_map/reduce_scatter | solution.py:310
  2943.6 10.3 fusion.78
  (525 shorter events, 392.2 us)
Async XLA Ops:
  7.2 156.3 %all-gather.4.cloned.1.call-start = ((), (), s32[]{:S(2)}) async-start(), calls=%async_computation.10 | async-start | bytes 10485760 | tf_op jit(solution)/shard_map/all_gather | solution.py:196
  10.9 152.6 %copy-start.91 = (f32[448]{0:T(512)S(1)}, f32[448]{0:T(512)}, u32[]{:S(2)}) copy-start(f32[448]{0:T(512)} %param.25) | copy-start | bytes 5380
  10.9 152.6 %copy-start.101 = (u32[32]{0:T(128)S(1)}, u32[32]{0:T(128)}, u32[]{:S(2)}) copy-start(u32[32]{0:T(128)} %constant.177) | copy-start | bytes 388
  10.9 172.9 %copy-start.95 = (s32[2,4]{1,0:T(2,128)S(1)}, s32[2,4]{1,0:T(2,128)}, u32[]{:S(2)}) copy-start(s32[2,4]{1,0:T(2,128)} %param.20) | copy-start | bytes 100
  10.9 173.9 %copy-start.87 = (s32[192]{0:T(256)S(1)}, s32[192]{0:T(256)}, u32[]{:S(2)}) copy-start(s32[192]{0:T(256)} %param.21) | copy-start | bytes 2308
  10.9 174.7 %copy-start.6 = (bf16[2,256,1024]{2,1,0:T(8,128)(2,1)S(1)}, bf16[2,256,1024]{2,1,0:T(8,128)(2,1)}, u32[]{:S(2)}) copy-start(bf16[2,256,1024]{2,1,0:T(8,128)(2,1)} %param.18) | copy-start | bytes 3145732
  11.0 455.4 %all-gather.6.cloned.1.call-start = ((), (), s32[]{:S(2)}) async-start(), calls=%async_computation.11 | async-start | bytes 75497472 | tf_op jit(solution)/shard_map/all_gather | solution.py:200
  183.2 327.1 %copy-start.61 = (f32[4,1,1792]{2,1,0:T(1,128)}, f32[4,1,1792]{2,1,0:T(1,128)S(1)}, u32[]{:S(2)}) copy-start(f32[4,1,1792]{2,1,0:T(1,128)S(1)} %get-tuple-element.313) | copy-start | bytes 86020
  693.0 8.7 copy-start.38
  710.8 76.1 %all-to-all-start = ((bf16[2,256,3,4,256]{1,4,2,0,3:T(8,128)(2,1)}), bf16[2,256,3,4,256]{1,4,2,0,3:T(8,128)(2,1)S(1)}, u32[]{:S(2)}, u32[]{:S(2)}) async-start(bf16[2,256,3,4,256]{1,4,2,0,3:T(8,128)(2,1)} %pad_maximum_fusion), calls=%async_computation | async-start | bytes 6291456 | tf_op jit(solution)/shard_map/all_to_all | solution.py:228
  744.7 49.3 %copy-start.37 = (s32[2,1024]{1,0:T(2,128)S(1)}, s32[2,1024]{1,0:T(2,128)}, u32[]{:S(2)}) copy-start(s32[2,1024]{1,0:T(2,128)} %copy-done.36) | copy-start | bytes 24580
  821.0 21.3 copy-start.2
  821.1 21.3 copy-start.59
  824.9 58.4 %all-to-all-start.1 = ((bf16[2,1024,256]{2,0,1:T(2,128)(2,1)}), bf16[2,1024,256]{2,0,1:T(2,128)(2,1)}, u32[]{:S(2)}, u32[]{:S(2)}) async-start(bf16[2,1024,256]{2,0,1:T(2,128)(2,1)} %copy.238), calls=%async_computation.1 | async-start | bytes 2097152 | tf_op jit(solution)/shard_map/all_to_all | solution.py:230
  860.9 8.9 copy-start.45
  860.9 10.0 copy-start.83
  883.3 8.8 copy-start.7
  883.3 8.8 copy-start.98
  883.3 29.9 %all-to-all-start.4 = ((bf16[2,256,4,256]{1,3,0,2:T(8,128)(2,1)}), bf16[2,256,4,256]{1,3,0,2:T(8,128)(2,1)S(1)}, u32[]{:S(2)}, u32[]{:S(2)}) async-start(bf16[2,256,4,256]{1,3,0,2:T(8,128)(2,1)} %copy.247), calls=%async_computation.4 | async-start | bytes 2097152 | tf_op jit(solution)/shard_map/all_to_all | solution.py:264
  905.5 12.8 copy-start.62
  905.5 13.4 copy-start.96
  913.2 75.3 %all-to-all-start.2 = ((bf16[2,256,3,4,256]{1,4,2,0,3:T(8,128)(2,1)}), bf16[2,256,3,4,256]{1,4,2,0,3:T(8,128)(2,1)}, u32[]{:S(2)}, u32[]{:S(2)}) async-start(bf16[2,256,3,4,256]{1,4,2,0,3:T(8,128)(2,1)} %pad_maximum_fusion.1), calls=%async_computation.2 | async-start | bytes 6291456 | tf_op jit(solution)/shard_map/all_to_all | solution.py:228
  1047.9 8.5 copy-start.34
  1056.4 7.9 copy-start
  1090.5 8.5 copy-start.34
  1099.0 7.9 copy-start
  1122.4 73.8 %all-to-all-start.5 = ((bf16[2,1024,3,1,256]{4,0,3,2,1:T(2,128)(2,1)}), bf16[2,1024,3,1,256]{4,0,3,2,1:T(2,128)(2,1)S(1)}, u32[]{:S(2)}, u32[]{:S(2)}) async-start(bf16[2,1024,3,1,256]{4,0,3,2,1:T(2,128)(2,1)} %copy.251), calls=%async_computation.5 | async-start | bytes 6291456 | tf_op jit(solution)/shard_map/all_to_all | solution.py:266
  1126.1 8.9 copy-start.31
  1126.1 8.9 copy-start.85
  1133.5 15.3 copy-start.105
  1135.0 15.8 copy-start.42
  1196.2 29.7 %all-to-all-start.3 = ((bf16[2,1024,256]{2,0,1:T(2,128)(2,1)}), bf16[2,1024,256]{2,0,1:T(2,128)(2,1)}, u32[]{:S(2)}, u32[]{:S(2)}) async-start(bf16[2,1024,256]{2,0,1:T(2,128)(2,1)} %copy.245), calls=%async_computation.3 | async-start | bytes 2097152 | tf_op jit(solution)/shard_map/all_to_all | solution.py:230
  1208.0 8.2 copy-start.13
  1217.8 8.1 copy-start.46
  1226.0 32.6 %all-to-all-start.6 = ((bf16[2,256,4,256]{3,1,0,2:T(8,128)(2,1)}), bf16[2,256,4,256]{3,1,0,2:T(8,128)(2,1)S(1)}, u32[]{:S(2)}, u32[]{:S(2)}) async-start(bf16[2,256,4,256]{3,1,0,2:T(8,128)(2,1)} %bitcast.256), calls=%async_computation.6 | async-start | bytes 2097152 | tf_op jit(solution)/shard_map/all_to_all | solution.py:264
  1279.7 8.5 copy-start.35
  1288.2 7.9 copy-start.1
  1321.2 8.5 copy-start.35
  1329.6 7.9 copy-start.1
  1344.0 13.7 copy-start.84
  1352.8 74.8 %all-to-all-start.7 = ((bf16[2,1024,3,1,256]{4,0,3,2,1:T(2,128)(2,1)}), bf16[2,1024,3,1,256]{4,0,3,2,1:T(2,128)(2,1)}, u32[]{:S(2)}, u32[]{:S(2)}) async-start(bf16[2,1024,3,1,256]{4,0,3,2,1:T(2,128)(2,1)} %copy.259), calls=%async_computation.7 | async-start | bytes 6291456 | tf_op jit(solution)/shard_map/all_to_all | solution.py:266
  1357.7 13.6 copy-start.14
  1357.7 1464.0 %reduce-scatter.3.cloned.1.call-start = ((), (), s32[]{:S(2)}) async-start(), calls=%async_computation.12 | async-start | bytes 83886080 | tf_op jit(solution)/shard_map/reduce_scatter | solution.py:302
  1385.0 9.5 copy-start.48
  1449.8 7.8 slice-start.6
  1453.4 9.2 slice-start.8
  1465.9 8.0 slice-start.2
  1527.3 34.0 %copy-start.88 = (s32[1024]{0:T(1024)S(1)}, s32[1024]{0:T(1024)}, u32[]{:S(2)}) copy-start(s32[1024]{0:T(1024)} %pad_clamp_fusion) | copy-start | bytes 12292
  1727.3 1216.2 %reduce-scatter.5.cloned.1.call-start = ((), (), s32[]{:S(2)}) async-start(), calls=%async_computation.13 | async-start | bytes 18874368 | tf_op jit(solution)/shard_map/reduce_scatter | solution.py:310
  2824.3 15.5 copy-start.86
  2839.9 15.8 copy-start.24
  2839.9 17.3 copy-start.5
  2839.9 17.3 copy-start.97
  2857.2 12.7 slice-start.12
  2862.1 7.8 copy-start.70
  2862.1 7.8 copy-start.75
  2870.0 38.4 %copy-start.92 = (f32[448]{0:T(512)S(1)}, f32[448]{0:T(512)}, u32[]{:S(2)}) copy-start(f32[448]{0:T(512)} %param.25) | copy-start | bytes 5380
  2870.0 38.4 %copy-start.99 = (f32[448]{0:T(512)S(1)}, f32[448]{0:T(512)}, u32[]{:S(2)}) copy-start(f32[448]{0:T(512)} %param.26) | copy-start | bytes 5380
  2870.0 38.4 %copy-start.100 = (f32[448]{0:T(512)S(1)}, f32[448]{0:T(512)}, u32[]{:S(2)}) copy-start(f32[448]{0:T(512)} %param.27) | copy-start | bytes 5380
  2870.1 39.0 %copy-start.65 = (f32[1024]{0:T(1024)S(1)}, f32[1024]{0:T(1024)}, u32[]{:S(2)}) copy-start(f32[1024]{0:T(1024)} %get-tuple-element.317) | copy-start | bytes 12292
  2870.1 39.0 %copy-start.68 = (f32[2,256]{1,0:T(2,128)S(1)}, f32[2,256]{1,0:T(2,128)}, u32[]{:S(2)}) copy-start(f32[2,256]{1,0:T(2,128)} %copy-done.66) | copy-start | bytes 6148
  2870.1 39.0 %copy-start.73 = (f32[2,256]{1,0:T(2,128)S(1)}, f32[2,256]{1,0:T(2,128)}, u32[]{:S(2)}) copy-start(f32[2,256]{1,0:T(2,128)} %copy-done.71) | copy-start | bytes 6148
  2870.1 39.0 %copy-start.77 = (f32[2,256]{1,0:T(2,128)S(1)}, f32[2,256]{1,0:T(2,128)}, u32[]{:S(2)}) copy-start(f32[2,256]{1,0:T(2,128)} %copy-done.76) | copy-start | bytes 6148
  2870.1 39.0 %copy-start.79 = (f32[2,256]{1,0:T(2,128)S(1)}, f32[2,256]{1,0:T(2,128)}, u32[]{:S(2)}) copy-start(f32[2,256]{1,0:T(2,128)} %copy-done.78) | copy-start | bytes 6148
  (89 other events, 330.6 us)
Sparse Core Ops, SparseCore 0:
  11.1 152.3 all-gather.3
  165.3 301.0 all-gather.5
  1727.5 1094.2 reduce-scatter.2
  2825.6 117.9 reduce-scatter.4
where the time goes:
time: 2970 us; the launch traced here: 2960 us
  waiting for transfers between devices  1660 us (56%)
  local copies, waits for them, and re-layouts  744 us (25%)
  matrix products  318 us (11%)
  other arithmetic  134 us (5%)
  blocking collectives  50.4 us (2%)
  starting transfers between devices  37 us (1%)
    reduce_scatter x1, waiting for transfers between devices, body(): lax.psum_scatter(term.astype(jnp.bfloat16), 'seq', scatter_dimension=1, t...  1090 us
    all_gather x1, waiting for transfers between devices, body(): lax.all_gather(by_seq, 'dp', axis=0, tiled=True)  277 us
    gather x3, local copies, waits for them, and re-layouts, body(): term = padded[block_of_slot]  156 us
    all_gather x1, waiting for transfers between devices, body(): lax.all_gather(low_masters, 'seq', axis=1, tiled=True)  152 us
    gather x3, local copies, waits for them, and re-layouts, body(): blocks = gathered[slot_of_block].reshape(-1)  138 us
    unnamed x248, local copies, waits for them, and re-layouts  132 us
    all_to_all x2, waiting for transfers between devices, body(): lax.all_to_all(rotated, 'seq', split_axis=3, concat_axis=1, tiled=True)  77.8 us
    reshape x4, local copies, waits for them, and re-layouts, layer_weights(): w_qkv = blocks[start:start + 3 * width * width].reshape(width, 3 * width)  59.7 us
  transfers between devices with their start and end apart: 12, of which 10 were waited for; matrix products, arithmetic and copies ran while one was open for 12% of the time, Pallas kernels for 0%

commit v1 on v0

v1 whole, which is shorter than its diff:
```python
import functools

import jax
import jax.numpy as jnp
import numpy as np
from jax import lax
from jax.experimental import pallas as pl
from jax.experimental.pallas import tpu as pltpu
from jax.sharding import PartitionSpec as P

HEADS = 16
HD = 64
ROT = 32
FF = 4096
LAYERS = 2
STEP = 10
TP = 4

norm_epsilon = 1e-05
gelu_coeff = 0.7978845608
gelu_cubic = 0.044715
beta_first = 0.9
beta_second = 0.999
learn_rate = 0.05
small_rate = 0.3
decay_rate = 0.1
adam_epsilon = 1e-08
BIG = 1e30
BF = jnp.bfloat16
F32 = jnp.float32


def gelu_tanh(values):
    return (
        0.5
        * values
        * (1.0 + jnp.tanh(gelu_coeff * (values + gelu_cubic * values * values * values)))
    )


def gelu_slope(values):
    tanh_part = jnp.tanh(gelu_coeff * (values + gelu_cubic * values * values * values))
    return 0.5 * (1.0 + tanh_part) + 0.5 * values * (1.0 - tanh_part * tanh_part) * gelu_coeff * (
        1.0 + 3.0 * gelu_cubic * values * values
    )


def dot(left, right):
    return jnp.dot(left, right, preferred_element_type=F32)


def dot_nt(left, right):
    return lax.dot_general(left, right, (((1,), (1,)), ((), ())), preferred_element_type=F32)


def dot_tn(left, right):
    return lax.dot_general(left, right, (((0,), (0,)), ((), ())), preferred_element_type=F32)


def rotate_lanes(x, cos_t, low_t, high_t, sign):
    halves = []
    for part in range(x.shape[1] // 128):
        v = x[:, 128 * part : 128 * (part + 1)]
        up = pltpu.roll(v, 128 - ROT // 2, 1)
        down = pltpu.roll(v, ROT // 2, 1)
        halves.append(v * cos_t + sign * (up * low_t + down * high_t))
    return jnp.concatenate(halves, axis=1)


def head_of(shape):
    return lax.broadcasted_iota(jnp.int32, shape, 1) // HD


def attend_kernel(proj_ref, tab_ref, qx_ref, kx_ref, ctx_ref, rot_ref, lse_ref, k_s, v_s, q_s):
    length, width = ctx_ref.shape
    heads = width // HD
    blk = min(256, length)
    cos_t, low_t, high_t = tab_ref[0], tab_ref[1], tab_ref[2]
    q = rotate_lanes(proj_ref[:, :width], cos_t, low_t, high_t, 1.0).astype(BF)
    k = rotate_lanes(proj_ref[:, width : 2 * width], cos_t, low_t, high_t, 1.0).astype(BF)
    v = proj_ref[:, 2 * width :].astype(BF)
    rot_ref[:, :width] = q
    rot_ref[:, width : 2 * width] = k
    rot_ref[:, 2 * width :] = v
    q = q * BF(HD**-0.5)
    head = head_of((length, width))
    zero = jnp.zeros((), BF)
    for h in range(heads):
        ext = (h + 1) % heads
        k_s[h] = jnp.where(head == h, k, jnp.where(head == ext, kx_ref[...], zero))
        v_s[h] = jnp.where(head == h, v, zero)
        q_s[h] = jnp.where(head == ext, qx_ref[...], q)
    tri = lax.broadcasted_iota(jnp.int32, (blk, blk), 0) <= lax.broadcasted_iota(
        jnp.int32, (blk, blk), 1
    )
    for i in range(length // blk):
        lo, hi = i * blk, (i + 1) * blk
        total = jnp.zeros((blk, width), F32)
        for h in range(heads):
            qb = q_s[h, lo:hi]
            diag = jnp.where(tri, dot_nt(k_s[h, lo:hi], qb), -BIG)
            top = jnp.max(diag, axis=0, keepdims=True)
            if i:
                past = dot_nt(k_s[h, :lo], qb)
                top = jnp.maximum(top, jnp.max(past, axis=0, keepdims=True))
            diag = jnp.exp(diag - top)
            mass = jnp.sum(diag, axis=0, keepdims=True)
            if i:
                past = jnp.exp(past - top)
                mass = mass + jnp.sum(past, axis=0, keepdims=True)
            lse_ref[h : h + 1, lo:hi] = top + jnp.log(mass)
            inv = 1.0 / mass
            total += dot_tn((diag * inv).astype(BF), v_s[h, lo:hi])
            if i:
                total += dot_tn((past * inv).astype(BF), v_s[h, :lo])
        ctx_ref[lo:hi] = total.astype(BF)


def attend_back_kernel(
    rot_ref, dctx_ref, lse_ref, tab_ref, qx_ref, kx_ref, out_ref, k_s, v_s, q_s, dk_s, dv_s, dq_s
):
    length, width = dctx_ref.shape
    heads = width // HD
    blk = min(256, length)
    head = head_of((length, width))
    zero = jnp.zeros((), BF)
    q = rot_ref[:, :width]
    k = rot_ref[:, width : 2 * width]
    v = rot_ref[:, 2 * width :]
    scaled = q * BF(HD**-0.5)
    for h in range(heads):
        ext = (h + 1) % heads
        k_s[h] = jnp.where(head == h, k, jnp.where(head == ext, kx_ref[...], zero))
        v_s[h] = jnp.where(head == h, v, zero)
        q_s[h] = jnp.where(head == ext, qx_ref[...], scaled)
    dk_s[...] = jnp.zeros_like(dk_s)
    dv_s[...] = jnp.zeros_like(dv_s)
    head_b = head_of((blk, width))
    tri = lax.broadcasted_iota(jnp.int32, (blk, blk), 0) <= lax.broadcasted_iota(
        jnp.int32, (blk, blk), 1
    )
    for i in range(length // blk):
        lo, hi = i * blk, (i + 1) * blk
        d_all = dctx_ref[lo:hi]
        q_all = rot_ref[lo:hi, :width]
        total = jnp.zeros((blk, width), F32)
        for h in range(heads):
            qb = q_s[h, lo:hi]
            d_h = jnp.where(head_b == h, d_all, zero)
            q_h = jnp.where(head_b == h, q_all, zero)
            lse = lse_ref[h : h + 1, lo:hi]
            p_d = jnp.exp(jnp.where(tri, dot_nt(k_s[h, lo:hi], qb), -BIG) - lse)
            g_d = dot_nt(v_s[h, lo:hi], d_all)
            delta = jnp.sum(p_d * g_d, axis=0, keepdims=True)
            if i:
                p_p = jnp.exp(dot_nt(k_s[h, :lo], qb) - lse)
                g_p = dot_nt(v_s[h, :lo], d_all)
                delta = delta + jnp.sum(p_p * g_p, axis=0, keepdims=True)
            s_d = (p_d * (g_d - delta)).astype(BF)
            dv_s[lo:hi] += dot(p_d.astype(BF), d_h)
            dk_s[lo:hi] += dot(s_d, q_h)
            k_d = jnp.where(head_b == h, rot_ref[lo:hi, width : 2 * width], zero)
            total += dot_tn(s_d, k_d)
            if i:
                s_p = (p_p * (g_p - delta)).astype(BF)
                dv_s[:lo] += dot(p_p.astype(BF), d_h)
                dk_s[:lo] += dot(s_p, q_h)
                k_p = jnp.where(head_of((lo, width)) == h, rot_ref[:lo, width : 2 * width], zero)
                total += dot_tn(s_p, k_p)
        dq_s[lo:hi] = total
    scale = HD**-0.5
    cos_t, low_t, high_t = tab_ref[0], tab_ref[1], tab_ref[2]
    for n, ref in ((0, dq_s), (1, dk_s)):
        low = (ref[...] * scale).astype(BF).astype(F32)
        out_ref[:, n * width : (n + 1) * width] = rotate_lanes(
            low, cos_t, low_t, high_t, -1.0
        ).astype(BF)
    out_ref[:, 2 * width :] = dv_s[...].astype(BF)


def attend(proj, tables, q_ext, k_ext):
    length, width = proj.shape[0], proj.shape[1] // 3
    heads = width // HD
    return pl.pallas_call(
        attend_kernel,
        out_shape=(
            jax.ShapeDtypeStruct((length, width), BF),
            jax.ShapeDtypeStruct((length, 3 * width), BF),
            jax.ShapeDtypeStruct((8, length), F32),
        ),
        scratch_shapes=[pltpu.VMEM((heads, length, width), BF)] * 3,
        compiler_params=pltpu.CompilerParams(vmem_limit_bytes=50 << 20),
        cost_estimate=pl.CostEstimate(
            flops=heads * length * length * width * 2,
            bytes_accessed=length * width * 24,
            transcendentals=heads * length * length // 2,
        ),
        name="attend",
    )(proj, tables, q_ext, k_ext)


def attend_back(rot, d_context, lse, tables, q_ext, k_ext):
    length, width = d_context.shape
    heads = width // HD
    return pl.pallas_call(
        attend_back_kernel,
        out_shape=jax.ShapeDtypeStruct((length, 3 * width), BF),
        scratch_shapes=[pltpu.VMEM((heads, length, width), BF)] * 3
        + [pltpu.VMEM((length, width), F32)] * 3,
        compiler_params=pltpu.CompilerParams(vmem_limit_bytes=50 << 20),
        cost_estimate=pl.CostEstimate(
            flops=heads * length * length * width * 5,
            bytes_accessed=length * width * 24,
            transcendentals=heads * length * length // 2,
        ),
        name="attend_back",
    )(rot, d_context, lse, tables, q_ext, k_ext)


@functools.lru_cache(maxsize=None)
def row_moves(n_seq, rows_here, length):
    local = length // n_seq
    per_dev = rows_here * local
    edges = {}
    for t in range(TP):
        for z in range(n_seq):
            for k in range(rows_here):
                row = rows_here * t + k
                token = (row // n_seq) * length + z * local
                target = (token // per_dev) * n_seq + row % n_seq
                edges.setdefault(t * n_seq + z, []).append((target, k, token % per_dev // local))
    steps = []
    for _ in range(rows_here):
        taken = {}

        def place(source, seen):
            for edge in edges[source]:
                if edge[0] not in seen:
                    seen.add(edge[0])
                    if edge[0] not in taken or place(taken[edge[0]][0], seen):
                        taken[edge[0]] = (source, edge)
                        return True
            return False

        for source in edges:
            assert place(source, set())
        pick = np.zeros(TP * n_seq, np.int32)
        put = np.zeros(TP * n_seq, np.int32)
        pairs = []
        for target, (source, edge) in taken.items():
            edges[source].remove(edge)
            pick[source] = edge[1]
            put[target] = edge[2]
            pairs.append((source, target))
        steps.append((sorted(pairs), pick, put))
    return steps


def adam_update(weights, grads, moment_one, moment_two, rate, decay):
    new_one = beta_first * moment_one + (1.0 - beta_first) * grads
    new_two = beta_second * moment_two + (1.0 - beta_second) * grads * grads
    corrected_one = new_one / (1.0 - beta_first**STEP)
    corrected_two = new_two / (1.0 - beta_second**STEP)
    new_weights = weights - rate * (
        corrected_one / (jnp.sqrt(corrected_two) + adam_epsilon) + decay * weights
    )
    return (new_weights, new_one, new_two)


def body(
    tokens,
    cotangent,
    lengths,
    owners,
    masters,
    first_moment,
    second_moment,
    small_params,
    small_first,
    small_second,
):
    n_dp = lax.axis_size("dp")
    n_seq = lax.axis_size("seq")
    n_g = n_dp // TP
    capacity, piece = masters.shape
    n_blocks = owners.shape[0]
    rows_here, local, width = tokens.shape
    length = local * n_seq
    per_dev = rows_here * local
    group_rows = TP * per_dev // length
    cols = width // TP
    chunks = piece // width // n_g
    place_dp = lax.axis_index("dp")
    place_z = lax.axis_index("seq")
    t = place_dp % TP
    g = place_dp // TP
    core, side = t % 2, t // 2
    groups = [[TP * a + b for b in range(TP)] for a in range(n_g)]
    across = [[TP * a + b for a in range(n_g)] for b in range(TP)]

    def swap(value, bit):
        return lax.ppermute(value, "dp", [(i, i ^ bit) for i in range(n_dp)])

    def order(first, second, flag):
        return jnp.concatenate(
            [jnp.where(flag == 0, first, second), jnp.where(flag == 0, second, first)], axis=0
        )

    steps = row_moves(n_seq, rows_here, length)

    def row_pairs(pairs, back):
        out = []
        for source, target in pairs:
            for a in range(n_g):
                ends = (a * TP * n_seq + source, a * TP * n_seq + target)
                out.append(ends[::-1] if back else ends)
        return out

    me = t * n_seq + place_z

    def to_rows(value):
        parts = []
        for pairs, pick, _ in steps:
            send = lax.dynamic_index_in_dim(value, jnp.asarray(pick)[me], 0, keepdims=False)
            parts.append(lax.ppermute(send, ("dp", "seq"), row_pairs(pairs, False)))
        puts = [jnp.asarray(put)[me] for _, _, put in steps]
        slots = []
        for s in range(rows_here):
            out = parts[0]
            for j in range(1, rows_here):
                out = jnp.where(puts[j] == s, parts[j], out)
            slots.append(out)
        return jnp.concatenate(slots, axis=0)

    def from_rows(value):
        value = value.reshape(rows_here, local, width)
        parts = []
        for pairs, _, put in steps:
            send = lax.dynamic_index_in_dim(value, jnp.asarray(put)[me], 0, keepdims=False)
            parts.append(lax.ppermute(send, ("dp", "seq"), row_pairs(pairs, True)))
        picks = [jnp.asarray(pick)[me] for _, pick, _ in steps]
        slots = []
        for s in range(rows_here):
            out = parts[0]
            for j in range(1, rows_here):
                out = jnp.where(picks[j] == s, parts[j], out)
            slots.append(out)
        return jnp.stack(slots, axis=0)

    block_index = jnp.arange(n_blocks, dtype=jnp.int32)
    same_owner = owners[:, None] == owners[None, :]
    earlier = block_index[None, :] < block_index[:, None]
    slot_rank = jnp.sum((same_owner & earlier).astype(jnp.int32), axis=1)
    slot_of_block = owners * capacity + slot_rank
    slot_ids = jnp.arange(n_dp * capacity, dtype=jnp.int32)
    hit = slot_of_block[None, :] == slot_ids[:, None]
    block_of_slot = jnp.sum(jnp.where(hit, block_index[None, :], 0), axis=1) + jnp.where(
        jnp.any(hit, axis=1), 0, n_blocks
    )

    packed = (
        masters.astype(BF)
        .reshape(capacity, n_g, chunks, TP, cols)
        .transpose(1, 3, 0, 2, 4)
        .reshape(n_dp, capacity, chunks, cols)
    )
    spread = lax.all_to_all(packed, "dp", split_axis=0, concat_axis=0, tiled=True)
    blocks = spread.reshape(n_dp * capacity, chunks, cols)[slot_of_block]

    small_all = lax.all_gather(small_params.astype(BF), ("dp", "seq"), axis=0, tiled=True)

    unit_rows = n_seq * n_g * chunks
    n_qkv = 3 * width // unit_rows
    n_out = width // unit_rows
    n_in = FF // unit_rows
    per_layer = n_qkv + n_out + 2 * n_in
    my_out = n_out // TP
    fold = FF // width

    def gather_blocks(value):
        by_z = lax.all_gather(value, "seq", axis=0)
        if n_g == 2:
            other = swap(by_z, TP)
            both = jnp.stack([jnp.where(g == 0, by_z, other), jnp.where(g == 0, other, by_z)])
        else:
            both = lax.all_gather(by_z, "dp", axis=0, axis_index_groups=across)
        units, rest = value.shape[0], value.shape[2]
        return both.transpose(2, 1, 0, 3, 4).reshape(units * unit_rows, rest)

    weights = []
    for layer in range(LAYERS):
        start = layer * per_layer
        mine = blocks[start : start + per_layer]
        w_qkv = gather_blocks(mine[:n_qkv]).reshape(width, 3 * cols)
        w_in = gather_blocks(mine[n_qkv + n_out : n_qkv + n_out + n_in]).reshape(width, fold * cols)
        outs = mine[n_qkv : n_qkv + n_out].reshape(TP, my_out, chunks, cols)
        downs = (
            mine[n_qkv + n_out + n_in :]
            .reshape(fold, TP, my_out, chunks, cols)
            .transpose(1, 0, 2, 3, 4)
            .reshape(TP, fold * my_out, chunks, cols)
        )
        both = lax.all_to_all(
            jnp.concatenate([outs, downs], axis=1),
            "dp",
            split_axis=0,
            concat_axis=0,
            tiled=True,
            axis_index_groups=groups,
        )
        both = both.transpose(1, 2, 0, 3).reshape((1 + fold) * my_out, chunks, width)
        both = gather_blocks(both)
        w_out, w_down = both[:cols], both[cols:]
        base = layer * (3 * width + FF)
        small_f = small_all[base : base + 3 * width + FF].astype(F32)
        gain = small_f[:width]
        shift = small_f[width : 2 * width]
        bias_in = lax.dynamic_index_in_dim(
            small_f[2 * width : 2 * width + FF].reshape(fold, TP, cols), t, 1, keepdims=False
        ).reshape(-1)
        bias_out = small_f[2 * width + FF :]
        weights.append((w_qkv, w_out, w_in, w_down, gain, shift, bias_in, bias_out))

    near = jnp.stack([lengths, swap(lengths, 1)])
    near = jnp.concatenate([near, swap(near, 2)])
    near = near[jnp.arange(TP) ^ t].reshape(TP * rows_here, -1)
    mine_rows = jnp.arange(group_rows) * n_seq + place_z
    if group_rows == 2:
        mine_rows = jnp.where(side == 0, mine_rows, mine_rows[::-1])
    row_lengths = near[mine_rows]
    ends = jnp.cumsum(row_lengths, axis=1)
    starts = ends - row_lengths
    places = jnp.arange(length, dtype=jnp.int32)
    segment = jnp.sum((places[None, :, None] >= ends[:, None, :]).astype(jnp.int32), axis=2)
    which = segment[:, :, None] == jnp.arange(lengths.shape[1], dtype=jnp.int32)[None, None, :]
    within = places[None, :] - jnp.sum(jnp.where(which, starts[:, None, :], 0), axis=2)
    lane = jnp.arange(128)
    feature = lane % HD
    inverse = 1.0 / 10000.0 ** (jnp.arange(0, ROT, 2, dtype=F32) / ROT)
    angle = within.astype(F32)[..., None] * jnp.tile(inverse, 128 // (ROT // 2))
    cosine, sine = jnp.cos(angle), jnp.sin(angle)
    tables = jnp.stack(
        [
            jnp.where(feature < ROT, cosine, 1.0),
            jnp.where(feature < ROT // 2, -sine, 0.0),
            jnp.where((feature >= ROT // 2) & (feature < ROT), sine, 0.0),
        ],
        axis=1,
    )
    wide = jnp.arange(cols) % HD
    hits = segment[:, :, None] == wide[None, None, :]
    q_ext = jnp.where(hits, 1.0, 0.0).astype(BF)
    k_ext = jnp.where(hits | (wide >= lengths.shape[1])[None, None, :], 0.0, -BIG).astype(BF)

    def gather_group(value):
        own = order(value, swap(value, 1), core)
        other = swap(own, 2)
        if group_rows == 2:
            return [own, other]
        return [order(own, other, side)]

    def scatter_group(parts):
        if group_rows == 2:
            own, other = parts
        else:
            pair = parts[0].reshape(2, 2 * per_dev, width)
            own = lax.dynamic_index_in_dim(pair, side, 0, keepdims=False)
            other = lax.dynamic_index_in_dim(pair, 1 - side, 0, keepdims=False)

        def halve(value):
            value = value.reshape(2, per_dev, width)
            keep = lax.dynamic_index_in_dim(value, core, 0, keepdims=False)
            send = lax.dynamic_index_in_dim(value, 1 - core, 0, keepdims=False)
            return keep + swap(send.astype(BF), 1).astype(F32)

        far = swap(halve(other).astype(BF), 2)
        return halve(own) + far.astype(F32)

    state = to_rows(tokens).astype(F32)
    stored = []
    for layer in range(LAYERS):
        w_qkv, w_out, w_in, w_down, gain, shift, bias_in, bias_out = weights[layer]
        centered = state - jnp.mean(state, axis=-1, keepdims=True)
        inv_std = lax.rsqrt(jnp.mean(centered * centered, axis=-1, keepdims=True) + norm_epsilon)
        normed = centered * inv_std
        hiddens = gather_group((normed * gain + shift).astype(BF))
        kept, parts = [], []
        for r, hidden in enumerate(hiddens):
            context, rot, lse = attend(dot(hidden, w_qkv), tables[r], q_ext[r], k_ext[r])
            inner = dot(hidden, w_in) + bias_in
            activated = gelu_tanh(inner).astype(BF)
            parts.append(dot(context, w_out) + dot(activated, w_down))
            kept.append((hidden, context, rot, lse, inner, activated))
        stored.append((normed, inv_std, kept))
        state = state + scatter_group(parts) + bias_out
    outputs = from_rows(state.astype(BF))

    d_state = to_rows(cotangent).astype(F32)
    big = [None] * LAYERS
    small_grads = [None] * LAYERS

    def reduce_blocks(value, units):
        rest = value.shape[1]
        value = value.astype(BF).reshape(units, n_seq, n_g, chunks, rest).transpose(2, 1, 0, 3, 4)
        if n_g == 2:
            keep = lax.dynamic_index_in_dim(value, g, 0, keepdims=False)
            send = lax.dynamic_index_in_dim(value, 1 - g, 0, keepdims=False)
            value = (keep.astype(F32) + swap(send, TP).astype(F32)).astype(BF)
        else:
            value = lax.psum_scatter(
                value, "dp", scatter_dimension=0, axis_index_groups=across, tiled=False
            )
        return lax.psum_scatter(value, "seq", scatter_dimension=0, tiled=False)

    for layer in reversed(range(LAYERS)):
        w_qkv, w_out, w_in, w_down, gain, shift, bias_in, bias_out = weights[layer]
        normed, inv_std, kept = stored[layer]
        d_branch = d_state.astype(BF)
        g_bias_out = jnp.sum(d_branch.astype(F32), axis=0)
        g_down = g_out = g_in = g_qkv = g_bias_in = 0.0
        parts = []
        for r, d_row in enumerate(gather_group(d_branch)):
            hidden, context, rot, lse, inner, activated = kept[r]
            d_context = dot_nt(d_row, w_out).astype(BF)
            d_projected = attend_back(rot, d_context, lse, tables[r], q_ext[r], k_ext[r])
            d_inner = (dot_nt(d_row, w_down) * gelu_slope(inner)).astype(BF)
            parts.append(dot_nt(d_inner, w_in) + dot_nt(d_projected, w_qkv))
            g_down += dot_tn(activated, d_row)
            g_out += dot_tn(context, d_row)
            g_in += dot_tn(hidden, d_inner)
            g_qkv += dot_tn(hidden, d_projected)
            g_bias_in += jnp.sum(d_inner.astype(F32), axis=0)
        d_hidden = scatter_group(parts)
        g_gain = jnp.sum(d_hidden * normed, axis=0)
        g_shift = jnp.sum(d_hidden, axis=0)
        d_normed = d_hidden * gain
        d_state = d_state + inv_std * (
            d_normed
            - jnp.mean(d_normed, axis=-1, keepdims=True)
            - normed * jnp.mean(d_normed * normed, axis=-1, keepdims=True)
        )
        r_qkv = reduce_blocks(g_qkv.reshape(3 * width, cols), n_qkv)
        r_in = reduce_blocks(g_in.reshape(FF, cols), n_in)
        both = reduce_blocks(jnp.concatenate([g_out, g_down]), (1 + fold) * my_out)
        both = both.reshape((1 + fold) * my_out, chunks, TP, cols).transpose(2, 0, 1, 3)
        both = lax.all_to_all(
            both, "dp", split_axis=0, concat_axis=0, tiled=True, axis_index_groups=groups
        )
        r_out = both[:, :my_out].reshape(n_out, chunks, cols)
        r_down = (
            both[:, my_out:]
            .reshape(TP, fold, my_out, chunks, cols)
            .transpose(1, 0, 2, 3, 4)
            .reshape(n_in, chunks, cols)
        )
        big[layer] = jnp.concatenate([r_qkv, r_out, r_in, r_down])
        wide_bias = (
            (jnp.arange(TP) == t).astype(F32)[None, :, None] * g_bias_in.reshape(fold, 1, cols)
        ).reshape(-1)
        small_grads[layer] = jnp.concatenate([g_gain, g_shift, wide_bias, g_bias_out])
    grad_in = from_rows(d_state.astype(BF))

    grads = jnp.concatenate(big + [jnp.zeros((1, chunks, cols), BF)])
    slots = grads[block_of_slot].reshape(n_dp, capacity, chunks, cols)
    owned = lax.all_to_all(slots, "dp", split_axis=0, concat_axis=0, tiled=True)
    owned = (
        owned.reshape(n_g, TP, capacity, chunks, cols)
        .transpose(2, 0, 3, 1, 4)
        .reshape(capacity, piece)
        .astype(F32)
    )
    small_owned = lax.psum_scatter(
        jnp.concatenate(small_grads), ("dp", "seq"), scatter_dimension=0, tiled=True
    )
    new_masters, new_first, new_second = adam_update(
        masters, owned, first_moment, second_moment, learn_rate, decay_rate
    )
    small_new, small_first_new, small_second_new = adam_update(
        small_params, small_owned, small_first, small_second, small_rate, 0.0
    )
    return (
        outputs,
        grad_in,
        new_masters,
        new_first,
        new_second,
        new_masters.astype(BF),
        small_new,
        small_first_new,
        small_second_new,
    )


def solution(mesh):
    placed = (
        P("dp", "seq", None),
        P("dp", "seq", None),
        P("dp", None),
        P(),
        P("dp", "seq"),
        P("dp", "seq"),
        P("dp", "seq"),
        P(("dp", "seq")),
        P(("dp", "seq")),
        P(("dp", "seq")),
    )
    return jax.shard_map(
        body,
        mesh=mesh,
        in_specs=placed,
        out_specs=(
            P("dp", "seq", None),
            P("dp", "seq", None),
            P("dp", "seq"),
            P("dp", "seq"),
            P("dp", "seq"),
            P("dp", "seq"),
            P(("dp", "seq")),
            P(("dp", "seq")),
            P(("dp", "seq")),
        ),
        check_vma=False,
    )
```

time: 2970 us -> 955 us (0.32)
  waiting for transfers between devices: 1660 us -> 189 us
  local copies, waits for them, and re-layouts: 744 us -> 134 us
  matrix products: 318 us -> 189 us
  blocking collectives: 50.4 us -> 164 us
  Pallas kernels: 0 us -> 89.3 us
  other arithmetic: 134 us -> 88.5 us
  starting transfers between devices: 37 us -> 67.9 us
    reduce_scatter x2 -> x6, waiting for transfers between devices: 1120 us -> 0.03 us  [reduce_blocks(): return lax.psum_scatter(value, 'seq', scatter_dimension=0, tiled=False)]
    all_gather x2 -> x4, waiting for transfers between devices: 429 us -> 0.03 us  [gather_blocks(): by_z = lax.all_gather(value, 'seq', axis=0)]
    gather x6 -> x4, local copies, waits for them, and re-layouts: 294 us -> 6.76 us  [the longest x1 3.62 us: body(): slots = grads[block_of_slot].reshape(n_dp, capacity, chunks, cols)]
    ppermute x0 -> x42, waiting for transfers between devices: none -> 164 us  [the longest x34 164 us: swap(): return lax.ppermute(value, 'dp', [(i, i ^ bit) for i in range(n_dp)])]
    reshape x13 -> x1, local copies, waits for them, and re-layouts: 154 us -> 2.77 us  [body(): packed = masters.astype(BF).reshape(capacity, n_g, chunks, TP, cols).tran...]
    dot_general x52 -> x48, matrix products: 318 us -> 189 us  [the longest x16 65.9 us: dot_nt(): lax.dot_general(left, right, (((1,), (1,)), ((), ())), preferred_element_...]
    unnamed x248 -> x263, local copies, waits for them, and re-layouts: 132 us -> 26.3 us
    pallas_call x0 -> x8, Pallas kernels: none -> 89.3 us  [the longest x4 50.7 us: attend_back(): pl.pallas_call(attend_back_kernel, out_shape=jax.ShapeDtypeStruct((length...]
  transfers between devices with their start and end apart: 12 -> 58, of which waited for: 10 -> 17; matrix products, arithmetic and copies ran while one was open for 12% -> 37% of each run, Pallas kernels for 0% -> 9%
where the time goes in v1:
time: 955 us; the launch traced here: 944 us
  waiting for transfers between devices  189 us (20%)
  matrix products  189 us (20%)
  blocking collectives  164 us (17%)
  local copies, waits for them, and re-layouts  134 us (14%)
  Pallas kernels  89.3 us (9%)
  other arithmetic  88.5 us (9%)
  starting transfers between devices  67.9 us (7%)
  between operations  22.3 us (2%)
    ppermute x34, waiting for transfers between devices, swap(): return lax.ppermute(value, 'dp', [(i, i ^ bit) for i in range(n_dp)])  164 us
    unnamed x2, blocking collectives  113 us
    dot_general x16, matrix products, dot_nt(): lax.dot_general(left, right, (((1,), (1,)), ((), ())), preferred_element_...  65.9 us
    dot_general x16, matrix products, dot_tn(): lax.dot_general(left, right, (((0,), (0,)), ((), ())), preferred_element_...  65.3 us
    dot_general x16, matrix products, dot(): return jnp.dot(left, right, preferred_element_type=F32)  57.4 us
    all_gather x2, blocking collectives, gather_blocks(): by_z = lax.all_gather(value, 'seq', axis=0)  51.5 us
    pallas_call x4, Pallas kernels, attend_back(): pl.pallas_call(attend_back_kernel, out_shape=jax.ShapeDtypeStruct((length...  50.7 us
    pallas_call x4, Pallas kernels, attend(): pl.pallas_call(attend_kernel, out_shape=(jax.ShapeDtypeStruct((length, wi...  38.6 us
  transfers between devices with their start and end apart: 58, of which 17 were waited for; matrix products, arithmetic and copies ran while one was open for 37% of the time, Pallas kernels for 9%

profile of v1, /device:TPU:0, one launch (start us, length us, event | category | flops | bytes accessed | tf_op | source)
XLA Modules:
  0.0 943.6 jit_solution(7443173063665273388)
XLA Ops:
  19.1 5.3 collective-permute-start.22
  26.7 5.3 collective-permute-start
  38.2 4.3 all-to-all-start
  43.3 59.0 %all-reduce = bf16[14336]{0:T(1024)(128)(2,1)S(1)} all-reduce(bf16[14336]{0:T(1024)(128)(2,1)S(1)} %dynamic-update-slice), channel_id=1, replica_groups=mesh['dp'=8,'seq'=4] {'dp','seq'}, use_global_device_ids=true, to_apply=%add | all-reduce | flops 14336 | bytes 57344
  144.9 25.3 %all-gather = bf16[96,16,256]{2,1,0:T(8,128)(2,1)} all-gather(bf16[24,16,256]{2,1,0:T(8,128)(2,1)S(1)} %get-tuple-element.91), channel_id=2, replica_groups=mesh['dp'=8,'seq'=4] {'seq'}, dimensions={0}, use_global_device_ids=true | all-gather | bytes 983040 | tf_op jit(solution)/shard_map/all_gather | solution.py:381
  179.8 26.2 %all-gather.2 = bf16[96,16,256]{2,1,0:T(8,128)(2,1)} all-gather(bf16[24,16,256]{2,1,0:T(8,128)(2,1)S(1)} %get-tuple-element.90), channel_id=4, replica_groups=mesh['dp'=8,'seq'=4] {'seq'}, dimensions={0}, use_global_device_ids=true | all-gather | bytes 983040 | tf_op jit(solution)/shard_map/all_gather | solution.py:381
  210.3 3.8 reshape_reshape.12
  216.1 5.2 fusion.90.proj_ref
  221.3 7.2 attend.4
  229.8 5.7 fusion.103.proj_ref
  235.4 16.9 %attend.5 = (bf16[1024,256]{1,0:T(8,128)(2,1)S(1)}, bf16[1024,768]{1,0:T(8,128)(2,1)S(1)}, f32[8,1024]{1,0:T(8,128)S(1)}) custom-call(f32[1024,768]{1,0:T(8,128)} %fusion.103.proj_ref, f32[3,1024,128]{2,1,0:T(8,128)} %get-tuple-element.58.tab_ref, bf16[1024,256]{1,0:T(8,128)(2,1)S(1)} %get-tuple-element.116.qx_ref, ...), custom_call_target="tpu_custom_call" | custom-call | flops 2147483648 | bytes 6291456 | tf_op jit(solution)/shard_map/attend/pallas_call | solution.py:184
  261.3 4.4 reshape_reshape.13
  265.7 4.7 fusion.89
  270.4 5.5 fusion.104
  275.9 20.5 %collective-permute-done.6 = bf16[4,10,16,1024]{3,2,0,1:T(8,128)(2,1)} collective-permute-done((bf16[4,10,16,1024]{3,2,0,1:T(8,128)(2,1)}, bf16[4,10,16,1024]{3,2,0,1:T(8,128)(2,1)}, u32[]{:S(2)}, u32[]{:S(2)}) %collective-permute-start.6) | collective-permute-done | bytes 1310752 | tf_op jit(solution)/shard_map/ppermute | solution.py:302
  315.5 4.0 reshape_reshape.14
  325.6 4.4 reshape_reshape.15
  330.0 5.3 collective-permute-done.11
  339.1 13.6 %collective-permute-done.14 = bf16[4,10,16,1024]{3,2,0,1:T(8,128)(2,1)} collective-permute-done((bf16[4,10,16,1024]{3,2,0,1:T(8,128)(2,1)}, bf16[4,10,16,1024]{3,2,0,1:T(8,128)(2,1)}, u32[]{:S(2)}, u32[]{:S(2)}) %collective-permute-start.14) | collective-permute-done | bytes 1310752 | tf_op jit(solution)/shard_map/ppermute | solution.py:302
  357.8 21.5 %collective-permute-done.26 = bf16[1024,1024]{1,0:T(8,128)(2,1)} collective-permute-done((bf16[1024,1024]{1,0:T(8,128)(2,1)}, bf16[1024,1024]{1,0:T(8,128)(2,1)}, u32[]{:S(2)}, u32[]{:S(2)}) %collective-permute-start.26) | collective-permute-done | bytes 2097184 | tf_op jit(solution)/shard_map/ppermute | solution.py:302
  387.9 8.0 convert_reduce_fusion.1
  395.9 4.8 fusion.82
  405.0 7.2 attend.6
  417.0 13.0 %attend_back.4 = bf16[1024,768]{1,0:T(8,128)(2,1)S(1)} custom-call(bf16[1024,768]{1,0:T(8,128)(2,1)} %copy-done.15, bf16[1024,256]{1,0:T(8,128)(2,1)S(1)} %convolution_convert_fusion.3.dctx_ref, f32[8,1024]{1,0:T(8,128)S(1)} %get-tuple-element.26.lse_ref, f32[3,1024,128]{2,1,0:T(8,128)} %get-tuple-element.57.tab_ref, ...), custom_call_target="tpu_custom_call" | custom-call | flops 5368709120 | bytes 6291456 | tf_op jit(solution)/shard_map/attend_back/pallas_call | solution.py:205
  430.1 5.2 fusion.107
  438.5 9.2 collective-permute-done.17
  447.7 5.3 fusion.105.proj_ref
  453.0 7.3 attend.7
  460.3 4.5 fusion.106
  464.9 4.8 fusion.86
  469.7 7.5 convert_reduce_fusion
  477.2 4.4 fusion.108
  481.6 12.5 %attend_back.5 = bf16[1024,768]{1,0:T(8,128)(2,1)S(1)} custom-call(bf16[1024,768]{1,0:T(8,128)(2,1)} %copy-done.14, bf16[1024,256]{1,0:T(8,128)(2,1)S(1)} %convolution_convert_fusion.2.dctx_ref, f32[8,1024]{1,0:T(8,128)S(1)} %get-tuple-element.28.lse_ref, f32[3,1024,128]{2,1,0:T(8,128)} %get-tuple-element.58.tab_ref, ...), custom_call_target="tpu_custom_call" | custom-call | flops 5368709120 | bytes 6291456 | tf_op jit(solution)/shard_map/attend_back/pallas_call | solution.py:205
  494.3 4.4 convolution_add_fusion.6
  501.2 4.6 fusion.85
  514.9 17.4 %collective-permute-done.28 = bf16[512,1024]{1,0:T(8,128)(2,1)S(1)} collective-permute-done((bf16[512,1024]{1,0:T(8,128)(2,1)S(1)}, bf16[512,1024]{1,0:T(8,128)(2,1)S(1)}, u32[]{:S(2)}, u32[]{:S(2)}) %collective-permute-start.28) | collective-permute-done | bytes 1048608 | tf_op jit(solution)/shard_map/ppermute | solution.py:302
  535.2 19.2 %collective-permute-done.19 = bf16[512,1024]{1,0:T(8,128)(2,1)S(1)} collective-permute-done((bf16[512,1024]{1,0:T(8,128)(2,1)S(1)}, bf16[512,1024]{1,0:T(8,128)(2,1)S(1)}, u32[]{:S(2)}, u32[]{:S(2)}) %collective-permute-start.19) | collective-permute-done | bytes 1048608 | tf_op jit(solution)/shard_map/ppermute | solution.py:302
  554.4 4.7 convert_reduce_fusion.6
  564.9 26.8 %collective-permute-done.40 = bf16[4,10,16,1024]{3,2,1,0:T(8,128)(2,1)S(1)} collective-permute-done((bf16[4,10,16,1024]{3,2,1,0:T(8,128)(2,1)S(1)}, bf16[4,10,16,1024]{3,2,1,0:T(8,128)(2,1)S(1)}, u32[]{:S(2)}, u32[]{:S(2)}) %collective-permute-start.40) | collective-permute-done | bytes 1310752 | tf_op jit(solution)/shard_map/ppermute | solution.py:302
  596.3 8.9 convert_reduce_fusion.3
  605.3 6.7 collective-permute-done.31
  612.0 4.7 fusion.83
  624.9 12.6 %attend_back.6 = bf16[1024,768]{1,0:T(8,128)(2,1)S(1)} custom-call(bf16[1024,768]{1,0:T(8,128)(2,1)} %copy-done.12, bf16[1024,256]{1,0:T(8,128)(2,1)S(1)} %convolution_convert_fusion.1.dctx_ref, f32[8,1024]{1,0:T(8,128)S(1)} %get-tuple-element.30.lse_ref, f32[3,1024,128]{2,1,0:T(8,128)} %get-tuple-element.57.tab_ref, ...), custom_call_target="tpu_custom_call" | custom-call | flops 5368709120 | bytes 6291456 | tf_op jit(solution)/shard_map/attend_back/pallas_call | solution.py:205
  640.4 12.6 %attend_back.7 = bf16[1024,768]{1,0:T(8,128)(2,1)S(1)} custom-call(bf16[1024,768]{1,0:T(8,128)(2,1)} %copy-done.13, bf16[1024,256]{1,0:T(8,128)(2,1)S(1)} %convolution_convert_fusion.dctx_ref, f32[8,1024]{1,0:T(8,128)S(1)} %get-tuple-element.32.lse_ref, f32[3,1024,128]{2,1,0:T(8,128)} %get-tuple-element.58.tab_ref, ...), custom_call_target="tpu_custom_call" | custom-call | flops 5368709120 | bytes 6291456 | tf_op jit(solution)/shard_map/attend_back/pallas_call | solution.py:205
  653.0 5.7 fusion.111
  660.8 5.2 add_convert_fusion.5
  670.7 7.1 convert_reduce_fusion.2
  677.8 6.8 fusion.113
  689.3 6.9 add_convert_fusion.2
  696.2 4.3 convert_element_type.430
  706.0 5.2 fusion.114
  711.2 17.2 %collective-permute-done.38 = bf16[4,32,16,256]{3,2,1,0:T(8,128)(2,1)} collective-permute-done((bf16[4,32,16,256]{3,2,1,0:T(8,128)(2,1)}, bf16[4,32,16,256]{3,2,1,0:T(8,128)(2,1)}, u32[]{:S(2)}, u32[]{:S(2)}) %collective-permute-start.38) | collective-permute-done | bytes 1048608 | tf_op jit(solution)/shard_map/ppermute | solution.py:302
  731.3 5.6 add_convert_fusion.4
  741.4 4.4 fusion.116
  749.5 4.4 convert_element_type.450
  764.2 5.8 collective-permute-start.20
  770.1 4.0 fusion.110
  795.5 18.2 %all-to-all-done.4 = bf16[4,10,16,256]{3,2,1,0:T(8,128)(2,1)S(1)} async-done(((bf16[4,10,16,256]{3,2,1,0:T(8,128)(2,1)}), bf16[4,10,16,256]{3,2,1,0:T(8,128)(2,1)S(1)}, u32[]{:S(2)}, u32[]{:S(2)}) %all-to-all-start.4) | async-done | bytes 327712 | tf_op jit(solution)/shard_map/all_to_all | solution.py:546
  815.9 4.0 fusion.44
  846.2 4.5 all-to-all-start.5
  855.2 53.6 %all-reduce.1 = f32[14336]{0:T(1024)S(1)} all-reduce(f32[14336]{0:T(1024)S(1)} %constant_dynamic-update-slice_fusion.6), channel_id=12, replica_groups=mesh['dp'=8,'seq'=4] {'dp','seq'}, use_global_device_ids=true, to_apply=%region_30.31.clone | all-reduce | flops 14336 | bytes 114688
  912.8 6.0 copy.276
  918.8 5.8 reshape.401
  924.6 11.7 %fusion.92 = (bf16[32,32768]{1,0:T(8,128)(2,1)}, f32[32,32768]{1,0:T(8,128)}, f32[32,32768]{1,0:T(8,128)}, f32[32,32768]{1,0:T(8,128)}) fusion(f32[32,32768]{1,0:T(8,128)} %param.18, f32[32,32768]{1,0:T(8,128)} %reshape.401, f32[32,32768]{1,0:T(8,128)} %param.19, f32[32,32768]{1,0:T(8,128)} %param.20), kind=kLoop, calls=%fused_computation.320 | loop fusion | flops 16777216 | bytes 31457280 | tf_op jit(solution)/shard_map/convert_element_type | solution.py:587
  (566 shorter events, 270.5 us)
Async XLA Ops:
  7.2 98.7 %collective-permute-start.4 = (s32[2,4]{1,0:T(2,128)}, s32[2,4]{1,0:T(2,128)S(1)}, u32[]{:S(2)}, u32[]{:S(2)}) collective-permute-start(s32[2,4]{1,0:T(2,128)} %param.16), channel_id=1, source_target_pairs={{0,4},{4,0},{8,12},{12,8},{16,20},{20,16},{24,28},{28,24},{1,5},{5... | collective-permute-start | bytes 104 | tf_op jit(solution)/shard_map/ppermute | solution.py:302
  16.5 114.3 %collective-permute-start.23 = (bf16[256,1024]{1,0:T(8,128)(2,1)}, bf16[256,1024]{1,0:T(8,128)(2,1)S(1)}, u32[]{:S(2)}, u32[]{:S(2)}) collective-permute-start(bf16[256,1024]{1,0:T(8,128)(2,1)} %get-tuple-element.107), channel_id=1, source_target_pairs={{0,1},{16,17},{1,0},{17,16},{2,5},{18,21},{3,4},{19,20},{4,3},{20,... | collective-permute-start | bytes 1572872 | tf_op jit(solution)/shard_map/ppermute | solution.py:325
  19.1 112.5 %collective-permute-start.22 = (bf16[256,1024]{1,0:T(8,128)(2,1)}, bf16[256,1024]{1,0:T(8,128)(2,1)}, u32[]{:S(2)}, u32[]{:S(2)}) collective-permute-start(bf16[256,1024]{1,0:T(8,128)(2,1)} %get-tuple-element.108), channel_id=1, source_target_pairs={{0,0},{16,16},{1,1},{17,17},{2,4},{18,20},{3,5},{19,21},{4,2},{20,... | collective-permute-start | bytes 1572872 | tf_op jit(solution)/shard_map/ppermute | solution.py:325
  26.7 94.8 %collective-permute-start.1 = (bf16[256,1024]{1,0:T(8,128)(2,1)}, bf16[256,1024]{1,0:T(8,128)(2,1)S(1)}, u32[]{:S(2)}, u32[]{:S(2)}) collective-permute-start(bf16[256,1024]{1,0:T(8,128)(2,1)} %get-tuple-element.119), channel_id=1, source_target_pairs={{0,1},{16,17},{1,0},{17,16},{2,5},{18,21},{3,4},{19,20},{4,3},{20,... | collective-permute-start | bytes 1572872 | tf_op jit(solution)/shard_map/ppermute | solution.py:325
  26.7 94.8 %collective-permute-start = (bf16[256,1024]{1,0:T(8,128)(2,1)}, bf16[256,1024]{1,0:T(8,128)(2,1)}, u32[]{:S(2)}, u32[]{:S(2)}) collective-permute-start(bf16[256,1024]{1,0:T(8,128)(2,1)} %get-tuple-element.120), channel_id=1, source_target_pairs={{0,0},{16,16},{1,1},{17,17},{2,4},{18,20},{3,5},{19,21},{4,2},{20,... | collective-permute-start | bytes 1572872 | tf_op jit(solution)/shard_map/ppermute | solution.py:325
  38.2 67.7 %copy-start.103 = (s32[2,4]{1,0:T(2,128)S(1)}, s32[2,4]{1,0:T(2,128)}, u32[]{:S(2)}) copy-start(s32[2,4]{1,0:T(2,128)} %param.16) | copy-start | bytes 100
  38.2 73.1 %all-to-all-start = ((bf16[8,32,16,256]{3,2,1,0:T(8,128)(2,1)}), bf16[8,32,16,256]{3,2,1,0:T(8,128)(2,1)S(1)}, u32[]{:S(2)}, u32[]{:S(2)}) async-start(bf16[8,32,16,256]{3,2,1,0:T(8,128)(2,1)} %bitcast.5), calls=%async_computation | async-start | bytes 4194304 | tf_op jit(solution)/shard_map/all_to_all | solution.py:367
  42.5 171.6 %all-gather.13.cloned.1.call-start = ((), (), s32[]{:S(2)}) async-start(), calls=%async_computation.20 | async-start | bytes 1310720 | tf_op jit(solution)/shard_map/all_gather | solution.py:381
  103.0 199.2 %copy-start.100 = (f32[4,1,256]{2,1,0:T(1,128)}, f32[4,1,256]{2,1,0:T(1,128)S(1)}, u32[]{:S(2)}) copy-start(f32[4,1,256]{2,1,0:T(1,128)S(1)} %constant_dynamic-slice_fusion.13) | copy-start | bytes 12292
  105.9 3.9 collective-permute-start.5
  115.5 114.3 %all-gather.15.cloned.1.call-start = ((), (), s32[]{:S(2)}) async-start(), calls=%async_computation.21 | async-start | bytes 1310720 | tf_op jit(solution)/shard_map/all_gather | solution.py:381
  123.7 16.7 %collective-permute-start.2 = (bf16[512,1024]{1,0:T(8,128)(2,1)S(1)}, bf16[512,1024]{1,0:T(8,128)(2,1)}, u32[]{:S(2)}, u32[]{:S(2)}) collective-permute-start(bf16[512,1024]{1,0:T(8,128)(2,1)S(1)} %fusion.38), channel_id=1, source_target_pairs={{0,4},{4,0},{8,12},{12,8},{16,20},{20,16},{24,28},{28,24},{1,5},{5... | collective-permute-start | bytes 3145736 | tf_op jit(solution)/shard_map/ppermute | solution.py:302
  127.0 10.5 %all-to-all-start.1 = ((bf16[4,10,16,256]{3,2,1,0:T(8,128)(2,1)}), bf16[4,10,16,256]{3,2,1,0:T(8,128)(2,1)S(1)}, u32[]{:S(2)}, u32[]{:S(2)}) async-start(bf16[4,10,16,256]{3,2,1,0:T(8,128)(2,1)} %pad_maximum_fusion.11), calls=%async_computation.1 | async-start | bytes 655360 | tf_op jit(solution)/shard_map/all_to_all | solution.py:403
  130.5 123.0 %all-gather.9.cloned.1.call-start = ((), (), s32[]{:S(2)}) async-start(), calls=%async_computation.12 | async-start | bytes 1638400 | tf_op jit(solution)/shard_map/all_gather | solution.py:381
  134.0 38.2 %collective-permute-start.24 = (bf16[512,1024]{1,0:T(8,128)(2,1)}, bf16[512,1024]{1,0:T(8,128)(2,1)}, u32[]{:S(2)}, u32[]{:S(2)}) collective-permute-start(bf16[512,1024]{1,0:T(8,128)(2,1)} %pad_maximum_fusion.9), channel_id=1, source_target_pairs={{0,4},{4,0},{8,12},{12,8},{16,20},{20,16},{24,28},{28,24},{1,5},{5... | collective-permute-start | bytes 3145736 | tf_op jit(solution)/shard_map/ppermute | solution.py:302
  143.8 85.9 %collective-permute-start.9 = (bf16[1024,1024]{1,0:T(8,128)(2,1)}, bf16[1024,1024]{1,0:T(8,128)(2,1)}, u32[]{:S(2)}, u32[]{:S(2)}) collective-permute-start(bf16[1024,1024]{1,0:T(8,128)(2,1)} %pad_maximum_fusion.3), channel_id=1, source_target_pairs={{0,8},{4,12},{8,0},{12,4},{16,24},{20,28},{24,16},{28,20},{1,9},{5... | collective-permute-start | bytes 6291464 | tf_op jit(solution)/shard_map/ppermute | solution.py:302
  170.2 37.1 %collective-permute-start.3 = (bf16[4,24,16,256]{3,2,1,0:T(8,128)(2,1)}, bf16[4,24,16,256]{3,2,1,0:T(8,128)(2,1)}, u32[]{:S(2)}, u32[]{:S(2)}) collective-permute-start(bf16[4,24,16,256]{3,2,1,0:T(8,128)(2,1)} %bitcast.7), channel_id=1, source_target_pairs={{0,16},{4,20},{8,24},{12,28},{16,0},{20,4},{24,8},{28,12},{1,17},{... | collective-permute-start | bytes 2359304 | tf_op jit(solution)/shard_map/ppermute | solution.py:302
  176.2 29.7 %all-to-all-start.2 = ((bf16[4,10,16,256]{3,2,1,0:T(8,128)(2,1)}), bf16[4,10,16,256]{3,2,1,0:T(8,128)(2,1)S(1)}, u32[]{:S(2)}, u32[]{:S(2)}) async-start(bf16[4,10,16,256]{3,2,1,0:T(8,128)(2,1)} %pad_maximum_fusion.12), calls=%async_computation.2 | async-start | bytes 655360 | tf_op jit(solution)/shard_map/all_to_all | solution.py:403
  179.7 139.8 %all-gather.11.cloned.1.call-start = ((), (), s32[]{:S(2)}) async-start(), calls=%async_computation.13 | async-start | bytes 1638400 | tf_op jit(solution)/shard_map/all_gather | solution.py:381
  206.0 106.5 %collective-permute-start.13 = (bf16[4,24,16,256]{3,2,1,0:T(8,128)(2,1)}, bf16[4,24,16,256]{3,2,1,0:T(8,128)(2,1)}, u32[]{:S(2)}, u32[]{:S(2)}) collective-permute-start(bf16[4,24,16,256]{3,2,1,0:T(8,128)(2,1)} %bitcast.43), channel_id=1, source_target_pairs={{0,16},{4,20},{8,24},{12,28},{16,0},{20,4},{24,8},{28,12},{1,17},{... | collective-permute-start | bytes 2359304 | tf_op jit(solution)/shard_map/ppermute | solution.py:302
  207.2 580.6 %reduce-scatter.15.cloned.1.call-start = ((), (), s32[]{:S(2)}) async-start(), calls=%async_computation.18 | async-start | bytes 1638400 | tf_op jit(solution)/shard_map/reduce_scatter | solution.py:513
  214.1 43.9 %collective-permute-start.7 = (bf16[4,32,16,256]{3,2,1,0:T(8,128)(2,1)}, bf16[4,32,16,256]{3,2,1,0:T(8,128)(2,1)}, u32[]{:S(2)}, u32[]{:S(2)}) collective-permute-start(bf16[4,32,16,256]{3,2,1,0:T(8,128)(2,1)} %bitcast.408), channel_id=1, source_target_pairs={{0,16},{4,20},{8,24},{12,28},{16,0},{20,4},{24,8},{28,12},{1,17},{... | collective-permute-start | bytes 3145736 | tf_op jit(solution)/shard_map/ppermute | solution.py:302
  229.7 75.3 %copy-start.2 = (bf16[1024,256]{1,0:T(8,128)(2,1)}, bf16[1024,256]{1,0:T(8,128)(2,1)S(1)}, u32[]{:S(2)}) copy-start(bf16[1024,256]{1,0:T(8,128)(2,1)S(1)} %get-tuple-element.21) | copy-start | bytes 1572868
  229.7 92.7 %collective-permute-start.15 = (bf16[4,32,16,256]{3,2,1,0:T(8,128)(2,1)}, bf16[4,32,16,256]{3,2,1,0:T(8,128)(2,1)}, u32[]{:S(2)}, u32[]{:S(2)}) collective-permute-start(bf16[4,32,16,256]{3,2,1,0:T(8,128)(2,1)} %bitcast.406), channel_id=1, source_target_pairs={{0,16},{4,20},{8,24},{12,28},{16,0},{20,4},{24,8},{28,12},{1,17},{... | collective-permute-start | bytes 3145736 | tf_op jit(solution)/shard_map/ppermute | solution.py:302
  256.2 40.2 %collective-permute-start.6 = (bf16[4,10,16,1024]{3,2,0,1:T(8,128)(2,1)}, bf16[4,10,16,1024]{3,2,0,1:T(8,128)(2,1)}, u32[]{:S(2)}, u32[]{:S(2)}) collective-permute-start(bf16[4,10,16,1024]{3,2,0,1:T(8,128)(2,1)} %copy.247), channel_id=1, source_target_pairs={{0,16},{4,20},{8,24},{12,28},{16,0},{20,4},{24,8},{28,12},{1,17},{... | collective-permute-start | bytes 3932168 | tf_op jit(solution)/shard_map/ppermute | solution.py:302
  302.2 5.5 collective-permute-start.10
  307.2 22.9 %collective-permute-start.8 = (bf16[512,1024]{1,0:T(8,128)(2,1)}, bf16[512,1024]{1,0:T(8,128)(2,1)}, u32[]{:S(2)}, u32[]{:S(2)}) collective-permute-start(bf16[512,1024]{1,0:T(8,128)(2,1)} %fusion.69), channel_id=1, source_target_pairs={{0,4},{4,0},{8,12},{12,8},{16,20},{20,16},{24,28},{28,24},{1,5},{5... | collective-permute-start | bytes 3145736 | tf_op jit(solution)/shard_map/ppermute | solution.py:302
  309.0 26.3 %collective-permute-start.11 = (bf16[512,1024]{1,0:T(8,128)(2,1)}, bf16[512,1024]{1,0:T(8,128)(2,1)}, u32[]{:S(2)}, u32[]{:S(2)}) collective-permute-start(bf16[512,1024]{1,0:T(8,128)(2,1)} %fusion.59), channel_id=1, source_target_pairs={{0,8},{4,12},{8,0},{12,4},{16,24},{20,28},{24,16},{28,20},{1,9},{5... | collective-permute-start | bytes 3145736 | tf_op jit(solution)/shard_map/ppermute | solution.py:302
  311.4 67.9 %collective-permute-start.26 = (bf16[1024,1024]{1,0:T(8,128)(2,1)}, bf16[1024,1024]{1,0:T(8,128)(2,1)}, u32[]{:S(2)}, u32[]{:S(2)}) collective-permute-start(bf16[1024,1024]{1,0:T(8,128)(2,1)} %pad_maximum_fusion.5), channel_id=1, source_target_pairs={{0,8},{4,12},{8,0},{12,4},{16,24},{20,28},{24,16},{28,20},{1,9},{5... | collective-permute-start | bytes 6291464 | tf_op jit(solution)/shard_map/ppermute | solution.py:302
  322.1 30.6 %collective-permute-start.14 = (bf16[4,10,16,1024]{3,2,0,1:T(8,128)(2,1)}, bf16[4,10,16,1024]{3,2,0,1:T(8,128)(2,1)}, u32[]{:S(2)}, u32[]{:S(2)}) collective-permute-start(bf16[4,10,16,1024]{3,2,0,1:T(8,128)(2,1)} %copy.255), channel_id=1, source_target_pairs={{0,16},{4,20},{8,24},{12,28},{16,0},{20,4},{24,8},{28,12},{1,17},{... | collective-permute-start | bytes 3932168 | tf_op jit(solution)/shard_map/ppermute | solution.py:302
  339.0 42.7 %collective-permute-start.12 = (bf16[512,1024]{1,0:T(8,128)(2,1)S(1)}, bf16[512,1024]{1,0:T(8,128)(2,1)S(1)}, u32[]{:S(2)}, u32[]{:S(2)}) collective-permute-start(bf16[512,1024]{1,0:T(8,128)(2,1)S(1)} %add_convert_fusion.6), channel_id=1, source_target_pairs={{0,4},{4,0},{8,12},{12,8},{16,20},{20,16},{24,28},{28,24},{1,5},{5... | collective-permute-start | bytes 3145736 | tf_op jit(solution)/shard_map/ppermute | solution.py:302
  400.7 47.0 %collective-permute-start.17 = (bf16[1024,1024]{1,0:T(8,128)(2,1)}, bf16[1024,1024]{1,0:T(8,128)(2,1)}, u32[]{:S(2)}, u32[]{:S(2)}) collective-permute-start(bf16[1024,1024]{1,0:T(8,128)(2,1)} %pad_maximum_fusion.4), channel_id=1, source_target_pairs={{0,8},{4,12},{8,0},{12,4},{16,24},{20,28},{24,16},{28,20},{1,9},{5... | collective-permute-start | bytes 6291464 | tf_op jit(solution)/shard_map/ppermute | solution.py:302
  417.0 118.2 %collective-permute-start.16 = (bf16[512,1024]{1,0:T(8,128)(2,1)}, bf16[512,1024]{1,0:T(8,128)(2,1)}, u32[]{:S(2)}, u32[]{:S(2)}) collective-permute-start(bf16[512,1024]{1,0:T(8,128)(2,1)} %fusion.71), channel_id=1, source_target_pairs={{0,4},{4,0},{8,12},{12,8},{16,20},{20,16},{24,28},{28,24},{1,5},{5... | collective-permute-start | bytes 3145736 | tf_op jit(solution)/shard_map/ppermute | solution.py:302
  438.5 76.4 %collective-permute-start.25 = (bf16[512,1024]{1,0:T(8,128)(2,1)}, bf16[512,1024]{1,0:T(8,128)(2,1)}, u32[]{:S(2)}, u32[]{:S(2)}) collective-permute-start(bf16[512,1024]{1,0:T(8,128)(2,1)} %fusion.73), channel_id=1, source_target_pairs={{0,4},{4,0},{8,12},{12,8},{16,20},{20,16},{24,28},{28,24},{1,5},{5... | collective-permute-start | bytes 3145736 | tf_op jit(solution)/shard_map/ppermute | solution.py:302
  498.9 6.9 collective-permute-start.27
  500.0 11.2 %collective-permute-start.18 = (bf16[512,1024]{1,0:T(8,128)(2,1)S(1)}, bf16[512,1024]{1,0:T(8,128)(2,1)S(1)}, u32[]{:S(2)}, u32[]{:S(2)}) collective-permute-start(bf16[512,1024]{1,0:T(8,128)(2,1)S(1)} %fusion.72), channel_id=1, source_target_pairs={{0,4},{4,0},{8,12},{12,8},{16,20},{20,16},{24,28},{28,24},{1,5},{5... | collective-permute-start | bytes 3145736 | tf_op jit(solution)/shard_map/ppermute | solution.py:302
  506.3 26.0 %collective-permute-start.28 = (bf16[512,1024]{1,0:T(8,128)(2,1)S(1)}, bf16[512,1024]{1,0:T(8,128)(2,1)S(1)}, u32[]{:S(2)}, u32[]{:S(2)}) collective-permute-start(bf16[512,1024]{1,0:T(8,128)(2,1)S(1)} %fusion.52), channel_id=1, source_target_pairs={{0,8},{4,12},{8,0},{12,4},{16,24},{20,28},{24,16},{28,20},{1,9},{5... | collective-permute-start | bytes 3145736 | tf_op jit(solution)/shard_map/ppermute | solution.py:302
  511.5 42.8 %collective-permute-start.19 = (bf16[512,1024]{1,0:T(8,128)(2,1)S(1)}, bf16[512,1024]{1,0:T(8,128)(2,1)S(1)}, u32[]{:S(2)}, u32[]{:S(2)}) collective-permute-start(bf16[512,1024]{1,0:T(8,128)(2,1)S(1)} %fusion.54), channel_id=1, source_target_pairs={{0,8},{4,12},{8,0},{12,4},{16,24},{20,28},{24,16},{28,20},{1,9},{5... | collective-permute-start | bytes 3145736 | tf_op jit(solution)/shard_map/ppermute | solution.py:302
  559.0 2.7 collective-permute-start.29
  560.5 31.3 %collective-permute-start.40 = (bf16[4,10,16,1024]{3,2,1,0:T(8,128)(2,1)S(1)}, bf16[4,10,16,1024]{3,2,1,0:T(8,128)(2,1)S(1)}, u32[]{:S(2)}, u32[]{:S(2)}) collective-permute-start(bf16[4,10,16,1024]{3,2,1,0:T(8,128)(2,1)S(1)} %bitcast.400), channel_id=1, source_target_pairs={{0,16},{4,20},{8,24},{12,28},{16,0},{20,4},{24,8},{28,12},{1,17},{... | collective-permute-start | bytes 3932168 | tf_op jit(solution)/shard_map/ppermute | solution.py:302
  564.0 48.0 %collective-permute-start.31 = (bf16[1024,1024]{1,0:T(8,128)(2,1)}, bf16[1024,1024]{1,0:T(8,128)(2,1)}, u32[]{:S(2)}, u32[]{:S(2)}) collective-permute-start(bf16[1024,1024]{1,0:T(8,128)(2,1)} %pad_maximum_fusion.6), channel_id=1, source_target_pairs={{0,8},{4,12},{8,0},{12,4},{16,24},{20,28},{24,16},{28,20},{1,9},{5... | collective-permute-start | bytes 6291464 | tf_op jit(solution)/shard_map/ppermute | solution.py:302
  593.4 227.1 %reduce-scatter.9.cloned.1.call-start = ((), (), s32[]{:S(2)}) async-start(), calls=%async_computation.15 | async-start | bytes 1638400 | tf_op jit(solution)/shard_map/reduce_scatter | solution.py:513
  623.9 34.8 %collective-permute-start.37 = (bf16[4,10,16,1024]{3,2,1,0:T(8,128)(2,1)S(1)}, bf16[4,10,16,1024]{3,2,1,0:T(8,128)(2,1)S(1)}, u32[]{:S(2)}, u32[]{:S(2)}) collective-permute-start(bf16[4,10,16,1024]{3,2,1,0:T(8,128)(2,1)S(1)} %bitcast.399), channel_id=1, source_target_pairs={{0,16},{4,20},{8,24},{12,28},{16,0},{20,4},{24,8},{28,12},{1,17},{... | collective-permute-start | bytes 3932168 | tf_op jit(solution)/shard_map/ppermute | solution.py:302
  660.4 166.7 %reduce-scatter.7.cloned.1.call-start = ((), (), s32[]{:S(2)}) async-start(), calls=%async_computation.14 | async-start | bytes 983040 | tf_op jit(solution)/shard_map/reduce_scatter | solution.py:513
  669.3 18.7 %collective-permute-start.36 = (bf16[4,24,16,256]{3,2,1,0:T(8,128)(2,1)S(1)}, bf16[4,24,16,256]{3,2,1,0:T(8,128)(2,1)S(1)}, u32[]{:S(2)}, u32[]{:S(2)}) collective-permute-start(bf16[4,24,16,256]{3,2,1,0:T(8,128)(2,1)S(1)} %bitcast.419), channel_id=1, source_target_pairs={{0,16},{4,20},{8,24},{12,28},{16,0},{20,4},{24,8},{28,12},{1,17},{... | collective-permute-start | bytes 2359304 | tf_op jit(solution)/shard_map/ppermute | solution.py:302
  689.2 144.8 %reduce-scatter.11.cloned.1.call-start = ((), (), s32[]{:S(2)}) async-start(), calls=%async_computation.16 | async-start | bytes 1310720 | tf_op jit(solution)/shard_map/reduce_scatter | solution.py:513
  704.4 23.9 %collective-permute-start.38 = (bf16[4,32,16,256]{3,2,1,0:T(8,128)(2,1)}, bf16[4,32,16,256]{3,2,1,0:T(8,128)(2,1)}, u32[]{:S(2)}, u32[]{:S(2)}) collective-permute-start(bf16[4,32,16,256]{3,2,1,0:T(8,128)(2,1)} %bitcast.357), channel_id=1, source_target_pairs={{0,16},{4,20},{8,24},{12,28},{16,0},{20,4},{24,8},{28,12},{1,17},{... | collective-permute-start | bytes 3145736 | tf_op jit(solution)/shard_map/ppermute | solution.py:302
  731.1 106.3 %reduce-scatter.13.cloned.1.call-start = ((), (), s32[]{:S(2)}) async-start(), calls=%async_computation.17 | async-start | bytes 983040 | tf_op jit(solution)/shard_map/reduce_scatter | solution.py:513
  740.7 17.7 %collective-permute-start.39 = (bf16[4,24,16,256]{3,2,1,0:T(8,128)(2,1)S(1)}, bf16[4,24,16,256]{3,2,1,0:T(8,128)(2,1)}, u32[]{:S(2)}, u32[]{:S(2)}) collective-permute-start(bf16[4,24,16,256]{3,2,1,0:T(8,128)(2,1)S(1)} %bitcast.418), channel_id=1, source_target_pairs={{0,16},{4,20},{8,24},{12,28},{16,0},{20,4},{24,8},{28,12},{1,17},{... | collective-permute-start | bytes 2359304 | tf_op jit(solution)/shard_map/ppermute | solution.py:302
  756.7 28.6 %collective-permute-start.41 = (bf16[4,32,16,256]{3,2,1,0:T(8,128)(2,1)}, bf16[4,32,16,256]{3,2,1,0:T(8,128)(2,1)}, u32[]{:S(2)}, u32[]{:S(2)}) collective-permute-start(bf16[4,32,16,256]{3,2,1,0:T(8,128)(2,1)} %bitcast.356), channel_id=1, source_target_pairs={{0,16},{4,20},{8,24},{12,28},{16,0},{20,4},{24,8},{28,12},{1,17},{... | collective-permute-start | bytes 3145736 | tf_op jit(solution)/shard_map/ppermute | solution.py:302
  760.8 78.8 %reduce-scatter.17.cloned.1.call-start = ((), (), s32[]{:S(2)}) async-start(), calls=%async_computation.19 | async-start | bytes 1310720 | tf_op jit(solution)/shard_map/reduce_scatter | solution.py:513
  763.3 30.0 %collective-permute-start.21 = (bf16[256,1024]{1,0:T(8,128)(2,1)}, bf16[256,1024]{1,0:T(8,128)(2,1)S(1)}, u32[]{:S(2)}, u32[]{:S(2)}) collective-permute-start(bf16[256,1024]{1,0:T(8,128)(2,1)} %get-tuple-element.111), channel_id=1, source_target_pairs={{1,0},{17,16},{0,1},{16,17},{5,2},{21,18},{4,3},{20,19},{3,4},{19,... | collective-permute-start | bytes 1572872 | tf_op jit(solution)/shard_map/ppermute | solution.py:340
  764.2 29.0 %collective-permute-start.20 = (bf16[256,1024]{1,0:T(8,128)(2,1)}, bf16[256,1024]{1,0:T(8,128)(2,1)}, u32[]{:S(2)}, u32[]{:S(2)}) collective-permute-start(bf16[256,1024]{1,0:T(8,128)(2,1)} %get-tuple-element.112), channel_id=1, source_target_pairs={{0,0},{16,16},{1,1},{17,17},{4,2},{20,18},{5,3},{21,19},{2,4},{18,... | collective-permute-start | bytes 1572872 | tf_op jit(solution)/shard_map/ppermute | solution.py:340
  776.1 6.9 collective-permute-start.32
  783.0 32.8 %collective-permute-start.30 = (bf16[512,1024]{1,0:T(8,128)(2,1)}, bf16[512,1024]{1,0:T(8,128)(2,1)}, u32[]{:S(2)}, u32[]{:S(2)}) collective-permute-start(bf16[512,1024]{1,0:T(8,128)(2,1)} %fusion.75), channel_id=1, source_target_pairs={{0,4},{4,0},{8,12},{12,8},{16,20},{20,16},{24,28},{28,24},{1,5},{5... | collective-permute-start | bytes 3145736 | tf_op jit(solution)/shard_map/ppermute | solution.py:302
  784.5 31.4 %collective-permute-start.33 = (bf16[512,1024]{1,0:T(8,128)(2,1)}, bf16[512,1024]{1,0:T(8,128)(2,1)}, u32[]{:S(2)}, u32[]{:S(2)}) collective-permute-start(bf16[512,1024]{1,0:T(8,128)(2,1)} %fusion.50), channel_id=1, source_target_pairs={{0,8},{4,12},{8,0},{12,4},{16,24},{20,28},{24,16},{28,20},{1,9},{5... | collective-permute-start | bytes 3145736 | tf_op jit(solution)/shard_map/ppermute | solution.py:302
  789.8 23.9 %all-to-all-start.4 = ((bf16[4,10,16,256]{3,2,1,0:T(8,128)(2,1)}), bf16[4,10,16,256]{3,2,1,0:T(8,128)(2,1)S(1)}, u32[]{:S(2)}, u32[]{:S(2)}) async-start(bf16[4,10,16,256]{3,2,1,0:T(8,128)(2,1)} %copy.272), calls=%async_computation.9 | async-start | bytes 655360 | tf_op jit(solution)/shard_map/all_to_all | solution.py:546
  822.4 10.2 %all-to-all-start.3 = ((bf16[4,10,16,256]{3,2,1,0:T(8,128)(2,1)}), bf16[4,10,16,256]{3,2,1,0:T(8,128)(2,1)S(1)}, u32[]{:S(2)}, u32[]{:S(2)}) async-start(bf16[4,10,16,256]{3,2,1,0:T(8,128)(2,1)} %copy.264), calls=%async_computation.5 | async-start | bytes 655360 | tf_op jit(solution)/shard_map/all_to_all | solution.py:546
  846.2 64.5 %all-to-all-start.5 = ((bf16[8,32,16,256]{3,2,1,0:T(8,128)(2,1)}), bf16[8,32,16,256]{3,2,1,0:T(8,128)(2,1)}, u32[]{:S(2)}, u32[]{:S(2)}) async-start(bf16[8,32,16,256]{3,2,1,0:T(8,128)(2,1)} %bitcast.370), calls=%async_computation.11 | async-start | bytes 4194304 | tf_op jit(solution)/shard_map/all_to_all | solution.py:565
  853.1 55.7 %copy-start.96 = (f32[448]{0:T(512)S(1)}, f32[448]{0:T(512)}, u32[]{:S(2)}) copy-start(f32[448]{0:T(512)} %param.21) | copy-start | bytes 5380
  853.1 55.7 %copy-start.104 = (f32[448]{0:T(512)S(1)}, f32[448]{0:T(512)}, u32[]{:S(2)}) copy-start(f32[448]{0:T(512)} %param.22) | copy-start | bytes 5380
  853.1 55.7 %copy-start.105 = (f32[448]{0:T(512)S(1)}, f32[448]{0:T(512)}, u32[]{:S(2)}) copy-start(f32[448]{0:T(512)} %param.23) | copy-start | bytes 5380
  853.2 56.3 %collective-permute-start.35 = (bf16[256,1024]{1,0:T(8,128)(2,1)S(1)}, bf16[256,1024]{1,0:T(8,128)(2,1)S(1)}, u32[]{:S(2)}, u32[]{:S(2)}) collective-permute-start(bf16[256,1024]{1,0:T(8,128)(2,1)S(1)} %get-tuple-element.103), channel_id=1, source_target_pairs={{1,0},{17,16},{0,1},{16,17},{5,2},{21,18},{4,3},{20,19},{3,4},{19,... | collective-permute-start | bytes 1572872 | tf_op jit(solution)/shard_map/ppermute | solution.py:340
  854.3 55.2 %collective-permute-start.34 = (bf16[256,1024]{1,0:T(8,128)(2,1)S(1)}, bf16[256,1024]{1,0:T(8,128)(2,1)S(1)}, u32[]{:S(2)}, u32[]{:S(2)}) collective-permute-start(bf16[256,1024]{1,0:T(8,128)(2,1)S(1)} %get-tuple-element.104), channel_id=1, source_target_pairs={{0,0},{16,16},{1,1},{17,17},{4,2},{20,18},{5,3},{21,19},{2,4},{18,... | collective-permute-start | bytes 1572872 | tf_op jit(solution)/shard_map/ppermute | solution.py:340
  (114 other events, 1070.2 us)
Sparse Core Ops, SparseCore 0:
  115.6 26.7 all-gather.12
  143.9 34.4 all-gather.14
  180.5 38.8 all-gather.8
  220.8 31.9 all-gather.10
  593.5 31.4 reduce-scatter.14
  660.6 32.0 reduce-scatter.8
  694.9 22.1 reduce-scatter.6
  731.2 27.3 reduce-scatter.10
  761.0 31.5 reduce-scatter.12
  795.3 30.9 reduce-scatter.16

commit v2 on v1

v2 whole, which is shorter than its diff:
```python
import functools

import jax
import jax.numpy as jnp
import numpy as np
from jax import lax
from jax.experimental import pallas as pl
from jax.experimental.pallas import tpu as pltpu
from jax.sharding import Mesh
from jax.sharding import PartitionSpec as P

HEADS = 16
HD = 64
ROT = 32
FF = 4096
LAYERS = 2
STEP = 10
DP = ("g", "x", "core")
ALL = ("g", "x", "core", "seq")
TP = 4

norm_epsilon = 1e-05
gelu_coeff = 0.7978845608
gelu_cubic = 0.044715
beta_first = 0.9
beta_second = 0.999
learn_rate = 0.05
small_rate = 0.3
decay_rate = 0.1
adam_epsilon = 1e-08
BIG = 1e30
BF = jnp.bfloat16
F32 = jnp.float32


def dot(left, right):
    return jnp.dot(left, right, preferred_element_type=F32)


def dot_nt(left, right):
    return lax.dot_general(left, right, (((1,), (1,)), ((), ())), preferred_element_type=F32)


def dot_tn(left, right):
    return lax.dot_general(left, right, (((0,), (0,)), ((), ())), preferred_element_type=F32)


def rotate_lanes(x, cos_t, low_t, high_t, sign):
    halves = []
    for part in range(x.shape[1] // 128):
        v = x[:, 128 * part : 128 * (part + 1)]
        up = pltpu.roll(v, 128 - ROT // 2, 1)
        down = pltpu.roll(v, ROT // 2, 1)
        halves.append(v * cos_t + sign * (up * low_t + down * high_t))
    return jnp.concatenate(halves, axis=1)


def head_of(shape):
    return lax.broadcasted_iota(jnp.int32, shape, 1) // HD


def half_place(flip_ref, row, half):
    if half is None:
        return row
    return pl.multiple_of((row // half + flip_ref[0]) % 2 * half + row % half, 256)


def attend_kernel(
    half, flip_ref, proj_ref, tab_ref, qx_ref, kx_ref, ctx_ref, rot_ref, lse_ref, k_s, v_s, q_s
):
    length, width = ctx_ref.shape
    heads = width // HD
    blk = min(256, length)
    span = half or length
    zero = jnp.zeros((), BF)
    head = head_of((span, width))
    for start in range(0, length, span):
        here = pl.ds(half_place(flip_ref, start, half), span)
        cos_t, low_t, high_t = tab_ref[0, here], tab_ref[1, here], tab_ref[2, here]
        proj = proj_ref[start : start + span]
        q = rotate_lanes(proj[:, :width], cos_t, low_t, high_t, 1.0).astype(BF)
        k = rotate_lanes(proj[:, width : 2 * width], cos_t, low_t, high_t, 1.0).astype(BF)
        v = proj[:, 2 * width :].astype(BF)
        rot_ref[here, :width] = q
        rot_ref[here, width : 2 * width] = k
        rot_ref[here, 2 * width :] = v
        q = q * BF(HD**-0.5)
        for h in range(heads):
            ext = (h + 1) % heads
            k_s[h, here] = jnp.where(head == h, k, jnp.where(head == ext, kx_ref[here], zero))
            v_s[h, here] = jnp.where(head == h, v, zero)
            q_s[h, here] = jnp.where(head == ext, qx_ref[here], q)
    tri = lax.broadcasted_iota(jnp.int32, (blk, blk), 0) <= lax.broadcasted_iota(
        jnp.int32, (blk, blk), 1
    )
    for i in range(length // blk):
        lo, hi = i * blk, (i + 1) * blk
        total = jnp.zeros((blk, width), F32)
        for h in range(heads):
            qb = q_s[h, lo:hi]
            diag = jnp.where(tri, dot_nt(k_s[h, lo:hi], qb), -BIG)
            top = jnp.max(diag, axis=0, keepdims=True)
            if i:
                past = dot_nt(k_s[h, :lo], qb)
                top = jnp.maximum(top, jnp.max(past, axis=0, keepdims=True))
            diag = jnp.exp(diag - top)
            mass = jnp.sum(diag, axis=0, keepdims=True)
            if i:
                past = jnp.exp(past - top)
                mass = mass + jnp.sum(past, axis=0, keepdims=True)
            lse_ref[h : h + 1, lo:hi] = top + jnp.log(mass)
            inv = 1.0 / mass
            total += dot_tn((diag * inv).astype(BF), v_s[h, lo:hi])
            if i:
                total += dot_tn((past * inv).astype(BF), v_s[h, :lo])
        ctx_ref[pl.ds(half_place(flip_ref, lo, half), blk)] = total.astype(BF)


def attend_back_kernel(
    half,
    flip_ref,
    rot_ref,
    dctx_ref,
    lse_ref,
    tab_ref,
    qx_ref,
    kx_ref,
    out_ref,
    k_s,
    v_s,
    q_s,
    dk_s,
    dv_s,
    dq_s,
):
    length, width = dctx_ref.shape
    heads = width // HD
    blk = min(256, length)
    head = head_of((length, width))
    zero = jnp.zeros((), BF)
    q = rot_ref[:, :width]
    k = rot_ref[:, width : 2 * width]
    v = rot_ref[:, 2 * width :]
    scaled = q * BF(HD**-0.5)
    for h in range(heads):
        ext = (h + 1) % heads
        k_s[h] = jnp.where(head == h, k, jnp.where(head == ext, kx_ref[...], zero))
        v_s[h] = jnp.where(head == h, v, zero)
        q_s[h] = jnp.where(head == ext, qx_ref[...], scaled)
    dk_s[...] = jnp.zeros_like(dk_s)
    dv_s[...] = jnp.zeros_like(dv_s)
    head_b = head_of((blk, width))
    tri = lax.broadcasted_iota(jnp.int32, (blk, blk), 0) <= lax.broadcasted_iota(
        jnp.int32, (blk, blk), 1
    )
    for i in range(length // blk):
        lo, hi = i * blk, (i + 1) * blk
        d_all = dctx_ref[pl.ds(half_place(flip_ref, lo, half), blk)]
        q_all = rot_ref[lo:hi, :width]
        total = jnp.zeros((blk, width), F32)
        for h in range(heads):
            qb = q_s[h, lo:hi]
            d_h = jnp.where(head_b == h, d_all, zero)
            q_h = jnp.where(head_b == h, q_all, zero)
            lse = lse_ref[h : h + 1, lo:hi]
            p_d = jnp.exp(jnp.where(tri, dot_nt(k_s[h, lo:hi], qb), -BIG) - lse)
            g_d = dot_nt(v_s[h, lo:hi], d_all)
            delta = jnp.sum(p_d * g_d, axis=0, keepdims=True)
            if i:
                p_p = jnp.exp(dot_nt(k_s[h, :lo], qb) - lse)
                g_p = dot_nt(v_s[h, :lo], d_all)
                delta = delta + jnp.sum(p_p * g_p, axis=0, keepdims=True)
            s_d = (p_d * (g_d - delta)).astype(BF)
            dv_s[lo:hi] += dot(p_d.astype(BF), d_h)
            dk_s[lo:hi] += dot(s_d, q_h)
            k_d = jnp.where(head_b == h, rot_ref[lo:hi, width : 2 * width], zero)
            total += dot_tn(s_d, k_d)
            if i:
                s_p = (p_p * (g_p - delta)).astype(BF)
                dv_s[:lo] += dot(p_p.astype(BF), d_h)
                dk_s[:lo] += dot(s_p, q_h)
                k_p = jnp.where(head_of((lo, width)) == h, rot_ref[:lo, width : 2 * width], zero)
                total += dot_tn(s_p, k_p)
        dq_s[lo:hi] = total
    scale = HD**-0.5
    cos_t, low_t, high_t = tab_ref[0], tab_ref[1], tab_ref[2]
    dq = rotate_lanes((dq_s[...] * scale).astype(BF).astype(F32), cos_t, low_t, high_t, -1.0)
    dk = rotate_lanes((dk_s[...] * scale).astype(BF).astype(F32), cos_t, low_t, high_t, -1.0)
    dv = dv_s[...]
    span = half or length
    for start in range(0, length, span):
        here = pl.ds(half_place(flip_ref, start, half), span)
        for n, grad in enumerate((dq, dk, dv)):
            out_ref[here, n * width : (n + 1) * width] = grad[start : start + span].astype(BF)


def attend(flip, half, proj, tables, q_ext, k_ext):
    length, width = proj.shape[0], proj.shape[1] // 3
    heads = width // HD
    return pl.pallas_call(
        functools.partial(attend_kernel, half),
        in_specs=[pl.BlockSpec(memory_space=pltpu.SMEM)]
        + [pl.BlockSpec(memory_space=pltpu.VMEM)] * 4,
        out_shape=(
            jax.ShapeDtypeStruct((length, width), BF),
            jax.ShapeDtypeStruct((length, 3 * width), BF),
            jax.ShapeDtypeStruct((8, length), F32),
        ),
        scratch_shapes=[pltpu.VMEM((heads, length, width), BF)] * 3,
        compiler_params=pltpu.CompilerParams(vmem_limit_bytes=50 << 20),
        cost_estimate=pl.CostEstimate(
            flops=heads * length * length * width * 2,
            bytes_accessed=length * width * 24,
            transcendentals=heads * length * length // 2,
        ),
        name="attend",
    )(flip, proj, tables, q_ext, k_ext)


def attend_back(flip, half, rot, d_context, lse, tables, q_ext, k_ext):
    length, width = d_context.shape
    heads = width // HD
    return pl.pallas_call(
        functools.partial(attend_back_kernel, half),
        in_specs=[pl.BlockSpec(memory_space=pltpu.SMEM)]
        + [pl.BlockSpec(memory_space=pltpu.VMEM)] * 6,
        out_shape=jax.ShapeDtypeStruct((length, 3 * width), BF),
        scratch_shapes=[pltpu.VMEM((heads, length, width), BF)] * 3
        + [pltpu.VMEM((length, width), F32)] * 3,
        compiler_params=pltpu.CompilerParams(vmem_limit_bytes=50 << 20),
        cost_estimate=pl.CostEstimate(
            flops=heads * length * length * width * 5,
            bytes_accessed=length * width * 24,
            transcendentals=heads * length * length // 2,
        ),
        name="attend_back",
    )(flip, rot, d_context, lse, tables, q_ext, k_ext)


def piece_row(at_ref, slot, side):
    z = (at_ref[1] + at_ref[2] * slot + 4) % 4
    g = at_ref[0] if side == 0 else 1 - at_ref[0]
    return pl.multiple_of(z * 32 + g * 16, 16)


def assemble_kernel(sources, plan, at_ref, *refs):
    n_in = 1 + max(source[0] for source in sources)
    ins, outs, flat = refs[:n_in], refs[n_in:-1], refs[-1]
    pieces = [
        (ins[ref] if index is None else ins[ref].at[index], piece_row(at_ref, slot, side))
        for ref, index, slot, side in sources
    ]
    for out_ref, (first, units, fold, parts) in zip(outs, plan):
        if fold == 1:
            rows = units // parts

            def put(u, carry):
                for part in range(parts):
                    for ref, row in pieces:
                        out_ref[pl.ds(u * 128 + row, 16), part * 256 : part * 256 + 256] = ref[
                            first + part * rows + u
                        ]
                return carry

            lax.fori_loop(0, rows, put, 0)
            continue

        def lay(u, carry):
            for ref, row in pieces:
                value = ref[first + u].astype(F32)
                for half in range(2):
                    flat[half, pl.ds(u * 128 + row, 16)] = value[:, 128 * half : 128 * (half + 1)]
            return carry

        lax.fori_loop(0, units, lay, 0)
        step = 128

        def take(n, carry):
            for p in range(fold):
                for half in range(2):
                    lane = p * 256 + half * 128
                    out_ref[pl.ds(n * step, step), lane : lane + 128] = flat[
                        half, pl.ds(n * step * fold + p, step, fold)
                    ].astype(BF)
            return carry

        lax.fori_loop(0, out_ref.shape[0] // step, take, 0)


def assemble(at, ins, sources, plan):
    vmem = pl.BlockSpec(memory_space=pltpu.VMEM)
    tall = max(units if fold > 1 else 1 for _, units, fold, _ in plan)
    total = sum(units for _, units, _, _ in plan)
    return pl.pallas_call(
        functools.partial(assemble_kernel, sources, plan),
        in_specs=[pl.BlockSpec(memory_space=pltpu.SMEM)] + [vmem] * len(ins),
        out_specs=[vmem] * len(plan),
        out_shape=[
            jax.ShapeDtypeStruct((units // parts * 128 // fold, 256 * fold * parts), BF)
            for _, units, fold, parts in plan
        ],
        scratch_shapes=[pltpu.VMEM((2, tall * 128, 128), F32)],
        compiler_params=pltpu.CompilerParams(vmem_limit_bytes=48 << 20),
        cost_estimate=pl.CostEstimate(
            flops=0, bytes_accessed=4 * total * 128 * 256, transcendentals=0
        ),
        name="assemble",
    )(at, *ins)


def disassemble_kernel(plan, at_ref, *refs):
    grads, outs, flat = refs[: len(plan)], refs[len(plan) : -1], refs[-1]
    pieces = [
        (
            outs[side].at[z] if len(outs) == 2 else outs[0].at[4 * side + z],
            piece_row(at_ref, z, side),
        )
        for side in range(2)
        for z in range(4)
    ]
    for g_ref, (first, units, fold, parts) in zip(grads, plan):
        if fold == 1:
            rows = units // parts

            def split(u, carry):
                for part in range(parts):
                    for ref, row in pieces:
                        ref[first + part * rows + u] = g_ref[
                            pl.ds(u * 128 + row, 16), part * 256 : part * 256 + 256
                        ].astype(BF)
                return carry

            lax.fori_loop(0, rows, split, 0)
            continue
        step = 128

        def lay(n, carry):
            for p in range(fold):
                for half in range(2):
                    lane = p * 256 + half * 128
                    flat[half, pl.ds(n * step * fold + p, step, fold)] = g_ref[
                        pl.ds(n * step, step), lane : lane + 128
                    ].astype(F32)
            return carry

        lax.fori_loop(0, g_ref.shape[0] // step, lay, 0)

        def give(u, carry):
            for ref, row in pieces:
                for half in range(2):
                    ref[first + u, :, 128 * half : 128 * (half + 1)] = flat[
                        half, pl.ds(u * 128 + row, 16)
                    ].astype(BF)
            return carry

        lax.fori_loop(0, units, give, 0)


def disassemble(at, grads, plan, one):
    vmem = pl.BlockSpec(memory_space=pltpu.VMEM)
    total = sum(units for _, units, _, _ in plan)
    tall = max(units if fold > 1 else 1 for _, units, fold, _ in plan)
    out = [jax.ShapeDtypeStruct((8 if one else 4, total, 16, 256), BF)] * (1 if one else 2)
    return pl.pallas_call(
        functools.partial(disassemble_kernel, plan),
        in_specs=[pl.BlockSpec(memory_space=pltpu.SMEM)] + [vmem] * len(grads),
        out_specs=[vmem] * len(out),
        out_shape=out,
        scratch_shapes=[pltpu.VMEM((2, tall * 128, 128), F32)],
        compiler_params=pltpu.CompilerParams(vmem_limit_bytes=48 << 20),
        cost_estimate=pl.CostEstimate(
            flops=0, bytes_accessed=6 * total * 128 * 256, transcendentals=0
        ),
        name="disassemble",
    )(at, *grads)


def adam_update(weights, grads, moment_one, moment_two, rate, decay):
    new_one = beta_first * moment_one + (1.0 - beta_first) * grads
    new_two = beta_second * moment_two + (1.0 - beta_second) * grads * grads
    corrected_one = new_one / (1.0 - beta_first**STEP)
    corrected_two = new_two / (1.0 - beta_second**STEP)
    new_weights = weights - rate * (
        corrected_one / (jnp.sqrt(corrected_two) + adam_epsilon) + decay * weights
    )
    return (new_weights, new_one, new_two)


def pack_kernel(masters_ref, out_ref, flat):
    slots = masters_ref.shape[0]
    for c in range(32):
        for part in range(8):
            place = (c // 16) * TP + part // 2
            flat[part % 2, pl.ds(place * slots * 16 + c % 16, slots, 16)] = masters_ref[
                :, c * 1024 + part * 128 : c * 1024 + part * 128 + 128
            ]
    for place in range(8):
        for side in range(2):
            out_ref[place, :, side * 128 : side * 128 + 128] = flat[
                side, place * slots * 16 : (place + 1) * slots * 16
            ].astype(BF)


def pack(masters):
    slots, piece = masters.shape
    return pl.pallas_call(
        pack_kernel,
        grid=(slots // 8,),
        in_specs=[pl.BlockSpec((8, piece), lambda i: (i, 0))],
        out_specs=pl.BlockSpec((8, 128, 256), lambda i: (0, i, 0)),
        out_shape=jax.ShapeDtypeStruct((8, slots * 16, 256), BF),
        scratch_shapes=[pltpu.VMEM((2, 1024, 128), F32)],
        compiler_params=pltpu.CompilerParams(vmem_limit_bytes=60 << 20),
        cost_estimate=pl.CostEstimate(
            flops=0, bytes_accessed=6 * slots * piece, transcendentals=0
        ),
        name="pack",
    )(masters)


def select_kernel(picks, table_ref, from_ref, *outs):
    for out_ref, blocks in zip(outs, picks):
        for n, block in enumerate(blocks):
            out_ref[n] = from_ref[pl.ds(pl.multiple_of(table_ref[block] * 16, 16), 16)]


def select(table, received, picks):
    vmem = pl.BlockSpec(memory_space=pltpu.VMEM)
    rows = received.shape[0]
    return pl.pallas_call(
        functools.partial(select_kernel, picks),
        in_specs=[pl.BlockSpec(memory_space=pltpu.SMEM), vmem],
        out_specs=[vmem] * len(picks),
        out_shape=[jax.ShapeDtypeStruct((len(p), 16, 256), BF) for p in picks],
        compiler_params=pltpu.CompilerParams(vmem_limit_bytes=60 << 20),
        cost_estimate=pl.CostEstimate(flops=0, bytes_accessed=rows * 900, transcendentals=0),
        name="select",
    )(table, received)


def place_kernel(takes, table_ref, turn_ref, extra_ref, *refs):
    ins, out_ref = refs[:-1], refs[-1]
    slots = out_ref.shape[1] // 16 - 1
    out_ref[...] = jnp.zeros_like(out_ref)
    for place in range(out_ref.shape[0]):
        out_ref[place, slots * 16 :] = extra_ref[place]
    for ref, take in zip(ins, takes):
        for n, (block, turn) in enumerate(take):
            if turn is not None:
                block = block + 2 * (turn_ref[0] ^ turn)
            slot = table_ref[block]
            out_ref[slot // slots, pl.ds(pl.multiple_of(slot % slots * 16, 16), 16)] = ref[n]


def place_blocks(table, turn, extra, ins, takes, slots):
    vmem = pl.BlockSpec(memory_space=pltpu.VMEM)
    smem = pl.BlockSpec(memory_space=pltpu.SMEM)
    return pl.pallas_call(
        functools.partial(place_kernel, takes),
        in_specs=[smem, smem, vmem] + [vmem] * len(ins),
        out_specs=vmem,
        out_shape=jax.ShapeDtypeStruct((8, slots * 16 + 16, 256), BF),
        compiler_params=pltpu.CompilerParams(vmem_limit_bytes=60 << 20),
        cost_estimate=pl.CostEstimate(flops=0, bytes_accessed=4 << 20, transcendentals=0),
        name="place",
    )(table, turn, extra, *ins)


def adam_kernel(from_ref, w_ref, one_ref, two_ref, w_out, one_out, two_out, low_out, flat):
    slots = w_ref.shape[0]
    part = pl.program_id(1)

    @pl.when(part == 0)
    def _():
        for place in range(8):
            for side in range(2):
                flat[side, place * slots * 16 : (place + 1) * slots * 16] = from_ref[
                    place, :, side * 128 : side * 128 + 128
                ].astype(F32)

    for c in range(8):
        for lane in range(8):
            at = slice(c * 1024 + lane * 128, c * 1024 + lane * 128 + 128)
            row = ((part // 2) * TP + lane // 2) * slots * 16 + (part % 2) * 8 + c
            grads = flat[lane % 2, pl.ds(row, slots, 16)]
            new, one, two = adam_update(
                w_ref[:, at], grads, one_ref[:, at], two_ref[:, at], learn_rate, decay_rate
            )
            w_out[:, at] = new
            one_out[:, at] = one
            two_out[:, at] = two
            low_out[:, at] = new.astype(BF)


def adam(received, masters, first_moment, second_moment):
    slots, piece = masters.shape
    block = pl.BlockSpec((16, piece // 4), lambda i, j: (i, j))
    whole = jax.ShapeDtypeStruct(masters.shape, F32)
    return pl.pallas_call(
        adam_kernel,
        grid=(slots // 16, 4),
        in_specs=[pl.BlockSpec((8, 256, 256), lambda i, j: (0, i, 0))] + [block] * 3,
        out_specs=[block] * 4,
        out_shape=[whole, whole, whole, jax.ShapeDtypeStruct(masters.shape, BF)],
        scratch_shapes=[pltpu.VMEM((2, 2048, 128), F32)],
        compiler_params=pltpu.CompilerParams(vmem_limit_bytes=60 << 20),
        cost_estimate=pl.CostEstimate(
            flops=20 * slots * piece, bytes_accessed=28 * slots * piece, transcendentals=0
        ),
        name="adam",
    )(received, masters, first_moment, second_moment)


@functools.lru_cache(maxsize=None)
def row_moves(n_seq, rows_here, length):
    local = length // n_seq
    per_dev = rows_here * local
    edges = {}
    for t in range(TP):
        for z in range(n_seq):
            for k in range(rows_here):
                row = rows_here * t + k
                token = (row // n_seq) * length + z * local
                target = (token // per_dev) * n_seq + row % n_seq
                edges.setdefault(t * n_seq + z, []).append((target, k, token % per_dev // local))
    steps = []
    for _ in range(rows_here):
        taken = {}

        def place(source, seen):
            for edge in edges[source]:
                if edge[0] not in seen:
                    seen.add(edge[0])
                    if edge[0] not in taken or place(taken[edge[0]][0], seen):
                        taken[edge[0]] = (source, edge)
                        return True
            return False

        for source in edges:
            assert place(source, set())
        pick = np.zeros(TP * n_seq, np.int32)
        put = np.zeros(TP * n_seq, np.int32)
        pairs = []
        for target, (source, edge) in taken.items():
            edges[source].remove(edge)
            pick[source] = edge[1]
            put[target] = edge[2]
            pairs.append((source, target))
        steps.append((sorted(pairs), pick, put))
    return steps


def body(
    tokens,
    cotangent,
    lengths,
    owners,
    masters,
    first_moment,
    second_moment,
    small_params,
    small_first,
    small_second,
):
    n_g = lax.axis_size("g")
    n_seq = lax.axis_size("seq")
    n_dp = n_g * TP
    capacity, piece = masters.shape
    n_blocks = owners.shape[0]
    rows_here, local, width = tokens.shape
    length = local * n_seq
    per_dev = rows_here * local
    group_rows = TP * per_dev // length
    cols = width // TP
    chunks = piece // width // n_g
    place_dp = lax.axis_index(DP)
    place_z = lax.axis_index("seq")
    t = place_dp % TP
    g = place_dp // TP
    core, side = t % 2, t // 2

    def swap(value, bit):
        return lax.ppermute(value, DP, [(i, i ^ bit) for i in range(n_dp)])

    pieces = n_seq == 4 and n_g == 2 and chunks == 16 and cols == 256 and capacity % 16 == 0
    at_hops = jnp.stack([g, place_z, -1]).astype(jnp.int32)
    at_near = jnp.stack([g, 0, 1]).astype(jnp.int32)
    at_all = jnp.array([0, 0, 1], jnp.int32)
    tie = lax.optimization_barrier
    n_all = n_dp * n_seq

    def to_all(value):
        return lax.all_to_all(
            value, ALL, split_axis=0, concat_axis=0, tiled=True
        )

    def order(first, second, flag):
        return jnp.concatenate(
            [jnp.where(flag == 0, first, second), jnp.where(flag == 0, second, first)], axis=0
        )

    steps = row_moves(n_seq, rows_here, length)

    def row_pairs(pairs, back):
        out = []
        for source, target in pairs:
            for a in range(n_g):
                ends = (a * TP * n_seq + source, a * TP * n_seq + target)
                out.append(ends[::-1] if back else ends)
        return out

    me = t * n_seq + place_z

    def to_rows(value):
        parts = []
        for pairs, pick, _ in steps:
            send = lax.dynamic_index_in_dim(value, jnp.asarray(pick)[me], 1, keepdims=False)
            parts.append(lax.ppermute(send, ALL, row_pairs(pairs, False)))
        puts = [jnp.asarray(put)[me] for _, _, put in steps]
        slots = []
        for s in range(rows_here):
            out = parts[0]
            for j in range(1, rows_here):
                out = jnp.where(puts[j] == s, parts[j], out)
            slots.append(out)
        return jnp.concatenate(slots, axis=1)

    def from_rows(value):
        value = value.reshape(rows_here, local, width)
        parts = []
        for pairs, _, put in steps:
            send = lax.dynamic_index_in_dim(value, jnp.asarray(put)[me], 0, keepdims=False)
            parts.append(lax.ppermute(send, ALL, row_pairs(pairs, True)))
        picks = [jnp.asarray(pick)[me] for _, pick, _ in steps]
        slots = []
        for s in range(rows_here):
            out = parts[0]
            for j in range(1, rows_here):
                out = jnp.where(picks[j] == s, parts[j], out)
            slots.append(out)
        return jnp.stack(slots, axis=0)

    block_index = jnp.arange(n_blocks, dtype=jnp.int32)
    same_owner = owners[:, None] == owners[None, :]
    earlier = block_index[None, :] < block_index[:, None]
    slot_rank = jnp.sum((same_owner & earlier).astype(jnp.int32), axis=1)
    slot_of_block = owners * capacity + slot_rank
    slot_ids = jnp.arange(n_dp * capacity, dtype=jnp.int32)
    hit = slot_of_block[None, :] == slot_ids[:, None]
    block_of_slot = jnp.sum(jnp.where(hit, block_index[None, :], 0), axis=1) + jnp.where(
        jnp.any(hit, axis=1), 0, n_blocks
    )

    if pieces:
        packed = pack(masters)
    else:
        packed = masters.astype(BF).reshape(capacity, n_g, chunks, TP, cols)
        packed = packed.transpose(1, 3, 0, 2, 4).reshape(n_dp, capacity * chunks, cols)
    small_here = small_params.shape[0]
    small_width = -(-(small_here + 2 * lengths.size) // 512) * 512
    note = jnp.concatenate(
        [
            small_params.astype(BF),
            (lengths.reshape(-1) // 32).astype(BF),
            (lengths.reshape(-1) % 32).astype(BF),
        ]
    )
    note = jnp.pad(note, (0, small_width - note.shape[0]))
    tokens, cotangent, packed = tie((tokens, cotangent, packed))
    both_rows = to_rows(jnp.stack([tokens, cotangent]))
    received = lax.all_to_all(packed, DP, split_axis=0, concat_axis=0, tiled=True)
    note, received, both_rows = tie((note, received, both_rows))
    token_rows, cotangent_rows = both_rows[0], both_rows[1]
    notes = to_all(jnp.broadcast_to(note[None], (n_all, small_width)))

    unit_rows = n_seq * n_g * chunks
    n_qkv = 3 * width // unit_rows
    n_out = width // unit_rows
    n_in = FF // unit_rows
    per_layer = n_qkv + n_out + 2 * n_in
    my_out = n_out // TP
    fold = FF // width

    def spread(value):
        return lax.all_gather(value, ("g", "seq"), axis=0)

    def build_hops(hops, plan):
        if not pieces:
            return build(hops, plan)
        own, along = hops
        ins = [own, *along, swap(own, TP), swap(jnp.stack(along), TP)]
        sources = [(by, None, by, 0) for by in range(n_seq)]
        sources += [(n_seq, None, 0, 1)]
        sources += [(n_seq + 1, by - 1, by, 1) for by in range(1, n_seq)]
        return assemble(at_hops, ins, sources, plan)

    def build(every, plan):
        if pieces:
            sources = [(0, a * n_seq + z, z, a) for a in range(n_g) for z in range(n_seq)]
            return assemble(at_all, [every], sources, plan)
        out = []
        for first, units, fold, parts in plan:
            rows = units // parts
            part = every[:, first : first + units]
            part = part.reshape(n_g, n_seq, parts, rows, chunks, cols).transpose(3, 1, 0, 4, 2, 5)
            out.append(part.reshape(rows * unit_rows // fold, parts * cols * fold))
        return out

    my_units = (1 + fold) * my_out
    n_both = TP * my_units

    def parts_of(layer):
        start = layer * per_layer
        qkv = list(range(start, start + n_qkv))
        inner = list(range(start + n_qkv + n_out, start + n_qkv + n_out + n_in))
        turned = []
        for a in range(TP):
            turned.append([start + n_qkv + my_out * a + e for e in range(my_out)])
            for q in range(fold):
                down = start + n_qkv + n_out + n_in + (q * TP + a) * my_out
                turned[a] += [down + e for e in range(my_out)]
        return qkv, inner, turned

    qkv0, in0, turned0 = parts_of(0)
    qkv1, in1, turned1 = parts_of(1)
    turned = [b for a in range(TP) for b in turned0[a] + turned1[a]]
    picks = [qkv0, in0, turned, qkv1 + in1]
    if pieces:
        m_qkv0, m_in0, swapped, m_rest1 = select(
            slot_of_block, received.reshape(n_dp * capacity * chunks, cols), picks
        )
    else:
        blocks = received.reshape(n_dp * capacity, chunks, cols)[slot_of_block]
        m_qkv0, m_in0, swapped, m_rest1 = [blocks[jnp.array(p)] for p in picks]
    swapped = swapped.reshape(TP, 2 * my_units, chunks, cols)
    plan_qkv = (0, n_qkv, 3, 1)
    plan_both = (0, n_both, 1, TP)
    def hop_z(value):
        return [
            lax.ppermute(value, "seq", [(i, (i + by) % n_seq) for i in range(n_seq)])
            for by in range(1, n_seq)
        ]

    m_qkv0, swapped, notes = tie((m_qkv0, swapped, notes))
    z_qkv0 = (m_qkv0, hop_z(m_qkv0)) if pieces else spread(m_qkv0)
    swapped = lax.all_to_all(swapped, ("x", "core"), split_axis=0, concat_axis=0, tiled=True)
    m_both0 = swapped[:, :my_units].reshape(n_both, chunks, cols)
    m_both1 = swapped[:, my_units:].reshape(n_both, chunks, cols)
    z_rest0 = spread(jnp.concatenate([m_in0, m_both0]))
    z_rest1 = spread(jnp.concatenate([m_rest1, m_both1]))

    small_all = notes[:, :small_here].reshape(-1)
    pairs = notes[::n_seq, small_here : small_here + 2 * lengths.size].astype(jnp.int32)
    pairs = pairs.reshape(n_dp, 2, rows_here, lengths.shape[1])
    all_lengths = (pairs[:, 0] * 32 + pairs[:, 1]).reshape(n_dp * rows_here, -1)
    vectors = []
    for layer in range(LAYERS):
        base = layer * (3 * width + FF)
        small_f = small_all[base : base + 3 * width + FF].astype(F32)
        bias_in = lax.dynamic_index_in_dim(
            small_f[2 * width : 2 * width + FF].reshape(fold, TP, cols), t, 1, keepdims=False
        ).reshape(-1)
        vectors.append(
            (small_f[:width], small_f[width : 2 * width], bias_in, small_f[2 * width + FF :])
        )

    mine_rows = jnp.arange(group_rows) * n_seq + place_z
    if group_rows == 2:
        mine_rows = jnp.where(side == 0, mine_rows, mine_rows[::-1])
    row_lengths = all_lengths[g * TP * rows_here + mine_rows]
    ends = jnp.cumsum(row_lengths, axis=1)
    starts = ends - row_lengths
    places = jnp.arange(length, dtype=jnp.int32)
    segment = jnp.sum((places[None, :, None] >= ends[:, None, :]).astype(jnp.int32), axis=2)
    which = segment[:, :, None] == jnp.arange(lengths.shape[1], dtype=jnp.int32)[None, None, :]
    within = places[None, :] - jnp.sum(jnp.where(which, starts[:, None, :], 0), axis=2)
    lane = jnp.arange(128)
    feature = lane % HD
    inverse = 1.0 / 10000.0 ** (jnp.arange(0, ROT, 2, dtype=F32) / ROT)
    angle = within.astype(F32)[..., None] * jnp.tile(inverse, 128 // (ROT // 2))
    cosine, sine = jnp.cos(angle), jnp.sin(angle)
    tables = jnp.stack(
        [
            jnp.where(feature < ROT, cosine, 1.0),
            jnp.where(feature < ROT // 2, -sine, 0.0),
            jnp.where((feature >= ROT // 2) & (feature < ROT), sine, 0.0),
        ],
        axis=1,
    )
    wide = jnp.arange(cols) % HD
    hits = segment[:, :, None] == wide[None, None, :]
    q_ext = jnp.where(hits, 1.0, 0.0).astype(BF)
    k_ext = jnp.where(hits | (wide >= lengths.shape[1])[None, None, :], 0.0, -BIG).astype(BF)

    half = 2 * per_dev // 2 if group_rows == 2 else None
    flip = jnp.full((1,), core, jnp.int32)

    def gather_group(value):
        far = swap(value, 2)
        near = swap(value, 1)
        far_near = swap(far, 1)
        if group_rows == 2:
            return [jnp.concatenate([value, near]), jnp.concatenate([far, far_near])]
        own, other = order(value, near, core), order(far, far_near, core)
        return [order(own, other, side)]

    def halve(value):
        if group_rows == 2:
            keep, send = value[:per_dev], value[per_dev:]
        else:
            value = value.reshape(2, per_dev, width)
            keep = lax.dynamic_index_in_dim(value, core, 0, keepdims=False)
            send = lax.dynamic_index_in_dim(value, 1 - core, 0, keepdims=False)
        return keep + swap(send.astype(BF), 1).astype(F32)

    def scatter_far(part):
        return swap(halve(part).astype(BF), 2)

    def scatter_pair(parts):
        if group_rows == 2:
            return parts
        pair = parts[0].reshape(2, 2 * per_dev, width)
        own = lax.dynamic_index_in_dim(pair, side, 0, keepdims=False)
        other = lax.dynamic_index_in_dim(pair, 1 - side, 0, keepdims=False)
        return own, other

    def scatter_group(parts):
        own, other = scatter_pair(parts)
        far = scatter_far(other)
        return halve(own) + far.astype(F32)

    state = token_rows.astype(F32)

    def norm(state, vector):
        gain, shift = vector[0], vector[1]
        centered = state - jnp.mean(state, axis=-1, keepdims=True)
        inv_std = lax.rsqrt(jnp.mean(centered * centered, axis=-1, keepdims=True) + norm_epsilon)
        normed = centered * inv_std
        return normed, inv_std, (normed * gain + shift).astype(BF)

    def front(hiddens, w_qkv):
        return [dot(hidden, w_qkv) for hidden in hiddens]

    def attention(projs):
        return [attend(flip, half, proj, tables[r], q_ext[r], k_ext[r]) for r, proj in enumerate(projs)]

    def gelu_pair(inner):
        tanh_part = jnp.tanh(gelu_coeff * (inner + gelu_cubic * inner * inner * inner))
        active = 0.5 * inner * (1.0 + tanh_part)
        slope = 0.5 * (1.0 + tanh_part) + 0.5 * inner * (1.0 - tanh_part * tanh_part) * (
            gelu_coeff * (1.0 + 3.0 * gelu_cubic * inner * inner)
        )
        return active.astype(BF), slope.astype(BF)

    def inside(hiddens, w_in, bias_in):
        pairs = [gelu_pair(dot(hidden, w_in) + bias_in) for hidden in hiddens]
        return [slope for _, slope in pairs], [active for active, _ in pairs]

    normed0, inv_std0, hidden = norm(state, vectors[0])
    hiddens0 = gather_group(hidden)
    (w_qkv0,) = build_hops(z_qkv0, [plan_qkv])
    attended0 = attention(front(hiddens0, w_qkv0))
    d_branch, attended0[0] = tie((cotangent_rows, attended0[0]))
    d_branch_rows = gather_group(d_branch)
    z_rest0, d_branch_rows = tie((z_rest0, d_branch_rows))
    w_in0, both = build(z_rest0, [(0, n_in, fold, 1), (n_in, n_both, 1, TP)])
    inners0, actives0 = inside(hiddens0, w_in0, vectors[0][2])
    w_out0, w_down0 = both[:cols], both[cols:]
    parts = [None] * len(hiddens0)
    for r in reversed(range(len(hiddens0))):
        parts[r] = dot(attended0[r][0], w_out0) + dot(actives0[r], w_down0)
    state = state + scatter_group(parts) + vectors[0][3]
    normed1, inv_std1, hidden = norm(state, vectors[1])
    hiddens1 = gather_group(hidden)
    w_qkv1, w_in1, both = build(
        z_rest1, [plan_qkv, (n_qkv, n_in, fold, 1), (n_qkv + n_in, n_both, 1, TP)]
    )
    attended1 = attention(front(hiddens1, w_qkv1))
    inners1, actives1 = inside(hiddens1, w_in1, vectors[1][2])
    w_out1, w_down1 = both[:cols], both[cols:]
    parts = [
        dot(attended1[r][0], w_out1) + dot(actives1[r], w_down1) for r in range(len(hiddens1))
    ]
    outputs = (state + scatter_group(parts) + vectors[1][3]).astype(BF)

    def lay_out(grads, plan):
        if pieces:
            return disassemble(at_all, grads, plan, True)[0]
        every = []
        for grad, (_, units, fold, parts) in zip(grads, plan):
            rows = units // parts
            grad = grad.astype(BF).reshape(rows, n_seq, n_g, chunks, parts, cols)
            grad = grad.transpose(2, 1, 4, 0, 3, 5)
            every.append(grad.reshape(n_g * n_seq, units, chunks, cols))
        return jnp.concatenate(every, axis=1)

    def sum_all(laid):
        return lax.psum_scatter(laid, ("g", "seq"), scatter_dimension=0, tiled=False)

    def lay_near(grads, plan):
        return disassemble(at_near, grads, plan, False) if pieces else lay_out(grads, plan)

    def sum_g(laid):
        if not pieces:
            return sum_all(laid)
        keep, send = laid
        return (keep.astype(F32) + swap(send, TP).astype(F32)).astype(BF)

    def sum_z(total):
        if not pieces:
            return total
        total = lax.all_to_all(total, "seq", split_axis=0, concat_axis=0, tiled=True)
        return jnp.sum(total.astype(F32), axis=0).astype(BF)

    def both_grads(d_rows, attended, actives):
        g_out = sum(dot_tn(a[0], d) for a, d in zip(attended, d_rows))
        g_down = sum(dot_tn(a, d) for a, d in zip(actives, d_rows))
        return jnp.concatenate([g_out, g_down])

    def back_inner(d_row, inner, w_down):
        return (dot_nt(d_row, w_down) * inner.astype(F32)).astype(BF)

    def back_attention(r, d_row, attended, w_out):
        d_context = dot_nt(d_row, w_out).astype(BF)
        return attend_back(flip, half, attended[1], d_context, attended[2], tables[r], q_ext[r], k_ext[r])

    def back_norm(d_state, d_hidden, normed, inv_std, vector):
        d_normed = d_hidden * vector[0]
        return d_state + inv_std * (
            d_normed
            - jnp.mean(d_normed, axis=-1, keepdims=True)
            - normed * jnp.mean(d_normed * normed, axis=-1, keepdims=True)
        )

    def sums(d_hidden, normed, d_inners, d_branch):
        g_bias_in = sum(jnp.sum(d.astype(F32), axis=0) for d in d_inners)
        wide_bias = (
            (jnp.arange(TP) == t).astype(F32)[None, :, None] * g_bias_in.reshape(fold, 1, cols)
        ).reshape(-1)
        return jnp.concatenate(
            [
                jnp.sum(d_hidden * normed, axis=0),
                jnp.sum(d_hidden, axis=0),
                wide_bias,
                jnp.sum(d_branch.astype(F32), axis=0),
            ]
        )

    turns = range(group_rows)
    last = group_rows - 1
    d_inners1, d_projs1, parts = [None] * group_rows, [None] * group_rows, [None] * group_rows
    d_rows = d_branch_rows
    for r in turns:
        d_inners1[r] = back_inner(d_rows[r], inners1[r], w_down1)
    g_in = sum(dot_tn(hiddens1[r], d_inners1[r]) for r in turns)
    laid = lay_out(
        [g_in, both_grads(d_rows, attended1, actives1)],
        [(0, n_in, fold, 1), (n_in, n_both, 1, TP)],
    )
    laid, d_rows, d_inners1 = tie((laid, d_rows, d_inners1))
    r_early1 = sum_all(laid)
    for r in reversed(turns):
        d_projs1[r] = back_attention(r, d_rows[r], attended1[r], w_out1)
        parts[r] = dot_nt(d_inners1[r], w_in1) + dot_nt(d_projs1[r], w_qkv1)
        if r == last and last:
            parts[r], d_rows, outputs = tie((parts[r], d_rows, outputs))
    d_state = cotangent_rows.astype(F32)
    d_hidden1 = scatter_group(parts)
    d_state = back_norm(d_state, d_hidden1, normed1, inv_std1, vectors[1])
    d_branch = d_state.astype(BF)
    d_branch, d_projs1, r_early1, outputs = tie((d_branch, d_projs1, r_early1, outputs))
    outputs = from_rows(outputs)
    d_rows = gather_group(d_branch)
    g_qkv = sum(dot_tn(hiddens1[r], d_projs1[r]) for r in turns)
    laid = lay_out([g_qkv], [plan_qkv])
    d_rows[0], laid = tie((d_rows[0], laid))
    r_qkv1 = sum_all(laid)
    d_inners0, d_projs0 = [None] * group_rows, [None] * group_rows
    d_inners0[0] = back_inner(d_rows[0], inners0[0], w_down0)
    d_projs0[0] = back_attention(0, d_rows[0], attended0[0], w_out0)
    d_rows, d_projs0[0], d_inners0[0] = tie((d_rows, d_projs0[0], d_inners0[0]))
    laid = lay_near([both_grads(d_rows, attended0, actives0)], [plan_both])
    d_rows, laid = tie((d_rows, laid))
    s_both0 = sum_g(laid)
    for r in turns[1:]:
        d_inners0[r] = back_inner(d_rows[r], inners0[r], w_down0)
    g_in = sum(dot_tn(hiddens0[r], d_inners0[r]) for r in turns)
    laid = lay_near([g_in], [(0, n_in, fold, 1)])
    d_rows, laid, s_both0 = tie((d_rows, laid, s_both0))
    r_both0 = sum_z(s_both0)
    s_in0 = sum_g(laid)
    for r in turns[1:]:
        d_projs0[r] = back_attention(r, d_rows[r], attended0[r], w_out0)
    g_qkv = sum(dot_tn(hiddens0[r], d_projs0[r]) for r in turns)
    laid = lay_near([g_qkv], [plan_qkv])
    d_projs0, laid, s_in0 = tie((d_projs0, laid, s_in0))
    s_qkv0 = sum_g(laid)
    for r in reversed(turns):
        parts[r] = dot_nt(d_inners0[r], w_in0) + dot_nt(d_projs0[r], w_qkv0)
    parts, r_both0, s_in0, r_qkv1 = tie((parts, r_both0, s_in0, r_qkv1))
    r_in0 = sum_z(s_in0)
    s_qkv0, r_in0 = tie((s_qkv0, r_in0))
    r_qkv0 = sum_z(s_qkv0)
    d_hidden0 = scatter_group(parts)
    small_grads = [
        sums(d_hidden0, normed0, d_inners0, d_branch),
        sums(d_hidden1, normed1, d_inners1, cotangent_rows),
    ]
    d_state = back_norm(d_state, d_hidden0, normed0, inv_std0, vectors[0])
    swapped = jnp.concatenate(
        [r.reshape(TP, my_units, chunks, cols) for r in (r_both0, r_early1[n_in:])], axis=1
    )
    mine = [lax.dynamic_index_in_dim(swapped, t ^ k, 0, keepdims=False) for k in range(TP)]
    mine = [mine[0]] + [swap(mine[k], k) for k in range(1, TP)]
    grad_in = from_rows(d_state.astype(BF))
    small_flat = jnp.concatenate(small_grads).reshape(n_all, small_here)
    small_flat = jnp.pad(small_flat, ((0, 0), (0, small_width - small_here)))
    if pieces:
        extra = small_flat.astype(BF).reshape(n_dp, -1, cols)
        extra = jnp.pad(extra, ((0, 0), (0, 16 - extra.shape[1]), (0, 0)))
        ins = [r_qkv0, r_in0, r_qkv1, r_early1[:n_in]] + mine
        takes = [[(b, None) for b in blocks] for blocks in (qkv0, in0, qkv1, in1)]
        takes += [[(b, k) for b in turned0[0] + turned1[0]] for k in range(TP)]
        slots = place_blocks(
            slot_of_block, jnp.full((1,), t, jnp.int32), extra, ins, takes, capacity
        )
        owned = lax.all_to_all(slots, DP, split_axis=0, concat_axis=0, tiled=True)
        small_part = owned[:, capacity * chunks :].astype(F32).sum(axis=0)
        small_part = small_part.reshape(-1, small_width)[:n_seq]
        small_owned = lax.all_to_all(
            small_part, "seq", split_axis=0, concat_axis=0, tiled=True
        ).sum(axis=0)[:small_here]
    else:
        swapped = jnp.stack(mine)[jnp.arange(TP) ^ t]
        ordered = [r_qkv0, r_in0, swapped.reshape(-1, chunks, cols), r_qkv1, r_early1[:n_in]]
        index = np.zeros(n_blocks + 1, np.int32)
        index[np.array(qkv0 + in0 + turned + qkv1 + in1)] = np.arange(n_blocks)
        index[n_blocks] = n_blocks
        grads = jnp.concatenate(ordered + [jnp.zeros((1, chunks, cols), BF)])
        slots = grads[jnp.asarray(index)[block_of_slot]].reshape(n_dp, capacity, chunks, cols)
        owned = lax.all_to_all(slots, DP, split_axis=0, concat_axis=0, tiled=True)
        owned = owned.reshape(n_g, TP, capacity, chunks, cols)
        owned = owned.transpose(2, 0, 3, 1, 4).reshape(capacity, piece).astype(F32)
        small_owned = jnp.sum(to_all(small_flat), axis=0)[:small_here]
    if pieces:
        new_masters, new_first, new_second, new_low = adam(
            owned, masters, first_moment, second_moment
        )
    else:
        new_masters, new_first, new_second = adam_update(
            masters, owned, first_moment, second_moment, learn_rate, decay_rate
        )
        new_low = new_masters.astype(BF)
    small_new, small_first_new, small_second_new = adam_update(
        small_params, small_owned, small_first, small_second, small_rate, 0.0
    )
    return (
        outputs,
        grad_in,
        new_masters,
        new_first,
        new_second,
        new_low,
        small_new,
        small_first_new,
        small_second_new,
    )


def solution(mesh):
    n_dp, n_seq = mesh.devices.shape
    cut = Mesh(mesh.devices.reshape(n_dp // TP, 2, 2, n_seq), ALL)
    placed = (
        P(DP, "seq", None),
        P(DP, "seq", None),
        P(DP, None),
        P(),
        P(DP, "seq"),
        P(DP, "seq"),
        P(DP, "seq"),
        P(ALL),
        P(ALL),
        P(ALL),
    )
    return jax.shard_map(
        body,
        mesh=cut,
        in_specs=placed,
        out_specs=(
            P(DP, "seq", None),
            P(DP, "seq", None),
            P(DP, "seq"),
            P(DP, "seq"),
            P(DP, "seq"),
            P(DP, "seq"),
            P(ALL),
            P(ALL),
            P(ALL),
        ),
        check_vma=False,
    )
```

time: 955 us -> 794 us (0.83)
  blocking collectives: 164 us -> 13.7 us
  local copies, waits for them, and re-layouts: 134 us -> 56.1 us
  Pallas kernels: 89.3 us -> 148 us
  starting transfers between devices: 67.9 us -> 108 us
  matrix products: 189 us -> 157 us
    unnamed x2 -> x0, blocking collectives: 113 us -> none
    pallas_call x8 -> x20, Pallas kernels: 89.3 us -> 148 us  [the longest x4 51.1 us: attend_back(): pl.pallas_call(functools.partial(attend_back_kernel, half), in_specs=[pl....]
    all_to_all x6 -> x7, starting transfers between devices: 22.6 us -> 77.8 us  [the longest x1 28.8 us: to_all(): return lax.all_to_all(value, ALL, split_axis=0, concat_axis=0, tiled=True)]
    all_gather x2 -> x0, blocking collectives: 51.5 us -> none  [gather_blocks(): by_z = lax.all_gather(value, 'seq', axis=0)]
    convert_element_type x14 -> x4, local copies, waits for them, and re-layouts: 31.9 us -> 0.35 us  [body(): small_f = small_all[base:base + 3 * width + FF].astype(F32)]
    all_gather x4 -> x2, waiting for transfers between devices: 0.03 us -> 23.6 us  [spread(): return lax.all_gather(value, ('g', 'seq'), axis=0)]
    another operation x9 -> x1, local copies, waits for them, and re-layouts: 22 us -> 0.1 us  [the longest x2 8.82 us: body(): gather_blocks(mine[n_qkv + n_out:n_qkv + n_out + n_in])]
    ppermute x42 -> x41, waiting for transfers between devices: 164 us -> 148 us  [the longest x32 94.7 us: swap(): return lax.ppermute(value, DP, [(i, i ^ bit) for i in range(n_dp)])]
  transfers between devices with their start and end apart: 58 -> 52, of which waited for: 17 -> 19; matrix products, arithmetic and copies ran while one was open for 37% -> 30% of each run, Pallas kernels for 9% -> 16%
where the time goes in v2:
time: 794 us; the launch traced here: 784 us
  waiting for transfers between devices  196 us (25%)
  matrix products  157 us (20%)
  Pallas kernels  148 us (19%)
  starting transfers between devices  108 us (14%)
  other arithmetic  83 us (10%)
  local copies, waits for them, and re-layouts  56.1 us (7%)
  between operations  21.4 us (3%)
  blocking collectives  13.7 us (2%)
    ppermute x32, waiting for transfers between devices, swap(): return lax.ppermute(value, DP, [(i, i ^ bit) for i in range(n_dp)])  94.7 us
    dot_general x16, matrix products, dot_nt(): lax.dot_general(left, right, (((1,), (1,)), ((), ())), preferred_element_...  60.8 us
    dot_general x16, matrix products, dot_tn(): lax.dot_general(left, right, (((0,), (0,)), ((), ())), preferred_element_...  52 us
    pallas_call x4, Pallas kernels, attend_back(): pl.pallas_call(functools.partial(attend_back_kernel, half), in_specs=[pl....  51.1 us
    dot_general x16, matrix products, dot(): return jnp.dot(left, right, preferred_element_type=F32)  44.4 us
    pallas_call x4, Pallas kernels, attend(): pl.pallas_call(functools.partial(attend_kernel, half), in_specs=[pl.Block...  41.9 us
    unnamed x264, local copies, waits for them, and re-layouts  29.6 us
    all_to_all x1, starting transfers between devices, to_all(): return lax.all_to_all(value, ALL, split_axis=0, concat_axis=0, tiled=True)  28.8 us
  transfers between devices with their start and end apart: 52, of which 19 were waited for; matrix products, arithmetic and copies ran while one was open for 30% of the time, Pallas kernels for 16%

profile of v2, /device:TPU:0, one launch (start us, length us, event | category | flops | bytes accessed | tf_op | source)
XLA Modules:
  0.0 783.7 jit_solution(266539030266250529)
XLA Ops:
  7.2 5.3 pack.1
  12.5 5.3 all-to-all-start
  29.9 22.2 %collective-permute-done.1 = bf16[2,256,1024]{2,1,0:T(8,128)(2,1)S(1)} collective-permute-done((bf16[2,256,1024]{2,1,0:T(8,128)(2,1)S(1)}, bf16[2,256,1024]{2,1,0:T(8,128)(2,1)S(1)}, u32[]{:S(2)}, u32[]{:S(2)}) %collective-permute-start.1) | collective-permute-done | bytes 1048608 | tf_op jit(solution)/shard_map/ppermute | solution.py:618
  54.6 28.8 %all-to-all-start.1 = ((bf16[32,2,256]{2,1,0:T(2,128)(2,1)}), bf16[32,2,256]{2,1,0:T(2,128)(2,1)S(1)}, u32[]{:S(2)}, u32[]{:S(2)}) async-start(bf16[32,2,256]{2,1,0:T(2,128)(2,1)} %reshape.267), calls=%async_computation.1 | async-start | bytes 65536 | tf_op jit(solution)/shard_map/all_to_all | solution.py:593
  86.9 3.8 all-to-all-done.1
  90.7 13.7 %all_to_all.48 = bf16[4,20,16,256]{3,2,1,0:T(8,128)(2,1)S(1)} all-to-all(bf16[4,20,16,256]{3,2,1,0:T(8,128)(2,1)} %bitcast.197), channel_id=1, replica_groups=mesh['g'=2,'x'=2,'core'=2,'seq'=4] {'x','core'}, dimensions={0} | all-to-all | bytes 1310720 | tf_op jit(solution)/shard_map/all_to_all | solution.py:746
  117.5 3.8 fusion.82
  123.6 11.8 %collective-permute-done.4.refs_2_ = bf16[24,16,256]{2,1,0:T(8,128)(2,1)S(1)} collective-permute-done((bf16[24,16,256]{2,1,0:T(8,128)(2,1)S(1)}, bf16[24,16,256]{2,1,0:T(8,128)(2,1)S(1)}, u32[]{:S(2)}, u32[]{:S(2)}) %collective-permute-start.4) | collective-permute-done | bytes 196640 | tf_op jit(solution)/shard_map/ppermute | solution.py:740
  137.3 3.7 slice_bitcast_fusion
  149.1 5.9 fusion.124.proj_ref
  155.0 7.8 attend.4
  165.5 18.8 %collective-permute-done.9 = bf16[512,1024]{1,0:T(8,128)(2,1)} collective-permute-done((bf16[512,1024]{1,0:T(8,128)(2,1)}, bf16[512,1024]{1,0:T(8,128)(2,1)}, u32[]{:S(2)}, u32[]{:S(2)}) %collective-permute-start.9) | collective-permute-done | bytes 1048608 | tf_op jit(solution)/shard_map/ppermute | solution.py:583
  186.9 3.8 pad_maximum_fusion.5
  194.1 17.8 %attend.5 = (bf16[1024,256]{1,0:T(8,128)(2,1)S(1)}, bf16[1024,768]{1,0:T(8,128)(2,1)S(1)}, f32[8,1024]{1,0:T(8,128)S(1)}) custom-call(s32[1]{0:T(128)} %bitcast.8.flip_ref, f32[1024,768]{1,0:T(8,128)} %fusion.137.proj_ref, f32[3,1024,128]{2,1,0:T(8,128)} %get-tuple-element.196.tab_ref, bf16[1024,256]{1,0:T(8,128)(2,1)S(1)} %copy-done.6, ...), custom_call_target="tpu_custom_call" | custom-call | flops 2147483648 | bytes 6291456 | tf_op jit(solution)/shard_map/attend/pallas_call | solution.py:200
  216.1 3.7 assemble.4
  226.5 3.9 fusion.123
  242.2 24.0 %collective-permute-done.15 = bf16[512,1024]{1,0:T(8,128)(2,1)} collective-permute-done((bf16[512,1024]{1,0:T(8,128)(2,1)}, bf16[512,1024]{1,0:T(8,128)(2,1)}, u32[]{:S(2)}, u32[]{:S(2)}) %collective-permute-start.15) | collective-permute-done | bytes 1048608 | tf_op jit(solution)/shard_map/ppermute | solution.py:583
  272.4 23.6 %all-gather.7.cloned.1.call-done = bf16[768,16,256]{2,1,0:T(8,128)(2,1)} async-done(((bf16[96,16,256]{2,1,0:T(8,128)(2,1)}), bf16[768,16,256]{2,1,0:T(8,128)(2,1)}) %all-gather.7.cloned.1.call-update) | async-done | bytes 6291472 | tf_op jit(solution)/shard_map/all_gather | solution.py:685
  296.0 6.4 assemble.5
  308.0 4.7 multiply_convert_fusion.5
  315.8 3.5 fusion.118.proj_ref
  319.3 7.8 attend.6
  327.2 6.3 fusion.119
  337.2 3.6 fusion.140.proj_ref
  340.8 5.1 fusion.125
  345.9 4.7 multiply_convert_fusion.4
  350.6 8.5 %attend.7 = (bf16[1024,256]{1,0:T(8,128)(2,1)S(1)}, bf16[1024,768]{1,0:T(8,128)(2,1)S(1)}, f32[8,1024]{1,0:T(8,128)S(1)}) custom-call(s32[1]{0:T(128)} %bitcast.8.flip_ref, f32[1024,768]{1,0:T(8,128)} %fusion.140.proj_ref, f32[3,1024,128]{2,1,0:T(8,128)} %get-tuple-element.196.tab_ref, bf16[1024,256]{1,0:T(8,128)(2,1)S(1)} %copy-done.6, ...), custom_call_target="tpu_custom_call" | custom-call | flops 2147483648 | bytes 6291456 | tf_op jit(solution)/shard_map/attend/pallas_call | solution.py:200
  359.9 6.7 convolution_add_fusion.9
  374.6 6.0 disassemble.5
  381.2 5.8 fusion.59
  395.6 4.4 fusion.143
  400.0 4.4 fusion.142
  407.3 12.8 %attend_back.4 = bf16[1024,768]{1,0:T(8,128)(2,1)S(1)} custom-call(s32[1]{0:T(128)} %bitcast.8.flip_ref, bf16[1024,768]{1,0:T(8,128)(2,1)} %copy-done.36, bf16[1024,256]{1,0:T(8,128)(2,1)S(1)} %convolution_convert_fusion.3.dctx_ref, f32[8,1024]{1,0:T(8,128)S(1)} %get-tuple-element.128.lse_ref, f32[3,1024,128]{2,1,0:T(8,128)} %get-tuple-element.196.tab_ref, ...), custom_call_target="tpu_custom_call" | custom-call | flops 5368709120 | bytes 6291456 | tf_op jit(solution)/shard_map/attend_back/pallas_call | solution.py:223
  420.2 4.7 convolution_add_fusion.8
  424.9 6.7 collective-permute-done.21
  435.4 12.9 %attend_back.5 = bf16[1024,768]{1,0:T(8,128)(2,1)S(1)} custom-call(s32[1]{0:T(128)} %bitcast.8.flip_ref, bf16[1024,768]{1,0:T(8,128)(2,1)} %copy-done.35, bf16[1024,256]{1,0:T(8,128)(2,1)S(1)} %convolution_convert_fusion.2.dctx_ref, f32[8,1024]{1,0:T(8,128)S(1)} %get-tuple-element.131.lse_ref, f32[3,1024,128]{2,1,0:T(8,128)} %get-tuple-element.197.tab_ref, ...), custom_call_target="tpu_custom_call" | custom-call | flops 5368709120 | bytes 6291456 | tf_op jit(solution)/shard_map/attend_back/pallas_call | solution.py:223
  448.3 4.6 convolution_add_fusion.7
  455.9 23.3 %collective-permute-done.24 = bf16[512,1024]{1,0:T(8,128)(2,1)S(1)} collective-permute-done((bf16[512,1024]{1,0:T(8,128)(2,1)S(1)}, bf16[512,1024]{1,0:T(8,128)(2,1)S(1)}, u32[]{:S(2)}, u32[]{:S(2)}) %collective-permute-start.24) | collective-permute-done | bytes 1048608 | tf_op jit(solution)/shard_map/ppermute | solution.py:583
  485.4 3.9 fusion.117
  499.1 12.6 %attend_back.6 = bf16[1024,768]{1,0:T(8,128)(2,1)S(1)} custom-call(s32[1]{0:T(128)} %bitcast.8.flip_ref, bf16[1024,768]{1,0:T(8,128)(2,1)} %copy-done.34, bf16[1024,256]{1,0:T(8,128)(2,1)S(1)} %convolution_convert_fusion.1.dctx_ref, f32[8,1024]{1,0:T(8,128)S(1)} %get-tuple-element.141.lse_ref, f32[3,1024,128]{2,1,0:T(8,128)} %get-tuple-element.197.tab_ref, ...), custom_call_target="tpu_custom_call" | custom-call | flops 5368709120 | bytes 6291456 | tf_op jit(solution)/shard_map/attend_back/pallas_call | solution.py:223
  512.0 6.7 multiply_convert_fusion.1
  536.9 6.5 convert_reduce_fusion.2
  544.2 4.7 fusion.122
  548.8 4.6 convolution_add_fusion.5.refs_0_
  553.4 4.3 disassemble.8
  557.7 5.2 fusion.121
  562.9 4.4 fusion.146
  567.3 9.3 %collective-permute-done.30 = bf16[4,40,16,256]{3,2,1,0:T(8,128)(2,1)S(1)} collective-permute-done((bf16[4,40,16,256]{3,2,1,0:T(8,128)(2,1)S(1)}, bf16[4,40,16,256]{3,2,1,0:T(8,128)(2,1)S(1)}, u32[]{:S(2)}, u32[]{:S(2)}) %collective-permute-start.30) | collective-permute-done | bytes 1310752 | tf_op jit(solution)/shard_map/ppermute | solution.py:583
  579.5 12.8 %attend_back.7 = bf16[1024,768]{1,0:T(8,128)(2,1)S(1)} custom-call(s32[1]{0:T(128)} %bitcast.8.flip_ref, bf16[1024,768]{1,0:T(8,128)(2,1)} %copy-done.33, bf16[1024,256]{1,0:T(8,128)(2,1)S(1)} %convolution_convert_fusion.dctx_ref, f32[8,1024]{1,0:T(8,128)S(1)} %get-tuple-element.155.lse_ref, f32[3,1024,128]{2,1,0:T(8,128)} %get-tuple-element.196.tab_ref, ...), custom_call_target="tpu_custom_call" | custom-call | flops 5368709120 | bytes 6291456 | tf_op jit(solution)/shard_map/attend_back/pallas_call | solution.py:223
  596.4 4.4 all-to-all-start.3
  608.3 3.8 convolution_add_fusion.4
  612.2 4.4 fusion.136
  616.6 15.4 %all-to-all-done.3 = bf16[4,40,16,256]{3,2,1,0:T(8,128)(2,1)} async-done(((bf16[4,40,16,256]{3,2,1,0:T(8,128)(2,1)}), bf16[4,40,16,256]{3,2,1,0:T(8,128)(2,1)}, u32[]{:S(2)}, u32[]{:S(2)}) %all-to-all-start.3) | async-done | bytes 1310752 | tf_op jit(solution)/shard_map/all_to_all | solution.py:912
  636.2 4.6 all-to-all-start.4
  656.7 6.2 collective-permute-done.37
  671.1 4.8 all-to-all-start.5
  676.3 5.0 fusion.43
  691.6 4.8 all-to-all-done.5
  698.0 4.3 place.1
  702.4 4.5 all-to-all-start.6
  713.1 7.6 collective-permute-done.26
  721.8 12.1 %collective-permute-done.36 = bf16[256,1024]{1,0:T(8,128)(2,1)S(1)} collective-permute-done((bf16[256,1024]{1,0:T(8,128)(2,1)S(1)}, bf16[256,1024]{1,0:T(8,128)(2,1)S(1)}, u32[]{:S(2)}, u32[]{:S(2)}) %collective-permute-start.36) | collective-permute-done | bytes 524320 | tf_op jit(solution)/shard_map/ppermute | solution.py:633
  735.7 25.4 %all-to-all-start.7 = ((f32[4,1,512]{2,1,0:T(1,128)}), f32[4,1,512]{2,1,0:T(1,128)S(1)}, u32[]{:S(2)}, u32[]{:S(2)}) async-start(f32[4,1,512]{2,1,0:T(1,128)} %all_to_all.38), calls=%async_computation.9 | async-start | bytes 16384 | tf_op jit(solution)/shard_map/all_to_all | solution.py:1030
  762.1 14.0 %adam.1 = (f32[32,32768]{1,0:T(8,128)}, f32[32,32768]{1,0:T(8,128)}, f32[32,32768]{1,0:T(8,128)}, bf16[32,32768]{1,0:T(8,128)(2,1)}) custom-call(bf16[8,528,256]{2,1,0:T(8,128)(2,1)} %all-to-all-done.6.from_ref, f32[32,32768]{1,0:T(8,128)} %w_ref.1, f32[32,32768]{1,0:T(8,128)} %one_ref.1, f32[32,32768]{1,0:T(8,128)} %two_ref.1), custom_call_target="tpu_custom_call" | custom-call | flops 20971520 | bytes 29360128 | tf_op jit(solution)/shard_map/adam/pallas_call | solution.py:499
  (510 shorter events, 215.6 us)
Async XLA Ops:
  12.5 40.0 %all-to-all-start = ((bf16[8,512,256]{2,1,0:T(8,128)(2,1)}), bf16[8,512,256]{2,1,0:T(8,128)(2,1)}, u32[]{:S(2)}, u32[]{:S(2)}) async-start(bf16[8,512,256]{2,1,0:T(8,128)(2,1)} %pack.1), calls=%async_computation | async-start | bytes 4194304 | tf_op jit(solution)/shard_map/all_to_all | solution.py:671
  24.1 5.8 collective-permute-start
  26.0 26.1 %collective-permute-start.1 = (bf16[2,256,1024]{2,1,0:T(8,128)(2,1)S(1)}, bf16[2,256,1024]{2,1,0:T(8,128)(2,1)S(1)}, u32[]{:S(2)}, u32[]{:S(2)}) collective-permute-start(bf16[2,256,1024]{2,1,0:T(8,128)(2,1)S(1)} %get-tuple-element.202), channel_id=1, source_target_pairs={{0,1},{16,17},{1,0},{17,16},{2,5},{18,21},{3,4},{19,20},{4,3},{20,... | collective-permute-start | bytes 3145736 | tf_op jit(solution)/shard_map/ppermute | solution.py:618
  52.5 57.0 %copy-start.41 = (bf16[2,512,1024]{2,1,0:T(8,128)(2,1)}, bf16[2,512,1024]{2,1,0:T(8,128)(2,1)S(1)}, u32[]{:S(2)}) copy-start(bf16[2,512,1024]{2,1,0:T(8,128)(2,1)S(1)} %pad_maximum_fusion.3) | copy-start | bytes 6291460
  54.6 36.1 %all-to-all-start.1 = ((bf16[32,2,256]{2,1,0:T(2,128)(2,1)}), bf16[32,2,256]{2,1,0:T(2,128)(2,1)S(1)}, u32[]{:S(2)}, u32[]{:S(2)}) async-start(bf16[32,2,256]{2,1,0:T(2,128)(2,1)} %reshape.267), calls=%async_computation.1 | async-start | bytes 65536 | tf_op jit(solution)/shard_map/all_to_all | solution.py:593
  83.4 132.7 %all-gather.5.cloned.1.call-start = ((), (), s32[]{:S(2)}) async-start(), calls=%async_computation.12 | async-start | bytes 5308416 | tf_op jit(solution)/shard_map/all_gather | solution.py:685
  106.1 189.8 %all-gather.7.cloned.1.call-start = ((), (), s32[]{:S(2)}) async-start(), calls=%async_computation.13 | async-start | bytes 7077888 | tf_op jit(solution)/shard_map/all_gather | solution.py:685
  109.0 14.3 %collective-permute-start.3 = (bf16[24,16,256]{2,1,0:T(8,128)(2,1)S(1)}, bf16[24,16,256]{2,1,0:T(8,128)(2,1)S(1)}, u32[]{:S(2)}, u32[]{:S(2)}) collective-permute-start(bf16[24,16,256]{2,1,0:T(8,128)(2,1)S(1)} %copy-done.14), channel_id=1, source_target_pairs={{0,1},{1,2},{2,3},{3,0},{4,5},{5,6},{6,7},{7,4},{8,9},{9,10},{10,1... | collective-permute-start | bytes 589832 | tf_op jit(solution)/shard_map/ppermute | solution.py:740
  109.4 26.0 %collective-permute-start.4 = (bf16[24,16,256]{2,1,0:T(8,128)(2,1)S(1)}, bf16[24,16,256]{2,1,0:T(8,128)(2,1)S(1)}, u32[]{:S(2)}, u32[]{:S(2)}) collective-permute-start(bf16[24,16,256]{2,1,0:T(8,128)(2,1)S(1)} %copy-done.14), channel_id=1, source_target_pairs={{0,2},{1,3},{2,0},{3,1},{4,6},{5,7},{6,4},{7,5},{8,10},{9,11},{10,... | collective-permute-start | bytes 589832 | tf_op jit(solution)/shard_map/ppermute | solution.py:740
  110.2 25.2 %collective-permute-start.5 = (bf16[24,16,256]{2,1,0:T(8,128)(2,1)S(1)}, bf16[24,16,256]{2,1,0:T(8,128)(2,1)S(1)}, u32[]{:S(2)}, u32[]{:S(2)}) collective-permute-start(bf16[24,16,256]{2,1,0:T(8,128)(2,1)S(1)} %copy-done.14), channel_id=1, source_target_pairs={{0,3},{1,0},{2,1},{3,2},{4,7},{5,4},{6,5},{7,6},{8,11},{9,8},{10,9... | collective-permute-start | bytes 589832 | tf_op jit(solution)/shard_map/ppermute | solution.py:740
  112.9 29.8 %collective-permute-start.6 = (bf16[24,16,256]{2,1,0:T(8,128)(2,1)S(1)}, bf16[24,16,256]{2,1,0:T(8,128)(2,1)S(1)}, u32[]{:S(2)}, u32[]{:S(2)}) collective-permute-start(bf16[24,16,256]{2,1,0:T(8,128)(2,1)S(1)} %copy-done.14), channel_id=1, source_target_pairs={{0,16},{4,20},{8,24},{12,28},{16,0},{20,4},{24,8},{28,12},{1,17},{... | collective-permute-start | bytes 589832 | tf_op jit(solution)/shard_map/ppermute | solution.py:583
  117.3 31.8 %collective-permute-start.2 = (bf16[512,1024]{1,0:T(8,128)(2,1)}, bf16[512,1024]{1,0:T(8,128)(2,1)}, u32[]{:S(2)}, u32[]{:S(2)}) collective-permute-start(bf16[512,1024]{1,0:T(8,128)(2,1)} %fusion.37), channel_id=1, source_target_pairs={{0,4},{4,0},{8,12},{12,8},{16,20},{20,16},{24,28},{28,24},{1,5},{5... | collective-permute-start | bytes 3145736 | tf_op jit(solution)/shard_map/ppermute | solution.py:583
  123.2 41.6 %collective-permute-start.12 = (bf16[512,1024]{1,0:T(8,128)(2,1)}, bf16[512,1024]{1,0:T(8,128)(2,1)}, u32[]{:S(2)}, u32[]{:S(2)}) collective-permute-start(bf16[512,1024]{1,0:T(8,128)(2,1)} %fusion.37), channel_id=1, source_target_pairs={{0,8},{4,12},{8,0},{12,4},{16,24},{20,28},{24,16},{28,20},{1,9},{5... | collective-permute-start | bytes 3145736 | tf_op jit(solution)/shard_map/ppermute | solution.py:583
  136.3 10.4 %collective-permute-start.7 = (bf16[3,24,16,256]{3,2,1,0:T(8,128)(2,1)}, bf16[3,24,16,256]{3,2,1,0:T(8,128)(2,1)S(1)}, u32[]{:S(2)}, u32[]{:S(2)}) collective-permute-start(bf16[3,24,16,256]{3,2,1,0:T(8,128)(2,1)} %pad_maximum_fusion.13), channel_id=1, source_target_pairs={{0,16},{4,20},{8,24},{12,28},{16,0},{20,4},{24,8},{28,12},{1,17},{... | collective-permute-start | bytes 1769480 | tf_op jit(solution)/shard_map/ppermute | solution.py:583
  137.3 346.5 %reduce-scatter.3.cloned.1.call-start = ((), (), s32[]{:S(2)}) async-start(), calls=%async_computation.10 | async-start | bytes 5308416 | tf_op jit(solution)/shard_map/reduce_scatter | solution.py:898
  149.1 41.6 %copy-start.4 = (bf16[1024,768]{1,0:T(8,128)(2,1)}, bf16[1024,768]{1,0:T(8,128)(2,1)S(1)}, u32[]{:S(2)}) copy-start(bf16[1024,768]{1,0:T(8,128)(2,1)S(1)} %assemble.3) | copy-start | bytes 4718596
  163.9 71.2 %copy-start = (bf16[1024,256]{1,0:T(8,128)(2,1)}, bf16[1024,256]{1,0:T(8,128)(2,1)S(1)}, u32[]{:S(2)}) copy-start(bf16[1024,256]{1,0:T(8,128)(2,1)S(1)} %get-tuple-element.107) | copy-start | bytes 1572868
  163.9 20.3 %collective-permute-start.9 = (bf16[512,1024]{1,0:T(8,128)(2,1)}, bf16[512,1024]{1,0:T(8,128)(2,1)}, u32[]{:S(2)}, u32[]{:S(2)}) collective-permute-start(bf16[512,1024]{1,0:T(8,128)(2,1)} %get-tuple-element.110), channel_id=1, source_target_pairs={{0,8},{4,12},{8,0},{12,4},{16,24},{20,28},{24,16},{28,20},{1,9},{5... | collective-permute-start | bytes 3145736 | tf_op jit(solution)/shard_map/ppermute | solution.py:583
  164.8 20.7 %collective-permute-start.13 = (bf16[512,1024]{1,0:T(8,128)(2,1)}, bf16[512,1024]{1,0:T(8,128)(2,1)}, u32[]{:S(2)}, u32[]{:S(2)}) collective-permute-start(bf16[512,1024]{1,0:T(8,128)(2,1)} %collective-permute-done.12), channel_id=1, source_target_pairs={{0,4},{4,0},{8,12},{12,8},{16,20},{20,16},{24,28},{28,24},{1,5},{5... | collective-permute-start | bytes 3145736 | tf_op jit(solution)/shard_map/ppermute | solution.py:583
  164.8 22.0 %collective-permute-start.8 = (bf16[512,1024]{1,0:T(8,128)(2,1)}, bf16[512,1024]{1,0:T(8,128)(2,1)}, u32[]{:S(2)}, u32[]{:S(2)}) collective-permute-start(bf16[512,1024]{1,0:T(8,128)(2,1)} %get-tuple-element.110), channel_id=1, source_target_pairs={{0,4},{4,0},{8,12},{12,8},{16,20},{20,16},{24,28},{28,24},{1,5},{5... | collective-permute-start | bytes 3145736 | tf_op jit(solution)/shard_map/ppermute | solution.py:583
  165.5 64.9 %copy-start.104 = (f32[4,1,256]{2,1,0:T(1,128)}, f32[4,1,256]{2,1,0:T(1,128)S(1)}, u32[]{:S(2)}) copy-start(f32[4,1,256]{2,1,0:T(1,128)S(1)} %fusion.106) | copy-start | bytes 12292
  184.3 28.9 %collective-permute-start.10 = (bf16[512,1024]{1,0:T(8,128)(2,1)}, bf16[512,1024]{1,0:T(8,128)(2,1)S(1)}, u32[]{:S(2)}, u32[]{:S(2)}) collective-permute-start(bf16[512,1024]{1,0:T(8,128)(2,1)} %collective-permute-done.9), channel_id=1, source_target_pairs={{0,4},{4,0},{8,12},{12,8},{16,20},{20,16},{24,28},{28,24},{1,5},{5... | collective-permute-start | bytes 3145736 | tf_op jit(solution)/shard_map/ppermute | solution.py:583
  225.9 13.1 %collective-permute-start.14 = (bf16[512,1024]{1,0:T(8,128)(2,1)S(1)}, bf16[512,1024]{1,0:T(8,128)(2,1)S(1)}, u32[]{:S(2)}, u32[]{:S(2)}) collective-permute-start(bf16[512,1024]{1,0:T(8,128)(2,1)S(1)} %slice.377), channel_id=1, source_target_pairs={{0,4},{4,0},{8,12},{12,8},{16,20},{20,16},{24,28},{28,24},{1,5},{5... | collective-permute-start | bytes 3145736 | tf_op jit(solution)/shard_map/ppermute | solution.py:583
  239.0 27.3 %copy-start.42 = (bf16[2,512,1024]{2,1,0:T(8,128)(2,1)S(1)}, bf16[2,512,1024]{2,1,0:T(8,128)(2,1)}, u32[]{:S(2)}) copy-start(bf16[2,512,1024]{2,1,0:T(8,128)(2,1)} %copy-done.41) | copy-start | bytes 6291460
  239.0 3.2 collective-permute-start.11
  240.4 25.9 %collective-permute-start.15 = (bf16[512,1024]{1,0:T(8,128)(2,1)}, bf16[512,1024]{1,0:T(8,128)(2,1)}, u32[]{:S(2)}, u32[]{:S(2)}) collective-permute-start(bf16[512,1024]{1,0:T(8,128)(2,1)} %fusion.53), channel_id=1, source_target_pairs={{0,8},{4,12},{8,0},{12,4},{16,24},{20,28},{24,16},{28,20},{1,9},{5... | collective-permute-start | bytes 3145736 | tf_op jit(solution)/shard_map/ppermute | solution.py:583
  270.4 45.4 %copy-start.69 = (bf16[512,1024]{1,0:T(8,128)(2,1)}, bf16[512,1024]{1,0:T(8,128)(2,1)S(1)}, u32[]{:S(2)}) copy-start(bf16[512,1024]{1,0:T(8,128)(2,1)S(1)} %add_convert_fusion.4) | copy-start | bytes 3145732
  270.4 32.0 %collective-permute-start.16 = (bf16[512,1024]{1,0:T(8,128)(2,1)S(1)}, bf16[512,1024]{1,0:T(8,128)(2,1)S(1)}, u32[]{:S(2)}, u32[]{:S(2)}) collective-permute-start(bf16[512,1024]{1,0:T(8,128)(2,1)S(1)} %add_convert_fusion.4), channel_id=1, source_target_pairs={{0,4},{4,0},{8,12},{12,8},{16,20},{20,16},{24,28},{28,24},{1,5},{5... | collective-permute-start | bytes 3145736 | tf_op jit(solution)/shard_map/ppermute | solution.py:583
  270.6 42.2 %collective-permute-start.17 = (bf16[512,1024]{1,0:T(8,128)(2,1)S(1)}, bf16[512,1024]{1,0:T(8,128)(2,1)}, u32[]{:S(2)}, u32[]{:S(2)}) collective-permute-start(bf16[512,1024]{1,0:T(8,128)(2,1)S(1)} %add_convert_fusion.4), channel_id=1, source_target_pairs={{0,8},{4,12},{8,0},{12,4},{16,24},{20,28},{24,16},{28,20},{1,9},{5... | collective-permute-start | bytes 3145736 | tf_op jit(solution)/shard_map/ppermute | solution.py:583
  302.4 32.4 %copy-start.22 = (bf16[1024,1024]{1,0:T(8,128)(2,1)}, bf16[1024,1024]{1,0:T(8,128)(2,1)S(1)}, u32[]{:S(2)}) copy-start(bf16[1024,1024]{1,0:T(8,128)(2,1)S(1)} %get-tuple-element.118) | copy-start | bytes 6291460
  302.4 34.8 %copy-start.24 = (bf16[1024,768]{1,0:T(8,128)(2,1)}, bf16[1024,768]{1,0:T(8,128)(2,1)S(1)}, u32[]{:S(2)}) copy-start(bf16[1024,768]{1,0:T(8,128)(2,1)S(1)} %get-tuple-element.120) | copy-start | bytes 4718596
  315.8 17.7 %collective-permute-start.18 = (bf16[512,1024]{1,0:T(8,128)(2,1)}, bf16[512,1024]{1,0:T(8,128)(2,1)}, u32[]{:S(2)}, u32[]{:S(2)}) collective-permute-start(bf16[512,1024]{1,0:T(8,128)(2,1)} %collective-permute-done.17), channel_id=1, source_target_pairs={{0,4},{4,0},{8,12},{12,8},{16,20},{20,16},{24,28},{28,24},{1,5},{5... | collective-permute-start | bytes 3145736 | tf_op jit(solution)/shard_map/ppermute | solution.py:583
  350.6 20.0 %copy-start.62 = (bf16[1024,1024]{1,0:T(8,128)(2,1)}, bf16[1024,1024]{1,0:T(8,128)(2,1)S(1)}, u32[]{:S(2)}) copy-start(bf16[1024,1024]{1,0:T(8,128)(2,1)S(1)} %multiply_convert_fusion.4) | copy-start | bytes 6291460
  380.7 253.6 %reduce-scatter.5.cloned.1.call-start = ((), (), s32[]{:S(2)}) async-start(), calls=%async_computation.11 | async-start | bytes 1769472 | tf_op jit(solution)/shard_map/reduce_scatter | solution.py:898
  388.9 36.0 %collective-permute-start.19 = (bf16[512,1024]{1,0:T(8,128)(2,1)}, bf16[512,1024]{1,0:T(8,128)(2,1)S(1)}, u32[]{:S(2)}, u32[]{:S(2)}) collective-permute-start(bf16[512,1024]{1,0:T(8,128)(2,1)} %slice.376), channel_id=1, source_target_pairs={{0,4},{4,0},{8,12},{12,8},{16,20},{20,16},{24,28},{28,24},{1,5},{5... | collective-permute-start | bytes 3145736 | tf_op jit(solution)/shard_map/ppermute | solution.py:583
  393.2 11.2 %collective-permute-start.20 = (bf16[512,1024]{1,0:T(8,128)(2,1)S(1)}, bf16[512,1024]{1,0:T(8,128)(2,1)S(1)}, u32[]{:S(2)}, u32[]{:S(2)}) collective-permute-start(bf16[512,1024]{1,0:T(8,128)(2,1)S(1)} %slice.375), channel_id=1, source_target_pairs={{0,4},{4,0},{8,12},{12,8},{16,20},{20,16},{24,28},{28,24},{1,5},{5... | collective-permute-start | bytes 3145736 | tf_op jit(solution)/shard_map/ppermute | solution.py:583
  405.8 25.8 %collective-permute-start.21 = (bf16[512,1024]{1,0:T(8,128)(2,1)}, bf16[512,1024]{1,0:T(8,128)(2,1)S(1)}, u32[]{:S(2)}, u32[]{:S(2)}) collective-permute-start(bf16[512,1024]{1,0:T(8,128)(2,1)} %fusion.48), channel_id=1, source_target_pairs={{0,8},{4,12},{8,0},{12,4},{16,24},{20,28},{24,16},{28,20},{1,9},{5... | collective-permute-start | bytes 3145736 | tf_op jit(solution)/shard_map/ppermute | solution.py:583
  433.5 20.2 %collective-permute-start.23 = (bf16[512,1024]{1,0:T(8,128)(2,1)S(1)}, bf16[512,1024]{1,0:T(8,128)(2,1)S(1)}, u32[]{:S(2)}, u32[]{:S(2)}) collective-permute-start(bf16[512,1024]{1,0:T(8,128)(2,1)S(1)} %slice.373), channel_id=1, source_target_pairs={{0,4},{4,0},{8,12},{12,8},{16,20},{20,16},{24,28},{28,24},{1,5},{5... | collective-permute-start | bytes 3145736 | tf_op jit(solution)/shard_map/ppermute | solution.py:583
  453.1 2.8 collective-permute-start.22
  454.0 27.3 %copy-start.43 = (bf16[2,512,1024]{2,1,0:T(8,128)(2,1)S(1)}, bf16[2,512,1024]{2,1,0:T(8,128)(2,1)}, u32[]{:S(2)}) copy-start(bf16[2,512,1024]{2,1,0:T(8,128)(2,1)} %copy-done.41) | copy-start | bytes 6291460
  454.0 25.2 %collective-permute-start.24 = (bf16[512,1024]{1,0:T(8,128)(2,1)S(1)}, bf16[512,1024]{1,0:T(8,128)(2,1)S(1)}, u32[]{:S(2)}, u32[]{:S(2)}) collective-permute-start(bf16[512,1024]{1,0:T(8,128)(2,1)S(1)} %add_convert_fusion.3), channel_id=1, source_target_pairs={{0,8},{4,12},{8,0},{12,4},{16,24},{20,28},{24,16},{28,20},{1,9},{5... | collective-permute-start | bytes 3145736 | tf_op jit(solution)/shard_map/ppermute | solution.py:583
  483.8 9.8 %collective-permute-start.27 = (bf16[512,1024]{1,0:T(8,128)(2,1)}, bf16[512,1024]{1,0:T(8,128)(2,1)}, u32[]{:S(2)}, u32[]{:S(2)}) collective-permute-start(bf16[512,1024]{1,0:T(8,128)(2,1)} %get-tuple-element.136), channel_id=1, source_target_pairs={{0,4},{4,0},{8,12},{12,8},{16,20},{20,16},{24,28},{28,24},{1,5},{5... | collective-permute-start | bytes 3145736 | tf_op jit(solution)/shard_map/ppermute | solution.py:583
  483.9 27.8 %collective-permute-start.28 = (bf16[512,1024]{1,0:T(8,128)(2,1)}, bf16[512,1024]{1,0:T(8,128)(2,1)}, u32[]{:S(2)}, u32[]{:S(2)}) collective-permute-start(bf16[512,1024]{1,0:T(8,128)(2,1)} %get-tuple-element.136), channel_id=1, source_target_pairs={{0,8},{4,12},{8,0},{12,4},{16,24},{20,28},{24,16},{28,20},{1,9},{5... | collective-permute-start | bytes 3145736 | tf_op jit(solution)/shard_map/ppermute | solution.py:583
  511.7 46.0 %copy-start.37 = (bf16[1024,768]{1,0:T(8,128)(2,1)}, bf16[1024,768]{1,0:T(8,128)(2,1)S(1)}, u32[]{:S(2)}) copy-start(bf16[1024,768]{1,0:T(8,128)(2,1)S(1)} %attend_back.6) | copy-start | bytes 4718596
  511.7 7.1 collective-permute-start.29
  518.7 25.4 %copy-start.64 = (bf16[1024,1024]{1,0:T(8,128)(2,1)}, bf16[1024,1024]{1,0:T(8,128)(2,1)S(1)}, u32[]{:S(2)}) copy-start(bf16[1024,1024]{1,0:T(8,128)(2,1)S(1)} %multiply_convert_fusion.1) | copy-start | bytes 6291460
  543.4 33.3 %collective-permute-start.30 = (bf16[4,40,16,256]{3,2,1,0:T(8,128)(2,1)S(1)}, bf16[4,40,16,256]{3,2,1,0:T(8,128)(2,1)S(1)}, u32[]{:S(2)}, u32[]{:S(2)}) collective-permute-start(bf16[4,40,16,256]{3,2,1,0:T(8,128)(2,1)S(1)} %get-tuple-element.153), channel_id=1, source_target_pairs={{0,16},{4,20},{8,24},{12,28},{16,0},{20,4},{24,8},{28,12},{1,17},{... | collective-permute-start | bytes 3932168 | tf_op jit(solution)/shard_map/ppermute | solution.py:583
  578.1 25.0 %collective-permute-start.31 = (bf16[4,32,16,256]{3,2,1,0:T(8,128)(2,1)}, bf16[4,32,16,256]{3,2,1,0:T(8,128)(2,1)}, u32[]{:S(2)}, u32[]{:S(2)}) collective-permute-start(bf16[4,32,16,256]{3,2,1,0:T(8,128)(2,1)} %get-tuple-element.159), channel_id=1, source_target_pairs={{0,16},{4,20},{8,24},{12,28},{16,0},{20,4},{24,8},{28,12},{1,17},{... | collective-permute-start | bytes 3145736 | tf_op jit(solution)/shard_map/ppermute | solution.py:583
  596.4 35.6 %all-to-all-start.3 = ((bf16[4,40,16,256]{3,2,1,0:T(8,128)(2,1)}), bf16[4,40,16,256]{3,2,1,0:T(8,128)(2,1)}, u32[]{:S(2)}, u32[]{:S(2)}) async-start(bf16[4,40,16,256]{3,2,1,0:T(8,128)(2,1)} %add_convert_fusion), calls=%async_computation.4 | async-start | bytes 2621440 | tf_op jit(solution)/shard_map/all_to_all | solution.py:912
  636.0 11.2 %collective-permute-start.33 = (bf16[512,1024]{1,0:T(8,128)(2,1)S(1)}, bf16[512,1024]{1,0:T(8,128)(2,1)}, u32[]{:S(2)}, u32[]{:S(2)}) collective-permute-start(bf16[512,1024]{1,0:T(8,128)(2,1)S(1)} %slice.371), channel_id=1, source_target_pairs={{0,4},{4,0},{8,12},{12,8},{16,20},{20,16},{24,28},{28,24},{1,5},{5... | collective-permute-start | bytes 3145736 | tf_op jit(solution)/shard_map/ppermute | solution.py:583
  636.2 32.8 %all-to-all-start.4 = ((bf16[4,32,16,256]{3,2,1,0:T(8,128)(2,1)}), bf16[4,32,16,256]{3,2,1,0:T(8,128)(2,1)}, u32[]{:S(2)}, u32[]{:S(2)}) async-start(bf16[4,32,16,256]{3,2,1,0:T(8,128)(2,1)} %add_convert_fusion.2), calls=%async_computation.6 | async-start | bytes 2097152 | tf_op jit(solution)/shard_map/all_to_all | solution.py:912
  642.9 19.9 %collective-permute-start.37 = (bf16[4,24,16,256]{3,2,1,0:T(8,128)(2,1)S(1)}, bf16[4,24,16,256]{3,2,1,0:T(8,128)(2,1)}, u32[]{:S(2)}, u32[]{:S(2)}) collective-permute-start(bf16[4,24,16,256]{3,2,1,0:T(8,128)(2,1)S(1)} %copy-done.27), channel_id=1, source_target_pairs={{0,16},{4,20},{8,24},{12,28},{16,0},{20,4},{24,8},{28,12},{1,17},{... | collective-permute-start | bytes 2359304 | tf_op jit(solution)/shard_map/ppermute | solution.py:583
  647.2 28.7 %collective-permute-start.32 = (bf16[512,1024]{1,0:T(8,128)(2,1)}, bf16[512,1024]{1,0:T(8,128)(2,1)}, u32[]{:S(2)}, u32[]{:S(2)}) collective-permute-start(bf16[512,1024]{1,0:T(8,128)(2,1)} %slice.372), channel_id=1, source_target_pairs={{0,4},{4,0},{8,12},{12,8},{16,20},{20,16},{24,28},{28,24},{1,5},{5... | collective-permute-start | bytes 3145736 | tf_op jit(solution)/shard_map/ppermute | solution.py:583
  650.0 26.3 %collective-permute-start.34 = (bf16[512,1024]{1,0:T(8,128)(2,1)}, bf16[512,1024]{1,0:T(8,128)(2,1)}, u32[]{:S(2)}, u32[]{:S(2)}) collective-permute-start(bf16[512,1024]{1,0:T(8,128)(2,1)} %add_convert_fusion.1), channel_id=1, source_target_pairs={{0,8},{4,12},{8,0},{12,4},{16,24},{20,28},{24,16},{28,20},{1,9},{5... | collective-permute-start | bytes 3145736 | tf_op jit(solution)/shard_map/ppermute | solution.py:583
  667.1 30.2 %collective-permute-start.38 = (bf16[20,16,256]{2,1,0:T(8,128)(2,1)}, bf16[20,16,256]{2,1,0:T(8,128)(2,1)S(1)}, u32[]{:S(2)}, u32[]{:S(2)}) collective-permute-start(bf16[20,16,256]{2,1,0:T(8,128)(2,1)} %get-tuple-element.218), channel_id=1, source_target_pairs={{0,4},{4,0},{8,12},{12,8},{16,20},{20,16},{24,28},{28,24},{1,5},{5... | collective-permute-start | bytes 491528 | tf_op jit(solution)/shard_map/ppermute | solution.py:583
  667.1 30.2 %collective-permute-start.39 = (bf16[20,16,256]{2,1,0:T(8,128)(2,1)}, bf16[20,16,256]{2,1,0:T(8,128)(2,1)S(1)}, u32[]{:S(2)}, u32[]{:S(2)}) collective-permute-start(bf16[20,16,256]{2,1,0:T(8,128)(2,1)} %get-tuple-element.219), channel_id=1, source_target_pairs={{0,8},{4,12},{8,0},{12,4},{16,24},{20,28},{24,16},{28,20},{1,9},{5... | collective-permute-start | bytes 491528 | tf_op jit(solution)/shard_map/ppermute | solution.py:583
  668.0 29.3 %collective-permute-start.40 = (bf16[20,16,256]{2,1,0:T(8,128)(2,1)S(1)}, bf16[20,16,256]{2,1,0:T(8,128)(2,1)S(1)}, u32[]{:S(2)}, u32[]{:S(2)}) collective-permute-start(bf16[20,16,256]{2,1,0:T(8,128)(2,1)S(1)} %get-tuple-element.216), channel_id=1, source_target_pairs={{0,12},{4,8},{8,4},{12,0},{16,28},{20,24},{24,20},{28,16},{1,13},{... | collective-permute-start | bytes 491528 | tf_op jit(solution)/shard_map/ppermute | solution.py:583
  671.1 25.3 %all-to-all-start.5 = ((bf16[4,24,16,256]{3,2,1,0:T(8,128)(2,1)}), bf16[4,24,16,256]{3,2,1,0:T(8,128)(2,1)S(1)}, u32[]{:S(2)}, u32[]{:S(2)}) async-start(bf16[4,24,16,256]{3,2,1,0:T(8,128)(2,1)} %add_convert_fusion.5), calls=%async_computation.7 | async-start | bytes 1572864 | tf_op jit(solution)/shard_map/all_to_all | solution.py:912
  702.4 31.9 %all-to-all-start.6 = ((bf16[8,528,256]{2,1,0:T(8,128)(2,1)}), bf16[8,528,256]{2,1,0:T(8,128)(2,1)}, u32[]{:S(2)}, u32[]{:S(2)}) async-start(bf16[8,528,256]{2,1,0:T(8,128)(2,1)} %place.1), calls=%async_computation.8 | async-start | bytes 4325376 | tf_op jit(solution)/shard_map/all_to_all | solution.py:1027
  707.0 6.2 collective-permute-start.25
  707.8 12.9 %collective-permute-start.26 = (bf16[256,1024]{1,0:T(8,128)(2,1)S(1)}, bf16[256,1024]{1,0:T(8,128)(2,1)S(1)}, u32[]{:S(2)}, u32[]{:S(2)}) collective-permute-start(bf16[256,1024]{1,0:T(8,128)(2,1)S(1)} %get-tuple-element.210), channel_id=1, source_target_pairs={{1,0},{17,16},{0,1},{16,17},{5,2},{21,18},{4,3},{20,19},{3,4},{19,... | collective-permute-start | bytes 1572872 | tf_op jit(solution)/shard_map/ppermute | solution.py:633
  710.9 10.9 %collective-permute-start.35 = (bf16[256,1024]{1,0:T(8,128)(2,1)S(1)}, bf16[256,1024]{1,0:T(8,128)(2,1)S(1)}, u32[]{:S(2)}, u32[]{:S(2)}) collective-permute-start(bf16[256,1024]{1,0:T(8,128)(2,1)S(1)} %get-tuple-element.207), channel_id=1, source_target_pairs={{0,0},{16,16},{1,1},{17,17},{4,2},{20,18},{5,3},{21,19},{2,4},{18,... | collective-permute-start | bytes 1572872 | tf_op jit(solution)/shard_map/ppermute | solution.py:633
  711.6 22.3 %collective-permute-start.36 = (bf16[256,1024]{1,0:T(8,128)(2,1)S(1)}, bf16[256,1024]{1,0:T(8,128)(2,1)S(1)}, u32[]{:S(2)}, u32[]{:S(2)}) collective-permute-start(bf16[256,1024]{1,0:T(8,128)(2,1)S(1)} %get-tuple-element.206), channel_id=1, source_target_pairs={{1,0},{17,16},{0,1},{16,17},{5,2},{21,18},{4,3},{20,19},{3,4},{19,... | collective-permute-start | bytes 1572872 | tf_op jit(solution)/shard_map/ppermute | solution.py:633
  735.7 40.4 %all-to-all-start.7 = ((f32[4,1,512]{2,1,0:T(1,128)}), f32[4,1,512]{2,1,0:T(1,128)S(1)}, u32[]{:S(2)}, u32[]{:S(2)}) async-start(f32[4,1,512]{2,1,0:T(1,128)} %all_to_all.38), calls=%async_computation.9 | async-start | bytes 16384 | tf_op jit(solution)/shard_map/all_to_all | solution.py:1030
  (113 other events, 734.9 us)
Sparse Core Ops, SparseCore 0:
  106.3 91.8 all-gather.4
  200.3 95.6 all-gather.6
  380.8 93.5 reduce-scatter.2
  496.8 64.6 reduce-scatter.4

commit v3 on v2

--- a/solution.py
+++ b/solution.py
@@ -318,14 +318,15 @@
         for side in range(2)
         for z in range(4)
     ]
-    for g_ref, (first, units, fold, parts) in zip(grads, plan):
+    for g_ref, (first, units, fold, parts, *stride) in zip(grads, plan):
         if fold == 1:
             rows = units // parts
+            (apart,) = stride or (rows,)
 
             def split(u, carry):
                 for part in range(parts):
                     for ref, row in pieces:
-                        ref[first + part * rows + u] = g_ref[
+                        ref[first + part * apart + u] = g_ref[
                             pl.ds(u * 128 + row, 16), part * 256 : part * 256 + 256
                         ].astype(BF)
                 return carry
@@ -358,8 +359,8 @@
 
 def disassemble(at, grads, plan, one):
     vmem = pl.BlockSpec(memory_space=pltpu.VMEM)
-    total = sum(units for _, units, _, _ in plan)
-    tall = max(units if fold > 1 else 1 for _, units, fold, _ in plan)
+    total = sum(entry[1] for entry in plan)
+    tall = max(entry[1] if entry[2] > 1 else 1 for entry in plan)
     out = [jax.ShapeDtypeStruct((8 if one else 4, total, 16, 256), BF)] * (1 if one else 2)
     return pl.pallas_call(
         functools.partial(disassemble_kernel, plan),
@@ -666,11 +667,10 @@
         ]
     )
     note = jnp.pad(note, (0, small_width - note.shape[0]))
-    tokens, cotangent, packed = tie((tokens, cotangent, packed))
-    both_rows = to_rows(jnp.stack([tokens, cotangent]))
+    tokens, packed = tie((tokens, packed))
+    token_rows = to_rows(tokens[None])[0]
     received = lax.all_to_all(packed, DP, split_axis=0, concat_axis=0, tiled=True)
-    note, received, both_rows = tie((note, received, both_rows))
-    token_rows, cotangent_rows = both_rows[0], both_rows[1]
+    note, received, token_rows = tie((note, received, token_rows))
     notes = to_all(jnp.broadcast_to(note[None], (n_all, small_width)))
 
     unit_rows = n_seq * n_g * chunks
@@ -680,6 +680,10 @@
     per_layer = n_qkv + n_out + 2 * n_in
     my_out = n_out // TP
     fold = FF // width
+
+    def turn(value):
+        mine = [lax.dynamic_index_in_dim(value, t ^ k, 0, keepdims=False) for k in range(TP)]
+        return [mine[0]] + [swap(mine[k], k) for k in range(1, TP)]
 
     def spread(value):
         return lax.all_gather(value, ("g", "seq"), axis=0)
@@ -743,7 +747,7 @@
 
     m_qkv0, swapped, notes = tie((m_qkv0, swapped, notes))
     z_qkv0 = (m_qkv0, hop_z(m_qkv0)) if pieces else spread(m_qkv0)
-    swapped = lax.all_to_all(swapped, ("x", "core"), split_axis=0, concat_axis=0, tiled=True)
+    swapped = jnp.stack(turn(swapped))[jnp.arange(TP) ^ t]
     m_both0 = swapped[:, :my_units].reshape(n_both, chunks, cols)
     m_both1 = swapped[:, my_units:].reshape(n_both, chunks, cols)
     z_rest0 = spread(jnp.concatenate([m_in0, m_both0]))
@@ -813,9 +817,6 @@
             send = lax.dynamic_index_in_dim(value, 1 - core, 0, keepdims=False)
         return keep + swap(send.astype(BF), 1).astype(F32)
 
-    def scatter_far(part):
-        return swap(halve(part).astype(BF), 2)
-
     def scatter_pair(parts):
         if group_rows == 2:
             return parts
@@ -824,9 +825,16 @@
         other = lax.dynamic_index_in_dim(pair, 1 - side, 0, keepdims=False)
         return own, other
 
-    def scatter_group(parts):
-        own, other = scatter_pair(parts)
-        far = scatter_far(other)
+    def scatter_first(part):
+        return halve(part).astype(BF) if group_rows == 2 else part
+
+    def scatter_cross(first):
+        return swap(first, 2) if group_rows == 2 else first
+
+    def scatter_rest(far, own):
+        if group_rows != 2:
+            own, far = scatter_pair([own])
+            far = swap(halve(far).astype(BF), 2)
         return halve(own) + far.astype(F32)
 
     state = token_rows.astype(F32)
@@ -860,28 +868,34 @@
     hiddens0 = gather_group(hidden)
     (w_qkv0,) = build_hops(z_qkv0, [plan_qkv])
     attended0 = attention(front(hiddens0, w_qkv0))
-    d_branch, attended0[0] = tie((cotangent_rows, attended0[0]))
-    d_branch_rows = gather_group(d_branch)
-    z_rest0, d_branch_rows = tie((z_rest0, d_branch_rows))
     w_in0, both = build(z_rest0, [(0, n_in, fold, 1), (n_in, n_both, 1, TP)])
     inners0, actives0 = inside(hiddens0, w_in0, vectors[0][2])
     w_out0, w_down0 = both[:cols], both[cols:]
-    parts = [None] * len(hiddens0)
-    for r in reversed(range(len(hiddens0))):
-        parts[r] = dot(attended0[r][0], w_out0) + dot(actives0[r], w_down0)
-    state = state + scatter_group(parts) + vectors[0][3]
+    def leave(r, attended, actives, w_out, w_down):
+        return dot(attended[r][0], w_out) + dot(actives[r], w_down)
+
+    last = group_rows - 1
+    first = scatter_first(leave(last, attended0, actives0, w_out0, w_down0))
+    own = first
+    if last:
+        first, actives0 = tie((first, actives0))
+        own = leave(0, attended0, actives0, w_out0, w_down0)
+    cotangent, own = tie((cotangent, own))
+    cotangent_rows = to_rows(cotangent[None])[0]
+    state = state + scatter_rest(scatter_cross(first), own) + vectors[0][3]
     normed1, inv_std1, hidden = norm(state, vectors[1])
     hiddens1 = gather_group(hidden)
     w_qkv1, w_in1, both = build(
         z_rest1, [plan_qkv, (n_qkv, n_in, fold, 1), (n_qkv + n_in, n_both, 1, TP)]
     )
-    attended1 = attention(front(hiddens1, w_qkv1))
+    projs = front(hiddens1, w_qkv1)
+    d_branch, projs = tie((cotangent_rows, projs))
+    d_branch_rows = gather_group(d_branch)
+    attended1 = attention(projs)
     inners1, actives1 = inside(hiddens1, w_in1, vectors[1][2])
     w_out1, w_down1 = both[:cols], both[cols:]
-    parts = [
-        dot(attended1[r][0], w_out1) + dot(actives1[r], w_down1) for r in range(len(hiddens1))
-    ]
-    outputs = (state + scatter_group(parts) + vectors[1][3]).astype(BF)
+    first_out = scatter_first(leave(last, attended1, actives1, w_out1, w_down1))
+    own_out = leave(0, attended1, actives1, w_out1, w_down1) if last else first_out
 
     def lay_out(grads, plan):
         if pieces:
@@ -915,7 +929,15 @@
     def both_grads(d_rows, attended, actives):
         g_out = sum(dot_tn(a[0], d) for a, d in zip(attended, d_rows))
         g_down = sum(dot_tn(a, d) for a, d in zip(actives, d_rows))
-        return jnp.concatenate([g_out, g_down])
+        return [g_out, g_down] if pieces else [jnp.concatenate([g_out, g_down])]
+
+    def both_plan(start):
+        if not pieces:
+            return [(start, n_both, 1, TP)]
+        return [
+            (start, TP * my_out, 1, TP, my_units),
+            (start + my_out, TP * fold * my_out, 1, TP, my_units),
+        ]
 
     def back_inner(d_row, inner, w_down):
         return (dot_nt(d_row, w_down) * inner.astype(F32)).astype(BF)
@@ -947,40 +969,50 @@
         )
 
     turns = range(group_rows)
-    last = group_rows - 1
-    d_inners1, d_projs1, parts = [None] * group_rows, [None] * group_rows, [None] * group_rows
+    d_inners1, d_projs1 = [None] * group_rows, [None] * group_rows
     d_rows = d_branch_rows
     for r in turns:
         d_inners1[r] = back_inner(d_rows[r], inners1[r], w_down1)
     g_in = sum(dot_tn(hiddens1[r], d_inners1[r]) for r in turns)
     laid = lay_out(
-        [g_in, both_grads(d_rows, attended1, actives1)],
-        [(0, n_in, fold, 1), (n_in, n_both, 1, TP)],
-    )
-    laid, d_rows, d_inners1 = tie((laid, d_rows, d_inners1))
+        [g_in, *both_grads(d_rows, attended1, actives1)],
+        [(0, n_in, fold, 1), *both_plan(n_in)],
+    )
+    laid, d_rows, d_inners1, first_out = tie((laid, d_rows, d_inners1, first_out))
     r_early1 = sum_all(laid)
-    for r in reversed(turns):
-        d_projs1[r] = back_attention(r, d_rows[r], attended1[r], w_out1)
-        parts[r] = dot_nt(d_inners1[r], w_in1) + dot_nt(d_projs1[r], w_qkv1)
-        if r == last and last:
-            parts[r], d_rows, outputs = tie((parts[r], d_rows, outputs))
+
+    def back_part(r, d_inners, d_projs, w_in, w_qkv):
+        return dot_nt(d_inners[r], w_in) + dot_nt(d_projs[r], w_qkv)
+
+    d_projs1[last] = back_attention(last, d_rows[last], attended1[last], w_out1)
+    far_out = scatter_cross(first_out)
+    d_projs1[last], far_out = tie((d_projs1[last], far_out))
+    first = scatter_first(back_part(last, d_inners1, d_projs1, w_in1, w_qkv1))
+    outputs = (state + scatter_rest(far_out, own_out) + vectors[1][3]).astype(BF)
+    own, far = first, first
+    if last:
+        first, d_rows, outputs = tie((first, d_rows, outputs))
+        d_projs1[0] = back_attention(0, d_rows[0], attended1[0], w_out1)
+        far = scatter_cross(first)
+        d_projs1[0], far = tie((d_projs1[0], far))
+        own = back_part(0, d_inners1, d_projs1, w_in1, w_qkv1)
     d_state = cotangent_rows.astype(F32)
-    d_hidden1 = scatter_group(parts)
+    d_hidden1 = scatter_rest(far, own)
     d_state = back_norm(d_state, d_hidden1, normed1, inv_std1, vectors[1])
     d_branch = d_state.astype(BF)
-    d_branch, d_projs1, r_early1, outputs = tie((d_branch, d_projs1, r_early1, outputs))
+    d_branch, d_projs1, outputs = tie((d_branch, d_projs1, outputs))
     outputs = from_rows(outputs)
     d_rows = gather_group(d_branch)
     g_qkv = sum(dot_tn(hiddens1[r], d_projs1[r]) for r in turns)
     laid = lay_out([g_qkv], [plan_qkv])
-    d_rows[0], laid = tie((d_rows[0], laid))
+    d_rows[0], laid, r_early1 = tie((d_rows[0], laid, r_early1))
     r_qkv1 = sum_all(laid)
     d_inners0, d_projs0 = [None] * group_rows, [None] * group_rows
     d_inners0[0] = back_inner(d_rows[0], inners0[0], w_down0)
     d_projs0[0] = back_attention(0, d_rows[0], attended0[0], w_out0)
     d_rows, d_projs0[0], d_inners0[0] = tie((d_rows, d_projs0[0], d_inners0[0]))
-    laid = lay_near([both_grads(d_rows, attended0, actives0)], [plan_both])
-    d_rows, laid = tie((d_rows, laid))
+    laid = lay_near(both_grads(d_rows, attended0, actives0), both_plan(0))
+    d_rows, laid, outputs = tie((d_rows, laid, outputs))
     s_both0 = sum_g(laid)
     for r in turns[1:]:
         d_inners0[r] = back_inner(d_rows[r], inners0[r], w_down0)
@@ -993,15 +1025,19 @@
         d_projs0[r] = back_attention(r, d_rows[r], attended0[r], w_out0)
     g_qkv = sum(dot_tn(hiddens0[r], d_projs0[r]) for r in turns)
     laid = lay_near([g_qkv], [plan_qkv])
-    d_projs0, laid, s_in0 = tie((d_projs0, laid, s_in0))
+    d_projs0, laid, s_in0, r_both0 = tie((d_projs0, laid, s_in0, r_both0))
     s_qkv0 = sum_g(laid)
-    for r in reversed(turns):
-        parts[r] = dot_nt(d_inners0[r], w_in0) + dot_nt(d_projs0[r], w_qkv0)
-    parts, r_both0, s_in0, r_qkv1 = tie((parts, r_both0, s_in0, r_qkv1))
     r_in0 = sum_z(s_in0)
+    first = scatter_first(back_part(last, d_inners0, d_projs0, w_in0, w_qkv0))
+    own = first
+    if last:
+        first, d_inners0, r_in0 = tie((first, d_inners0, r_in0))
+        own = back_part(0, d_inners0, d_projs0, w_in0, w_qkv0)
     s_qkv0, r_in0 = tie((s_qkv0, r_in0))
     r_qkv0 = sum_z(s_qkv0)
-    d_hidden0 = scatter_group(parts)
+    own, far = tie((own, scatter_cross(first)))
+    d_hidden0 = scatter_rest(far, own)
+    d_hidden0, r_qkv0, r_qkv1 = tie((d_hidden0, r_qkv0, r_qkv1))
     small_grads = [
         sums(d_hidden0, normed0, d_inners0, d_branch),
         sums(d_hidden1, normed1, d_inners1, cotangent_rows),
@@ -1010,15 +1046,14 @@
     swapped = jnp.concatenate(
         [r.reshape(TP, my_units, chunks, cols) for r in (r_both0, r_early1[n_in:])], axis=1
     )
-    mine = [lax.dynamic_index_in_dim(swapped, t ^ k, 0, keepdims=False) for k in range(TP)]
-    mine = [mine[0]] + [swap(mine[k], k) for k in range(1, TP)]
+    mine = turn(swapped)
     grad_in = from_rows(d_state.astype(BF))
     small_flat = jnp.concatenate(small_grads).reshape(n_all, small_here)
     small_flat = jnp.pad(small_flat, ((0, 0), (0, small_width - small_here)))
     if pieces:
         extra = small_flat.astype(BF).reshape(n_dp, -1, cols)
         extra = jnp.pad(extra, ((0, 0), (0, 16 - extra.shape[1]), (0, 0)))
-        ins = [r_qkv0, r_in0, r_qkv1, r_early1[:n_in]] + mine
+        ins = [r_qkv0, r_in0, r_qkv1, r_early1] + mine
         takes = [[(b, None) for b in blocks] for blocks in (qkv0, in0, qkv1, in1)]
         takes += [[(b, k) for b in turned0[0] + turned1[0]] for k in range(TP)]
         slots = place_blocks(

time: 794 us -> 781 us (0.984)
  waiting for transfers between devices: 196 us -> 244 us
  starting transfers between devices: 108 us -> 86.3 us
  blocking collectives: 13.7 us -> 0 us
  other arithmetic: 83 us -> 70.2 us
  local copies, waits for them, and re-layouts: 56.1 us -> 44 us
  matrix products: 157 us -> 169 us
  Pallas kernels: 148 us -> 137 us
    all_to_all x1, starting transfers between devices: 25.4 us -> 6.04 us  [body(): lax.all_to_all(small_part, 'seq', split_axis=0, concat_axis=0, tiled=True)]
    ppermute x32 -> x35, waiting for transfers between devices: 94.7 us -> 112 us  [swap(): return lax.ppermute(value, DP, [(i, i ^ bit) for i in range(n_dp)])]
    ppermute x2 -> x4, waiting for transfers between devices: 22.2 us -> 39.2 us  [to_rows(): parts.append(lax.ppermute(send, ALL, row_pairs(pairs, False)))]
    all_to_all x1, starting transfers between devices: 28.8 us -> 12.9 us  [to_all(): return lax.all_to_all(value, ALL, split_axis=0, concat_axis=0, tiled=True)]
    all_to_all x1 -> x0, blocking collectives: 13.7 us -> none  [body(): lax.all_to_all(swapped, ('x', 'core'), split_axis=0, concat_axis=0, tiled...]
    dot_general x16, matrix products: 44.4 us -> 57.2 us  [dot(): return jnp.dot(left, right, preferred_element_type=F32)]
    ppermute x3, waiting for transfers between devices: 11.8 us -> 0.26 us  [hop_z(): lax.ppermute(value, 'seq', [(i, (i + by) % n_seq) for i in range(n_seq)])]
    all_to_all x1, waiting for transfers between devices: 0.24 us -> 11 us  [body(): owned = lax.all_to_all(slots, DP, split_axis=0, concat_axis=0, tiled=True)]
  transfers between devices with their start and end apart: 52 -> 57, of which waited for: 19 -> 26; matrix products, arithmetic and copies ran while one was open for 30% -> 28% of each run, Pallas kernels for 16% -> 14%
where the time goes in v3:
time: 781 us; the launch traced here: 772 us
  waiting for transfers between devices  244 us (31%)
  matrix products  169 us (22%)
  Pallas kernels  137 us (18%)
  starting transfers between devices  86.3 us (11%)
  other arithmetic  70.2 us (9%)
  local copies, waits for them, and re-layouts  44 us (6%)
  between operations  21.5 us (3%)
    ppermute x35, waiting for transfers between devices, swap(): return lax.ppermute(value, DP, [(i, i ^ bit) for i in range(n_dp)])  112 us
    dot_general x16, matrix products, dot_nt(): lax.dot_general(left, right, (((1,), (1,)), ((), ())), preferred_element_...  62.3 us
    dot_general x16, matrix products, dot(): return jnp.dot(left, right, preferred_element_type=F32)  57.2 us
    pallas_call x4, Pallas kernels, attend_back(): pl.pallas_call(functools.partial(attend_back_kernel, half), in_specs=[pl....  50.8 us
    dot_general x16, matrix products, dot_tn(): lax.dot_general(left, right, (((0,), (0,)), ((), ())), preferred_element_...  49.5 us
    ppermute x4, waiting for transfers between devices, to_rows(): parts.append(lax.ppermute(send, ALL, row_pairs(pairs, False)))  39.2 us
    pallas_call x4, Pallas kernels, attend(): pl.pallas_call(functools.partial(attend_kernel, half), in_specs=[pl.Block...  31.6 us
    ppermute x4, waiting for transfers between devices, from_rows(): parts.append(lax.ppermute(send, ALL, row_pairs(pairs, True)))  26.5 us
  transfers between devices with their start and end apart: 57, of which 26 were waited for; matrix products, arithmetic and copies ran while one was open for 28% of the time, Pallas kernels for 14%

profile of v3, /device:TPU:0, one launch (start us, length us, event | category | flops | bytes accessed | tf_op | source)
XLA Modules:
  0.0 772.2 jit_solution(4475970906645811923)
XLA Ops:
  7.2 5.3 pack.1
  12.5 5.3 all-to-all-start
  27.7 10.2 %collective-permute-done.1 = bf16[1,256,1024]{2,1,0:T(8,128)(2,1)S(1)} collective-permute-done((bf16[1,256,1024]{2,1,0:T(8,128)(2,1)S(1)}, bf16[1,256,1024]{2,1,0:T(8,128)(2,1)S(1)}, u32[]{:S(2)}, u32[]{:S(2)}) %collective-permute-start.1) | collective-permute-done | bytes 524320 | tf_op jit(solution)/shard_map/ppermute | solution.py:619
  38.1 6.4 all-to-all-done
  46.6 12.9 %all-to-all-start.1 = ((bf16[32,2,256]{2,1,0:T(2,128)(2,1)}), bf16[32,2,256]{2,1,0:T(2,128)(2,1)S(1)}, u32[]{:S(2)}, u32[]{:S(2)}) async-start(bf16[32,2,256]{2,1,0:T(2,128)(2,1)} %reshape.298), calls=%async_computation.1 | async-start | bytes 65536 | tf_op jit(solution)/shard_map/all_to_all | solution.py:594
  63.0 3.8 all-to-all-done.1
  70.0 5.2 collective-permute-done.9
  88.3 3.8 fusion.75
  92.3 18.6 %collective-permute-done.11 = bf16[512,1024]{1,0:T(8,128)(2,1)} collective-permute-done((bf16[512,1024]{1,0:T(8,128)(2,1)}, bf16[512,1024]{1,0:T(8,128)(2,1)}, u32[]{:S(2)}, u32[]{:S(2)}) %collective-permute-start.11) | collective-permute-done | bytes 1048608 | tf_op jit(solution)/shard_map/ppermute | solution.py:584
  118.4 16.4 %collective-permute-done.7.refs_5_ = bf16[3,24,16,256]{3,2,1,0:T(8,128)(2,1)S(1)} collective-permute-done((bf16[3,24,16,256]{3,2,1,0:T(8,128)(2,1)}, bf16[3,24,16,256]{3,2,1,0:T(8,128)(2,1)S(1)}, u32[]{:S(2)}, u32[]{:S(2)}) %collective-permute-start.7) | collective-permute-done | bytes 589856 | tf_op jit(solution)/shard_map/ppermute | solution.py:584
  140.2 3.5 fusion.128.proj_ref
  143.7 7.7 %attend.5 = (bf16[1024,256]{1,0:T(8,128)(2,1)S(1)}, bf16[1024,768]{1,0:T(8,128)(2,1)S(1)}, f32[8,1024]{1,0:T(8,128)S(1)}) custom-call(s32[1]{0:T(128)} %bitcast.1.flip_ref, f32[1024,768]{1,0:T(8,128)} %fusion.128.proj_ref, f32[3,1024,128]{2,1,0:T(8,128)} %get-tuple-element.222.tab_ref, bf16[1024,256]{1,0:T(8,128)(2,1)S(1)} %copy-done.6, ...), custom_call_target="tpu_custom_call" | custom-call | flops 2147483648 | bytes 6291456 | tf_op jit(solution)/shard_map/attend/pallas_call | solution.py:200
  152.6 19.2 %all-gather.5.cloned.1.call-done = bf16[576,16,256]{2,1,0:T(8,128)(2,1)} async-done(((bf16[72,16,256]{2,1,0:T(8,128)(2,1)}), bf16[576,16,256]{2,1,0:T(8,128)(2,1)}) %all-gather.5.cloned.1.call-update) | async-done | bytes 4718608 | tf_op jit(solution)/shard_map/all_gather | solution.py:689
  171.8 4.0 assemble.4
  178.3 10.3 %multiply_convert_fusion.6 = (bf16[1024,1024]{1,0:T(8,128)(2,1)}, bf16[1024,1024]{1,0:T(8,128)(2,1)S(1)}, f32[1024,1024]{1,0:T(8,128)}) fusion(f32[1024]{0:T(1024)S(1)} %bitcast.180, f32[1024,1024]{1,0:T(8,128)S(1)} %fusion.129, bf16[1024,1024]{1,0:T(8,128)(2,1)S(1)} %get-tuple-element.119, bf16[512,1024]{1,0:T(8,128)(2,1)} %collective-permute-done.2, ...), kind=kOutput, calls=%fused_computation.48 | convolution fusion | flops 2172649472 | bytes 16781312 | tf_op jit(solution)/shard_map/dot_general | solution.py:37
  192.0 5.1 fusion.114.proj_ref
  197.1 7.9 %attend.4 = (bf16[1024,256]{1,0:T(8,128)(2,1)S(1)}, bf16[1024,768]{1,0:T(8,128)(2,1)S(1)}, f32[8,1024]{1,0:T(8,128)S(1)}) custom-call(s32[1]{0:T(128)} %bitcast.1.flip_ref, f32[1024,768]{1,0:T(8,128)} %fusion.114.proj_ref, f32[3,1024,128]{2,1,0:T(8,128)} %get-tuple-element.221.tab_ref, bf16[1024,256]{1,0:T(8,128)(2,1)S(1)} %copy-done.9, ...), custom_call_target="tpu_custom_call" | custom-call | flops 2147483648 | bytes 6291456 | tf_op jit(solution)/shard_map/attend/pallas_call | solution.py:200
  219.5 22.8 %collective-permute-done.17 = bf16[512,1024]{1,0:T(8,128)(2,1)} collective-permute-done((bf16[512,1024]{1,0:T(8,128)(2,1)}, bf16[512,1024]{1,0:T(8,128)(2,1)}, u32[]{:S(2)}, u32[]{:S(2)}) %collective-permute-start.17) | collective-permute-done | bytes 1048608 | tf_op jit(solution)/shard_map/ppermute | solution.py:584
  252.4 28.9 %collective-permute-done.15 = bf16[1,256,1024]{2,1,0:T(8,128)(2,1)} collective-permute-done((bf16[1,256,1024]{2,1,0:T(8,128)(2,1)S(1)}, bf16[1,256,1024]{2,1,0:T(8,128)(2,1)}, u32[]{:S(2)}, u32[]{:S(2)}) %collective-permute-start.15) | collective-permute-done | bytes 524320 | tf_op jit(solution)/shard_map/ppermute | solution.py:619
  284.6 6.3 assemble.5
  290.8 7.3 collective-permute-start.20
  298.1 3.6 fusion.109
  301.7 5.6 fusion.110.proj_ref
  308.6 4.8 fusion.56
  324.8 8.2 %attend.7 = (bf16[1024,256]{1,0:T(8,128)(2,1)S(1)}, bf16[1024,768]{1,0:T(8,128)(2,1)S(1)}, f32[8,1024]{1,0:T(8,128)S(1)}) custom-call(s32[1]{0:T(128)} %bitcast.1.flip_ref, f32[1024,768]{1,0:T(8,128)} %fusion.130.proj_ref, f32[3,1024,128]{2,1,0:T(8,128)} %get-tuple-element.222.tab_ref, bf16[1024,256]{1,0:T(8,128)(2,1)S(1)} %copy-done.6, ...), custom_call_target="tpu_custom_call" | custom-call | flops 2147483648 | bytes 6291456 | tf_op jit(solution)/shard_map/attend/pallas_call | solution.py:200
  337.8 7.8 %attend.6 = (bf16[1024,256]{1,0:T(8,128)(2,1)S(1)}, bf16[1024,768]{1,0:T(8,128)(2,1)S(1)}, f32[8,1024]{1,0:T(8,128)S(1)}) custom-call(s32[1]{0:T(128)} %bitcast.1.flip_ref, f32[1024,768]{1,0:T(8,128)} %fusion.110.proj_ref, f32[3,1024,128]{2,1,0:T(8,128)} %get-tuple-element.221.tab_ref, bf16[1024,256]{1,0:T(8,128)(2,1)S(1)} %copy-done.10, ...), custom_call_target="tpu_custom_call" | custom-call | flops 2147483648 | bytes 6291456 | tf_op jit(solution)/shard_map/attend/pallas_call | solution.py:200
  349.4 7.1 multiply_convert_fusion.5
  359.9 3.8 fusion.108
  367.7 4.7 multiply_convert_fusion.4
  372.4 5.3 convolution_add_fusion.9.refs_2_
  381.8 6.2 disassemble.5
  398.3 12.5 %attend_back.4 = bf16[1024,768]{1,0:T(8,128)(2,1)S(1)} custom-call(s32[1]{0:T(128)} %bitcast.1.flip_ref, bf16[1024,768]{1,0:T(8,128)(2,1)} %copy-done.28, bf16[1024,256]{1,0:T(8,128)(2,1)S(1)} %convolution_convert_fusion.3.dctx_ref, f32[8,1024]{1,0:T(8,128)S(1)} %get-tuple-element.138.lse_ref, f32[3,1024,128]{2,1,0:T(8,128)} %get-tuple-element.222.tab_ref, ...), custom_call_target="tpu_custom_call" | custom-call | flops 5368709120 | bytes 6291456 | tf_op jit(solution)/shard_map/attend_back/pallas_call | solution.py:223
  426.7 13.0 %attend_back.5 = bf16[1024,768]{1,0:T(8,128)(2,1)S(1)} custom-call(s32[1]{0:T(128)} %bitcast.1.flip_ref, bf16[1024,768]{1,0:T(8,128)(2,1)} %copy-done.27, bf16[1024,256]{1,0:T(8,128)(2,1)S(1)} %convolution_convert_fusion.2.dctx_ref, f32[8,1024]{1,0:T(8,128)S(1)} %get-tuple-element.144.lse_ref, f32[3,1024,128]{2,1,0:T(8,128)} %get-tuple-element.221.tab_ref, ...), custom_call_target="tpu_custom_call" | custom-call | flops 5368709120 | bytes 6291456 | tf_op jit(solution)/shard_map/attend_back/pallas_call | solution.py:223
  439.7 8.7 %collective-permute-done.28 = bf16[512,1024]{1,0:T(8,128)(2,1)} collective-permute-done((bf16[512,1024]{1,0:T(8,128)(2,1)}, bf16[512,1024]{1,0:T(8,128)(2,1)}, u32[]{:S(2)}, u32[]{:S(2)}) %collective-permute-start.28) | collective-permute-done | bytes 1048608 | tf_op jit(solution)/shard_map/ppermute | solution.py:584
  465.5 5.4 collective-permute-start.34
  474.1 12.4 %collective-permute-done.31 = bf16[512,1024]{1,0:T(8,128)(2,1)} collective-permute-done((bf16[512,1024]{1,0:T(8,128)(2,1)}, bf16[512,1024]{1,0:T(8,128)(2,1)}, u32[]{:S(2)}, u32[]{:S(2)}) %collective-permute-start.31) | collective-permute-done | bytes 1048608 | tf_op jit(solution)/shard_map/ppermute | solution.py:584
  491.6 14.5 %collective-permute-done.34 = bf16[256,1024]{1,0:T(8,128)(2,1)} collective-permute-done((bf16[256,1024]{1,0:T(8,128)(2,1)}, bf16[256,1024]{1,0:T(8,128)(2,1)}, u32[]{:S(2)}, u32[]{:S(2)}) %collective-permute-start.34) | collective-permute-done | bytes 524320 | tf_op jit(solution)/shard_map/ppermute | solution.py:634
  517.6 7.5 multiply_convert_fusion.1
  525.2 12.6 %attend_back.6 = bf16[1024,768]{1,0:T(8,128)(2,1)S(1)} custom-call(s32[1]{0:T(128)} %bitcast.1.flip_ref, bf16[1024,768]{1,0:T(8,128)(2,1)} %copy-done.26, bf16[1024,256]{1,0:T(8,128)(2,1)S(1)} %convolution_convert_fusion.1.dctx_ref, f32[8,1024]{1,0:T(8,128)S(1)} %get-tuple-element.155.lse_ref, f32[3,1024,128]{2,1,0:T(8,128)} %get-tuple-element.221.tab_ref, ...), custom_call_target="tpu_custom_call" | custom-call | flops 5368709120 | bytes 6291456 | tf_op jit(solution)/shard_map/attend_back/pallas_call | solution.py:223
  542.9 4.6 convolution_add_fusion.6.refs_1_
  550.8 6.4 multiply_convert_fusion
  557.3 4.8 fusion.112
  562.1 4.6 convolution_add_fusion.5.refs_0_
  570.1 4.4 fusion.137
  574.5 5.4 collective-permute-done.35
  581.3 5.9 all-to-all-start.2
  587.3 5.7 fusion.111
  596.1 12.8 %attend_back.7 = bf16[1024,768]{1,0:T(8,128)(2,1)S(1)} custom-call(s32[1]{0:T(128)} %bitcast.1.flip_ref, bf16[1024,768]{1,0:T(8,128)(2,1)} %copy-done.25, bf16[1024,256]{1,0:T(8,128)(2,1)S(1)} %convolution_convert_fusion.dctx_ref, f32[8,1024]{1,0:T(8,128)S(1)} %get-tuple-element.172.lse_ref, f32[3,1024,128]{2,1,0:T(8,128)} %get-tuple-element.222.tab_ref, ...), custom_call_target="tpu_custom_call" | custom-call | flops 5368709120 | bytes 6291456 | tf_op jit(solution)/shard_map/attend_back/pallas_call | solution.py:223
  608.9 4.3 convolution_add_fusion.11.refs_0_
  615.3 3.7 collective-permute-done.36
  622.7 4.8 all-to-all-start.3
  627.5 4.5 convolution_add_fusion.4
  641.3 18.8 %all-to-all-done.3 = bf16[4,32,16,256]{3,2,1,0:T(8,128)(2,1)S(1)} async-done(((bf16[4,32,16,256]{3,2,1,0:T(8,128)(2,1)}), bf16[4,32,16,256]{3,2,1,0:T(8,128)(2,1)S(1)}, u32[]{:S(2)}, u32[]{:S(2)}) %all-to-all-start.3) | async-done | bytes 1048608 | tf_op jit(solution)/shard_map/all_to_all | solution.py:926
  661.0 5.3 fusion.138
  668.7 3.7 all-to-all-start.4
  672.4 5.3 fusion.127
  677.8 5.8 collective-permute-done.38
  695.6 7.1 reduce-scatter.5.cloned.1.call-done
  705.7 4.4 place.1
  710.1 4.5 all-to-all-start.5
  718.9 12.0 %collective-permute-done.42 = bf16[256,1024]{1,0:T(8,128)(2,1)S(1)} collective-permute-done((bf16[256,1024]{1,0:T(8,128)(2,1)S(1)}, bf16[256,1024]{1,0:T(8,128)(2,1)S(1)}, u32[]{:S(2)}, u32[]{:S(2)}) %collective-permute-start.42) | collective-permute-done | bytes 524320 | tf_op jit(solution)/shard_map/ppermute | solution.py:634
  731.0 11.0 %all-to-all-done.5.from_ref = bf16[8,528,256]{2,1,0:T(8,128)(2,1)} async-done(((bf16[8,528,256]{2,1,0:T(8,128)(2,1)}), bf16[8,528,256]{2,1,0:T(8,128)(2,1)}, u32[]{:S(2)}, u32[]{:S(2)}) %all-to-all-start.5) | async-done | bytes 2162720 | tf_op jit(solution)/shard_map/all_to_all | solution.py:1062
  743.5 6.0 all-to-all-start.6
  750.6 14.0 %adam.1 = (f32[32,32768]{1,0:T(8,128)}, f32[32,32768]{1,0:T(8,128)}, f32[32,32768]{1,0:T(8,128)}, bf16[32,32768]{1,0:T(8,128)(2,1)}) custom-call(bf16[8,528,256]{2,1,0:T(8,128)(2,1)} %all-to-all-done.5.from_ref, f32[32,32768]{1,0:T(8,128)} %w_ref.1, f32[32,32768]{1,0:T(8,128)} %one_ref.1, f32[32,32768]{1,0:T(8,128)} %two_ref.1), custom_call_target="tpu_custom_call" | custom-call | flops 20971520 | bytes 29360128 | tf_op jit(solution)/shard_map/adam/pallas_call | solution.py:500
  (495 shorter events, 226.5 us)
Async XLA Ops:
  12.5 32.1 %all-to-all-start = ((bf16[8,512,256]{2,1,0:T(8,128)(2,1)}), bf16[8,512,256]{2,1,0:T(8,128)(2,1)}, u32[]{:S(2)}, u32[]{:S(2)}) async-start(bf16[8,512,256]{2,1,0:T(8,128)(2,1)} %pack.1), calls=%async_computation | async-start | bytes 4194304 | tf_op jit(solution)/shard_map/all_to_all | solution.py:672
  23.0 4.7 collective-permute-start
  23.7 14.2 %collective-permute-start.1 = (bf16[1,256,1024]{2,1,0:T(8,128)(2,1)S(1)}, bf16[1,256,1024]{2,1,0:T(8,128)(2,1)S(1)}, u32[]{:S(2)}, u32[]{:S(2)}) collective-permute-start(bf16[1,256,1024]{2,1,0:T(8,128)(2,1)S(1)} %get-tuple-element.241), channel_id=1, source_target_pairs={{0,1},{16,17},{1,0},{17,16},{2,5},{18,21},{3,4},{19,20},{4,3},{20,... | collective-permute-start | bytes 1572872 | tf_op jit(solution)/shard_map/ppermute | solution.py:619
  38.1 46.8 %copy-start.32 = (bf16[512,1024]{1,0:T(8,128)(2,1)}, bf16[512,1024]{1,0:T(8,128)(2,1)S(1)}, u32[]{:S(2)}) copy-start(bf16[512,1024]{1,0:T(8,128)(2,1)S(1)} %maximum_bitcast_fusion) | copy-start | bytes 3145732
  46.6 20.2 %all-to-all-start.1 = ((bf16[32,2,256]{2,1,0:T(2,128)(2,1)}), bf16[32,2,256]{2,1,0:T(2,128)(2,1)S(1)}, u32[]{:S(2)}, u32[]{:S(2)}) async-start(bf16[32,2,256]{2,1,0:T(2,128)(2,1)} %reshape.298), calls=%async_computation.1 | async-start | bytes 65536 | tf_op jit(solution)/shard_map/all_to_all | solution.py:594
  59.5 112.3 %all-gather.5.cloned.1.call-start = ((), (), s32[]{:S(2)}) async-start(), calls=%async_computation.11 | async-start | bytes 5308416 | tf_op jit(solution)/shard_map/all_gather | solution.py:689
  68.1 2.0 collective-permute-start.8
  68.1 7.1 collective-permute-start.9
  68.8 9.0 %collective-permute-start.10 = (bf16[20,16,256]{2,1,0:T(8,128)(2,1)S(1)}, bf16[20,16,256]{2,1,0:T(8,128)(2,1)S(1)}, u32[]{:S(2)}, u32[]{:S(2)}) collective-permute-start(bf16[20,16,256]{2,1,0:T(8,128)(2,1)S(1)} %get-tuple-element.250), channel_id=1, source_target_pairs={{0,12},{4,8},{8,4},{12,0},{16,28},{20,24},{24,20},{28,16},{1,13},{... | collective-permute-start | bytes 491528 | tf_op jit(solution)/shard_map/ppermute | solution.py:584
  79.5 205.1 %all-gather.7.cloned.1.call-start = ((), (), s32[]{:S(2)}) async-start(), calls=%async_computation.12 | async-start | bytes 7077888 | tf_op jit(solution)/shard_map/all_gather | solution.py:689
  80.6 32.1 %collective-permute-start.5 = (bf16[24,16,256]{2,1,0:T(8,128)(2,1)S(1)}, bf16[24,16,256]{2,1,0:T(8,128)(2,1)S(1)}, u32[]{:S(2)}, u32[]{:S(2)}) collective-permute-start(bf16[24,16,256]{2,1,0:T(8,128)(2,1)S(1)} %copy-done.13), channel_id=1, source_target_pairs={{0,3},{1,0},{2,1},{3,2},{4,7},{5,4},{6,5},{7,6},{8,11},{9,8},{10,9... | collective-permute-start | bytes 589832 | tf_op jit(solution)/shard_map/ppermute | solution.py:744
  81.2 32.0 %collective-permute-start.3 = (bf16[24,16,256]{2,1,0:T(8,128)(2,1)S(1)}, bf16[24,16,256]{2,1,0:T(8,128)(2,1)S(1)}, u32[]{:S(2)}, u32[]{:S(2)}) collective-permute-start(bf16[24,16,256]{2,1,0:T(8,128)(2,1)S(1)} %copy-done.13), channel_id=1, source_target_pairs={{0,1},{1,2},{2,3},{3,0},{4,5},{5,6},{6,7},{7,4},{8,9},{9,10},{10,1... | collective-permute-start | bytes 589832 | tf_op jit(solution)/shard_map/ppermute | solution.py:744
  82.7 30.8 %collective-permute-start.4 = (bf16[24,16,256]{2,1,0:T(8,128)(2,1)S(1)}, bf16[24,16,256]{2,1,0:T(8,128)(2,1)S(1)}, u32[]{:S(2)}, u32[]{:S(2)}) collective-permute-start(bf16[24,16,256]{2,1,0:T(8,128)(2,1)S(1)} %copy-done.13), channel_id=1, source_target_pairs={{0,2},{1,3},{2,0},{3,1},{4,6},{5,7},{6,4},{7,5},{8,10},{9,11},{10,... | collective-permute-start | bytes 589832 | tf_op jit(solution)/shard_map/ppermute | solution.py:744
  83.2 34.5 %collective-permute-start.6 = (bf16[24,16,256]{2,1,0:T(8,128)(2,1)S(1)}, bf16[24,16,256]{2,1,0:T(8,128)(2,1)S(1)}, u32[]{:S(2)}, u32[]{:S(2)}) collective-permute-start(bf16[24,16,256]{2,1,0:T(8,128)(2,1)S(1)} %copy-done.13), channel_id=1, source_target_pairs={{0,16},{4,20},{8,24},{12,28},{16,0},{20,4},{24,8},{28,12},{1,17},{... | collective-permute-start | bytes 589832 | tf_op jit(solution)/shard_map/ppermute | solution.py:584
  86.3 24.5 %collective-permute-start.11 = (bf16[512,1024]{1,0:T(8,128)(2,1)}, bf16[512,1024]{1,0:T(8,128)(2,1)}, u32[]{:S(2)}, u32[]{:S(2)}) collective-permute-start(bf16[512,1024]{1,0:T(8,128)(2,1)} %fusion.35), channel_id=1, source_target_pairs={{0,8},{4,12},{8,0},{12,4},{16,24},{20,28},{24,16},{28,20},{1,9},{5... | collective-permute-start | bytes 3145736 | tf_op jit(solution)/shard_map/ppermute | solution.py:584
  88.2 426.3 %reduce-scatter.3.cloned.1.call-start = ((), (), s32[]{:S(2)}) async-start(), calls=%async_computation.9 | async-start | bytes 5308416 | tf_op jit(solution)/shard_map/reduce_scatter | solution.py:912
  110.9 28.0 %collective-permute-start.12 = (bf16[512,1024]{1,0:T(8,128)(2,1)}, bf16[512,1024]{1,0:T(8,128)(2,1)}, u32[]{:S(2)}, u32[]{:S(2)}) collective-permute-start(bf16[512,1024]{1,0:T(8,128)(2,1)} %collective-permute-done.11), channel_id=1, source_target_pairs={{0,4},{4,0},{8,12},{12,8},{16,20},{20,16},{24,28},{28,24},{1,5},{5... | collective-permute-start | bytes 3145736 | tf_op jit(solution)/shard_map/ppermute | solution.py:584
  112.7 65.5 %collective-permute-start.2 = (bf16[512,1024]{1,0:T(8,128)(2,1)}, bf16[512,1024]{1,0:T(8,128)(2,1)}, u32[]{:S(2)}, u32[]{:S(2)}) collective-permute-start(bf16[512,1024]{1,0:T(8,128)(2,1)} %fusion.35), channel_id=1, source_target_pairs={{0,4},{4,0},{8,12},{12,8},{16,20},{20,16},{24,28},{28,24},{1,5},{5... | collective-permute-start | bytes 3145736 | tf_op jit(solution)/shard_map/ppermute | solution.py:584
  114.4 20.5 %collective-permute-start.7 = (bf16[3,24,16,256]{3,2,1,0:T(8,128)(2,1)}, bf16[3,24,16,256]{3,2,1,0:T(8,128)(2,1)S(1)}, u32[]{:S(2)}, u32[]{:S(2)}) collective-permute-start(bf16[3,24,16,256]{3,2,1,0:T(8,128)(2,1)} %pad_maximum_fusion.9), channel_id=1, source_target_pairs={{0,16},{4,20},{8,24},{12,28},{16,0},{20,4},{24,8},{28,12},{1,17},{... | collective-permute-start | bytes 1769480 | tf_op jit(solution)/shard_map/ppermute | solution.py:584
  117.7 60.5 %copy-start.93 = (f32[4,1,256]{2,1,0:T(1,128)}, f32[4,1,256]{2,1,0:T(1,128)S(1)}, u32[]{:S(2)}) copy-start(f32[4,1,256]{2,1,0:T(1,128)S(1)} %fusion.95) | copy-start | bytes 12292
  137.0 55.0 %copy-start.4 = (bf16[1024,768]{1,0:T(8,128)(2,1)}, bf16[1024,768]{1,0:T(8,128)(2,1)S(1)}, u32[]{:S(2)}) copy-start(bf16[1024,768]{1,0:T(8,128)(2,1)S(1)} %assemble.3) | copy-start | bytes 4718596
  152.6 38.4 %copy-start = (bf16[1024,256]{1,0:T(8,128)(2,1)}, bf16[1024,256]{1,0:T(8,128)(2,1)S(1)}, u32[]{:S(2)}) copy-start(bf16[1024,256]{1,0:T(8,128)(2,1)S(1)} %get-tuple-element.118) | copy-start | bytes 1572868
  175.9 34.9 %copy-start.11 = (bf16[1280,1024]{1,0:T(8,128)(2,1)}, bf16[1280,1024]{1,0:T(8,128)(2,1)S(1)}, u32[]{:S(2)}) copy-start(bf16[1280,1024]{1,0:T(8,128)(2,1)S(1)} %get-tuple-element.117) | copy-start | bytes 7864324
  191.9 13.2 %collective-permute-start.13 = (bf16[512,1024]{1,0:T(8,128)(2,1)S(1)}, bf16[512,1024]{1,0:T(8,128)(2,1)}, u32[]{:S(2)}, u32[]{:S(2)}) collective-permute-start(bf16[512,1024]{1,0:T(8,128)(2,1)S(1)} %slice.354), channel_id=1, source_target_pairs={{0,4},{4,0},{8,12},{12,8},{16,20},{20,16},{24,28},{28,24},{1,5},{5... | collective-permute-start | bytes 3145736 | tf_op jit(solution)/shard_map/ppermute | solution.py:584
  213.5 28.8 %copy-start.33 = (bf16[512,1024]{1,0:T(8,128)(2,1)S(1)}, bf16[512,1024]{1,0:T(8,128)(2,1)}, u32[]{:S(2)}) copy-start(bf16[512,1024]{1,0:T(8,128)(2,1)} %copy-done.32) | copy-start | bytes 3145732
  216.4 3.1 collective-permute-start.16
  216.9 25.4 %collective-permute-start.17 = (bf16[512,1024]{1,0:T(8,128)(2,1)}, bf16[512,1024]{1,0:T(8,128)(2,1)}, u32[]{:S(2)}, u32[]{:S(2)}) collective-permute-start(bf16[512,1024]{1,0:T(8,128)(2,1)} %fusion.53), channel_id=1, source_target_pairs={{0,8},{4,12},{8,0},{12,4},{16,24},{20,28},{24,16},{28,20},{1,9},{5... | collective-permute-start | bytes 3145736 | tf_op jit(solution)/shard_map/ppermute | solution.py:584
  246.6 55.1 %copy-start.59 = (bf16[512,1024]{1,0:T(8,128)(2,1)}, bf16[512,1024]{1,0:T(8,128)(2,1)S(1)}, u32[]{:S(2)}) copy-start(bf16[512,1024]{1,0:T(8,128)(2,1)S(1)} %add_convert_fusion.2) | copy-start | bytes 3145732
  246.6 51.5 %collective-permute-start.18 = (bf16[512,1024]{1,0:T(8,128)(2,1)S(1)}, bf16[512,1024]{1,0:T(8,128)(2,1)}, u32[]{:S(2)}, u32[]{:S(2)}) collective-permute-start(bf16[512,1024]{1,0:T(8,128)(2,1)S(1)} %add_convert_fusion.2), channel_id=1, source_target_pairs={{0,4},{4,0},{8,12},{12,8},{16,20},{20,16},{24,28},{28,24},{1,5},{5... | collective-permute-start | bytes 3145736 | tf_op jit(solution)/shard_map/ppermute | solution.py:584
  246.6 44.2 %collective-permute-start.19 = (bf16[512,1024]{1,0:T(8,128)(2,1)S(1)}, bf16[512,1024]{1,0:T(8,128)(2,1)}, u32[]{:S(2)}, u32[]{:S(2)}) collective-permute-start(bf16[512,1024]{1,0:T(8,128)(2,1)S(1)} %add_convert_fusion.2), channel_id=1, source_target_pairs={{0,8},{4,12},{8,0},{12,4},{16,24},{20,28},{24,16},{28,20},{1,9},{5... | collective-permute-start | bytes 3145736 | tf_op jit(solution)/shard_map/ppermute | solution.py:584
  248.1 3.4 collective-permute-start.14
  249.8 31.5 %collective-permute-start.15 = (bf16[1,256,1024]{2,1,0:T(8,128)(2,1)S(1)}, bf16[1,256,1024]{2,1,0:T(8,128)(2,1)}, u32[]{:S(2)}, u32[]{:S(2)}) collective-permute-start(bf16[1,256,1024]{2,1,0:T(8,128)(2,1)S(1)} %get-tuple-element.233), channel_id=1, source_target_pairs={{0,1},{16,17},{1,0},{17,16},{2,5},{18,21},{3,4},{19,20},{4,3},{20,... | collective-permute-start | bytes 1572872 | tf_op jit(solution)/shard_map/ppermute | solution.py:619
  290.8 22.6 %collective-permute-start.20 = (bf16[512,1024]{1,0:T(8,128)(2,1)}, bf16[512,1024]{1,0:T(8,128)(2,1)S(1)}, u32[]{:S(2)}, u32[]{:S(2)}) collective-permute-start(bf16[512,1024]{1,0:T(8,128)(2,1)} %collective-permute-done.19), channel_id=1, source_target_pairs={{0,4},{4,0},{8,12},{12,8},{16,20},{20,16},{24,28},{28,24},{1,5},{5... | collective-permute-start | bytes 3145736 | tf_op jit(solution)/shard_map/ppermute | solution.py:584
  319.4 28.7 %collective-permute-start.21 = (bf16[512,1024]{1,0:T(8,128)(2,1)}, bf16[512,1024]{1,0:T(8,128)(2,1)}, u32[]{:S(2)}, u32[]{:S(2)}) collective-permute-start(bf16[512,1024]{1,0:T(8,128)(2,1)} %maximum_bitcast_fusion.1), channel_id=1, source_target_pairs={{0,4},{4,0},{8,12},{12,8},{16,20},{20,16},{24,28},{28,24},{1,5},{5... | collective-permute-start | bytes 3145736 | tf_op jit(solution)/shard_map/ppermute | solution.py:584
  320.2 25.5 %collective-permute-start.22 = (bf16[512,1024]{1,0:T(8,128)(2,1)}, bf16[512,1024]{1,0:T(8,128)(2,1)}, u32[]{:S(2)}, u32[]{:S(2)}) collective-permute-start(bf16[512,1024]{1,0:T(8,128)(2,1)} %maximum_bitcast_fusion.1), channel_id=1, source_target_pairs={{0,8},{4,12},{8,0},{12,4},{16,24},{20,28},{24,16},{28,20},{1,9},{5... | collective-permute-start | bytes 3145736 | tf_op jit(solution)/shard_map/ppermute | solution.py:584
  336.3 20.2 %collective-permute-start.24 = (bf16[512,1024]{1,0:T(8,128)(2,1)}, bf16[512,1024]{1,0:T(8,128)(2,1)}, u32[]{:S(2)}, u32[]{:S(2)}) collective-permute-start(bf16[512,1024]{1,0:T(8,128)(2,1)} %slice.352), channel_id=1, source_target_pairs={{0,4},{4,0},{8,12},{12,8},{16,20},{20,16},{24,28},{28,24},{1,5},{5... | collective-permute-start | bytes 3145736 | tf_op jit(solution)/shard_map/ppermute | solution.py:584
  345.7 21.9 %collective-permute-start.23 = (bf16[512,1024]{1,0:T(8,128)(2,1)}, bf16[512,1024]{1,0:T(8,128)(2,1)S(1)}, u32[]{:S(2)}, u32[]{:S(2)}) collective-permute-start(bf16[512,1024]{1,0:T(8,128)(2,1)} %collective-permute-done.22), channel_id=1, source_target_pairs={{0,4},{4,0},{8,12},{12,8},{16,20},{20,16},{24,28},{28,24},{1,5},{5... | collective-permute-start | bytes 3145736 | tf_op jit(solution)/shard_map/ppermute | solution.py:584
  388.0 25.6 %collective-permute-start.25 = (bf16[512,1024]{1,0:T(8,128)(2,1)}, bf16[512,1024]{1,0:T(8,128)(2,1)}, u32[]{:S(2)}, u32[]{:S(2)}) collective-permute-start(bf16[512,1024]{1,0:T(8,128)(2,1)} %fusion.52), channel_id=1, source_target_pairs={{0,8},{4,12},{8,0},{12,4},{16,24},{20,28},{24,16},{28,20},{1,9},{5... | collective-permute-start | bytes 3145736 | tf_op jit(solution)/shard_map/ppermute | solution.py:584
  395.5 22.7 %collective-permute-start.27 = (bf16[512,1024]{1,0:T(8,128)(2,1)}, bf16[512,1024]{1,0:T(8,128)(2,1)}, u32[]{:S(2)}, u32[]{:S(2)}) collective-permute-start(bf16[512,1024]{1,0:T(8,128)(2,1)} %slice.350), channel_id=1, source_target_pairs={{0,4},{4,0},{8,12},{12,8},{16,20},{20,16},{24,28},{28,24},{1,5},{5... | collective-permute-start | bytes 3145736 | tf_op jit(solution)/shard_map/ppermute | solution.py:584
  418.1 3.8 collective-permute-start.26
  423.2 25.2 %collective-permute-start.28 = (bf16[512,1024]{1,0:T(8,128)(2,1)}, bf16[512,1024]{1,0:T(8,128)(2,1)}, u32[]{:S(2)}, u32[]{:S(2)}) collective-permute-start(bf16[512,1024]{1,0:T(8,128)(2,1)} %fusion.51), channel_id=1, source_target_pairs={{0,8},{4,12},{8,0},{12,4},{16,24},{20,28},{24,16},{28,20},{1,9},{5... | collective-permute-start | bytes 3145736 | tf_op jit(solution)/shard_map/ppermute | solution.py:584
  452.8 2.7 collective-permute-start.29
  461.0 25.5 %collective-permute-start.31 = (bf16[512,1024]{1,0:T(8,128)(2,1)}, bf16[512,1024]{1,0:T(8,128)(2,1)}, u32[]{:S(2)}, u32[]{:S(2)}) collective-permute-start(bf16[512,1024]{1,0:T(8,128)(2,1)} %get-tuple-element.149), channel_id=1, source_target_pairs={{0,8},{4,12},{8,0},{12,4},{16,24},{20,28},{24,16},{28,20},{1,9},{5... | collective-permute-start | bytes 3145736 | tf_op jit(solution)/shard_map/ppermute | solution.py:584
  462.8 45.6 %collective-permute-start.30 = (bf16[512,1024]{1,0:T(8,128)(2,1)}, bf16[512,1024]{1,0:T(8,128)(2,1)}, u32[]{:S(2)}, u32[]{:S(2)}) collective-permute-start(bf16[512,1024]{1,0:T(8,128)(2,1)} %get-tuple-element.149), channel_id=1, source_target_pairs={{0,4},{4,0},{8,12},{12,8},{16,20},{20,16},{24,28},{28,24},{1,5},{5... | collective-permute-start | bytes 3145736 | tf_op jit(solution)/shard_map/ppermute | solution.py:584
  463.8 26.9 %collective-permute-start.33 = (bf16[256,1024]{1,0:T(8,128)(2,1)}, bf16[256,1024]{1,0:T(8,128)(2,1)S(1)}, u32[]{:S(2)}, u32[]{:S(2)}) collective-permute-start(bf16[256,1024]{1,0:T(8,128)(2,1)} %get-tuple-element.230), channel_id=1, source_target_pairs={{0,0},{16,16},{1,1},{17,17},{4,2},{20,18},{5,3},{21,19},{2,4},{18,... | collective-permute-start | bytes 1572872 | tf_op jit(solution)/shard_map/ppermute | solution.py:634
  465.5 40.5 %collective-permute-start.34 = (bf16[256,1024]{1,0:T(8,128)(2,1)}, bf16[256,1024]{1,0:T(8,128)(2,1)}, u32[]{:S(2)}, u32[]{:S(2)}) collective-permute-start(bf16[256,1024]{1,0:T(8,128)(2,1)} %get-tuple-element.229), channel_id=1, source_target_pairs={{1,0},{17,16},{0,1},{16,17},{5,2},{21,18},{4,3},{20,19},{3,4},{19,... | collective-permute-start | bytes 1572872 | tf_op jit(solution)/shard_map/ppermute | solution.py:634
  486.5 25.0 %collective-permute-start.32 = (bf16[512,1024]{1,0:T(8,128)(2,1)}, bf16[512,1024]{1,0:T(8,128)(2,1)}, u32[]{:S(2)}, u32[]{:S(2)}) collective-permute-start(bf16[512,1024]{1,0:T(8,128)(2,1)} %collective-permute-done.31), channel_id=1, source_target_pairs={{0,4},{4,0},{8,12},{12,8},{16,20},{20,16},{24,28},{28,24},{1,5},{5... | collective-permute-start | bytes 3145736 | tf_op jit(solution)/shard_map/ppermute | solution.py:584
  550.7 29.2 %collective-permute-start.35 = (bf16[4,40,16,256]{3,2,1,0:T(8,128)(2,1)S(1)}, bf16[4,40,16,256]{3,2,1,0:T(8,128)(2,1)S(1)}, u32[]{:S(2)}, u32[]{:S(2)}) collective-permute-start(bf16[4,40,16,256]{3,2,1,0:T(8,128)(2,1)S(1)} %get-tuple-element.170), channel_id=1, source_target_pairs={{0,16},{4,20},{8,24},{12,28},{16,0},{20,4},{24,8},{28,12},{1,17},{... | collective-permute-start | bytes 3932168 | tf_op jit(solution)/shard_map/ppermute | solution.py:584
  581.3 38.9 %all-to-all-start.2 = ((bf16[4,40,16,256]{3,2,1,0:T(8,128)(2,1)}), bf16[4,40,16,256]{3,2,1,0:T(8,128)(2,1)}, u32[]{:S(2)}, u32[]{:S(2)}) async-start(bf16[4,40,16,256]{3,2,1,0:T(8,128)(2,1)} %add_convert_fusion), calls=%async_computation.3 | async-start | bytes 2621440 | tf_op jit(solution)/shard_map/all_to_all | solution.py:926
  593.0 26.0 %collective-permute-start.36 = (bf16[4,32,16,256]{3,2,1,0:T(8,128)(2,1)S(1)}, bf16[4,32,16,256]{3,2,1,0:T(8,128)(2,1)S(1)}, u32[]{:S(2)}, u32[]{:S(2)}) collective-permute-start(bf16[4,32,16,256]{3,2,1,0:T(8,128)(2,1)S(1)} %get-tuple-element.176), channel_id=1, source_target_pairs={{0,16},{4,20},{8,24},{12,28},{16,0},{20,4},{24,8},{28,12},{1,17},{... | collective-permute-start | bytes 3145736 | tf_op jit(solution)/shard_map/ppermute | solution.py:584
  622.7 37.4 %all-to-all-start.3 = ((bf16[4,32,16,256]{3,2,1,0:T(8,128)(2,1)}), bf16[4,32,16,256]{3,2,1,0:T(8,128)(2,1)S(1)}, u32[]{:S(2)}, u32[]{:S(2)}) async-start(bf16[4,32,16,256]{3,2,1,0:T(8,128)(2,1)} %add_convert_fusion.1), calls=%async_computation.4 | async-start | bytes 2097152 | tf_op jit(solution)/shard_map/all_to_all | solution.py:926
  627.5 75.2 %reduce-scatter.5.cloned.1.call-start = ((), (), s32[]{:S(2)}) async-start(), calls=%async_computation.10 | async-start | bytes 1769472 | tf_op jit(solution)/shard_map/reduce_scatter | solution.py:912
  635.1 3.0 collective-permute-start.37
  635.1 31.2 %collective-permute-start.40 = (bf16[4,24,16,256]{3,2,1,0:T(8,128)(2,1)}, bf16[4,24,16,256]{3,2,1,0:T(8,128)(2,1)}, u32[]{:S(2)}, u32[]{:S(2)}) collective-permute-start(bf16[4,24,16,256]{3,2,1,0:T(8,128)(2,1)} %get-tuple-element.186), channel_id=1, source_target_pairs={{0,16},{4,20},{8,24},{12,28},{16,0},{20,4},{24,8},{28,12},{1,17},{... | collective-permute-start | bytes 2359304 | tf_op jit(solution)/shard_map/ppermute | solution.py:584
  661.0 22.5 %collective-permute-start.38 = (bf16[512,1024]{1,0:T(8,128)(2,1)}, bf16[512,1024]{1,0:T(8,128)(2,1)}, u32[]{:S(2)}, u32[]{:S(2)}) collective-permute-start(bf16[512,1024]{1,0:T(8,128)(2,1)} %fusion.45), channel_id=1, source_target_pairs={{0,8},{4,12},{8,0},{12,4},{16,24},{20,28},{24,16},{28,20},{1,9},{5... | collective-permute-start | bytes 3145736 | tf_op jit(solution)/shard_map/ppermute | solution.py:584
  668.7 23.2 %all-to-all-start.4 = ((bf16[4,24,16,256]{3,2,1,0:T(8,128)(2,1)}), bf16[4,24,16,256]{3,2,1,0:T(8,128)(2,1)S(1)}, u32[]{:S(2)}, u32[]{:S(2)}) async-start(bf16[4,24,16,256]{3,2,1,0:T(8,128)(2,1)} %add_convert_fusion.3), calls=%async_computation.5 | async-start | bytes 1572864 | tf_op jit(solution)/shard_map/all_to_all | solution.py:926
  684.7 8.1 %collective-permute-start.39 = (bf16[512,1024]{1,0:T(8,128)(2,1)}, bf16[512,1024]{1,0:T(8,128)(2,1)}, u32[]{:S(2)}, u32[]{:S(2)}) collective-permute-start(bf16[512,1024]{1,0:T(8,128)(2,1)} %slice.347), channel_id=1, source_target_pairs={{0,4},{4,0},{8,12},{12,8},{16,20},{20,16},{24,28},{28,24},{1,5},{5... | collective-permute-start | bytes 3145736 | tf_op jit(solution)/shard_map/ppermute | solution.py:584
  689.2 15.8 %collective-permute-start.43 = (bf16[20,16,256]{2,1,0:T(8,128)(2,1)}, bf16[20,16,256]{2,1,0:T(8,128)(2,1)S(1)}, u32[]{:S(2)}, u32[]{:S(2)}) collective-permute-start(bf16[20,16,256]{2,1,0:T(8,128)(2,1)} %get-tuple-element.245), channel_id=1, source_target_pairs={{0,4},{4,0},{8,12},{12,8},{16,20},{20,16},{24,28},{28,24},{1,5},{5... | collective-permute-start | bytes 491528 | tf_op jit(solution)/shard_map/ppermute | solution.py:584
  689.7 15.3 %collective-permute-start.44 = (bf16[20,16,256]{2,1,0:T(8,128)(2,1)}, bf16[20,16,256]{2,1,0:T(8,128)(2,1)S(1)}, u32[]{:S(2)}, u32[]{:S(2)}) collective-permute-start(bf16[20,16,256]{2,1,0:T(8,128)(2,1)} %get-tuple-element.246), channel_id=1, source_target_pairs={{0,8},{4,12},{8,0},{12,4},{16,24},{20,28},{24,16},{28,20},{1,9},{5... | collective-permute-start | bytes 491528 | tf_op jit(solution)/shard_map/ppermute | solution.py:584
  690.0 15.1 %collective-permute-start.45 = (bf16[20,16,256]{2,1,0:T(8,128)(2,1)}, bf16[20,16,256]{2,1,0:T(8,128)(2,1)}, u32[]{:S(2)}, u32[]{:S(2)}) collective-permute-start(bf16[20,16,256]{2,1,0:T(8,128)(2,1)} %get-tuple-element.243), channel_id=1, source_target_pairs={{0,12},{4,8},{8,4},{12,0},{16,28},{20,24},{24,20},{28,16},{1,13},{... | collective-permute-start | bytes 491528 | tf_op jit(solution)/shard_map/ppermute | solution.py:584
  710.1 31.9 %all-to-all-start.5 = ((bf16[8,528,256]{2,1,0:T(8,128)(2,1)}), bf16[8,528,256]{2,1,0:T(8,128)(2,1)}, u32[]{:S(2)}, u32[]{:S(2)}) async-start(bf16[8,528,256]{2,1,0:T(8,128)(2,1)} %place.1), calls=%async_computation.7 | async-start | bytes 4325376 | tf_op jit(solution)/shard_map/all_to_all | solution.py:1062
  717.1 1.8 collective-permute-start.41
  717.8 13.2 %collective-permute-start.42 = (bf16[256,1024]{1,0:T(8,128)(2,1)S(1)}, bf16[256,1024]{1,0:T(8,128)(2,1)S(1)}, u32[]{:S(2)}, u32[]{:S(2)}) collective-permute-start(bf16[256,1024]{1,0:T(8,128)(2,1)S(1)} %get-tuple-element.225), channel_id=1, source_target_pairs={{1,0},{17,16},{0,1},{16,17},{5,2},{21,18},{4,3},{20,19},{3,4},{19,... | collective-permute-start | bytes 1572872 | tf_op jit(solution)/shard_map/ppermute | solution.py:634
  743.5 21.1 %all-to-all-start.6 = ((f32[4,1,512]{2,1,0:T(1,128)}), f32[4,1,512]{2,1,0:T(1,128)S(1)}, u32[]{:S(2)}, u32[]{:S(2)}) async-start(f32[4,1,512]{2,1,0:T(1,128)} %all_to_all.34), calls=%async_computation.8 | async-start | bytes 16384 | tf_op jit(solution)/shard_map/all_to_all | solution.py:1065
  (102 other events, 651.6 us)
Sparse Core Ops, SparseCore 0:
  79.6 92.1 all-gather.4
  173.9 109.3 all-gather.6
  396.0 111.7 reduce-scatter.2
  635.5 67.0 reduce-scatter.4

commit v4 on v3

--- a/solution.py
+++ b/solution.py
@@ -1001,18 +1001,25 @@
     d_state = back_norm(d_state, d_hidden1, normed1, inv_std1, vectors[1])
     d_branch = d_state.astype(BF)
     d_branch, d_projs1, outputs = tie((d_branch, d_projs1, outputs))
-    outputs = from_rows(outputs)
-    d_rows = gather_group(d_branch)
+    if group_rows == 2:
+        d_rows = [jnp.concatenate([d_branch, swap(d_branch, 1)]), swap(d_branch, 2)]
+    else:
+        d_rows = gather_group(d_branch)
     g_qkv = sum(dot_tn(hiddens1[r], d_projs1[r]) for r in turns)
     laid = lay_out([g_qkv], [plan_qkv])
-    d_rows[0], laid, r_early1 = tie((d_rows[0], laid, r_early1))
+    d_rows[0], laid, r_early1, outputs = tie((d_rows[0], laid, r_early1, outputs))
+    outputs = from_rows(outputs)
     r_qkv1 = sum_all(laid)
     d_inners0, d_projs0 = [None] * group_rows, [None] * group_rows
     d_inners0[0] = back_inner(d_rows[0], inners0[0], w_down0)
     d_projs0[0] = back_attention(0, d_rows[0], attended0[0], w_out0)
-    d_rows, d_projs0[0], d_inners0[0] = tie((d_rows, d_projs0[0], d_inners0[0]))
+    d_rows, d_projs0[0], d_inners0[0], outputs = tie(
+        (d_rows, d_projs0[0], d_inners0[0], outputs)
+    )
+    if group_rows == 2:
+        d_rows[1] = jnp.concatenate([d_rows[1], swap(d_rows[1], 1)])
     laid = lay_near(both_grads(d_rows, attended0, actives0), both_plan(0))
-    d_rows, laid, outputs = tie((d_rows, laid, outputs))
+    d_rows, laid = tie((d_rows, laid))
     s_both0 = sum_g(laid)
     for r in turns[1:]:
         d_inners0[r] = back_inner(d_rows[r], inners0[r], w_down0)
@@ -1025,7 +1032,7 @@
         d_projs0[r] = back_attention(r, d_rows[r], attended0[r], w_out0)
     g_qkv = sum(dot_tn(hiddens0[r], d_projs0[r]) for r in turns)
     laid = lay_near([g_qkv], [plan_qkv])
-    d_projs0, laid, s_in0, r_both0 = tie((d_projs0, laid, s_in0, r_both0))
+    d_projs0, laid, s_in0, r_both0, r_qkv1 = tie((d_projs0, laid, s_in0, r_both0, r_qkv1))
     s_qkv0 = sum_g(laid)
     r_in0 = sum_z(s_in0)
     first = scatter_first(back_part(last, d_inners0, d_projs0, w_in0, w_qkv0))
@@ -1037,7 +1044,7 @@
     r_qkv0 = sum_z(s_qkv0)
     own, far = tie((own, scatter_cross(first)))
     d_hidden0 = scatter_rest(far, own)
-    d_hidden0, r_qkv0, r_qkv1 = tie((d_hidden0, r_qkv0, r_qkv1))
+    d_hidden0, r_qkv0 = tie((d_hidden0, r_qkv0))
     small_grads = [
         sums(d_hidden0, normed0, d_inners0, d_branch),
         sums(d_hidden1, normed1, d_inners1, cotangent_rows),

time: 781 us -> 768 us (0.983)
  waiting for transfers between devices: 244 us -> 230 us
    ppermute x4, waiting for transfers between devices: 26.5 us -> 12.6 us  [from_rows(): parts.append(lax.ppermute(send, ALL, row_pairs(pairs, True)))]
    unnamed x234 -> x235, local copies, waits for them, and re-layouts: 21.9 us -> 21 us
  transfers between devices with their start and end apart: 57 -> 57, of which waited for: 26 -> 25; matrix products, arithmetic and copies ran while one was open for 28% -> 32% of each run, Pallas kernels for 14% -> 16%
where the time goes in v4:
time: 768 us; the launch traced here: 759 us
  waiting for transfers between devices  230 us (30%)
  matrix products  171 us (22%)
  Pallas kernels  137 us (18%)
  starting transfers between devices  90.6 us (12%)
  other arithmetic  65.3 us (9%)
  local copies, waits for them, and re-layouts  43.6 us (6%)
  between operations  21.5 us (3%)
    ppermute x35, waiting for transfers between devices, swap(): return lax.ppermute(value, DP, [(i, i ^ bit) for i in range(n_dp)])  108 us
    dot_general x16, matrix products, dot_nt(): lax.dot_general(left, right, (((1,), (1,)), ((), ())), preferred_element_...  63.9 us
    dot_general x16, matrix products, dot(): return jnp.dot(left, right, preferred_element_type=F32)  57.2 us
    pallas_call x4, Pallas kernels, attend_back(): pl.pallas_call(functools.partial(attend_back_kernel, half), in_specs=[pl....  50.8 us
    dot_general x16, matrix products, dot_tn(): lax.dot_general(left, right, (((0,), (0,)), ((), ())), preferred_element_...  50.1 us
    ppermute x4, waiting for transfers between devices, to_rows(): parts.append(lax.ppermute(send, ALL, row_pairs(pairs, False)))  39.2 us
    ppermute x35, starting transfers between devices, swap(): return lax.ppermute(value, DP, [(i, i ^ bit) for i in range(n_dp)])  32.3 us
    pallas_call x4, Pallas kernels, attend(): pl.pallas_call(functools.partial(attend_kernel, half), in_specs=[pl.Block...  31.6 us
  transfers between devices with their start and end apart: 57, of which 25 were waited for; matrix products, arithmetic and copies ran while one was open for 32% of the time, Pallas kernels for 16%

profile of v4, /device:TPU:0, one launch (start us, length us, event | category | flops | bytes accessed | tf_op | source)
XLA Modules:
  0.0 758.9 jit_solution(15867397445643963596)
XLA Ops:
  7.2 5.3 pack.1
  12.5 5.3 all-to-all-start
  27.7 10.2 %collective-permute-done.1 = bf16[1,256,1024]{2,1,0:T(8,128)(2,1)S(1)} collective-permute-done((bf16[1,256,1024]{2,1,0:T(8,128)(2,1)S(1)}, bf16[1,256,1024]{2,1,0:T(8,128)(2,1)S(1)}, u32[]{:S(2)}, u32[]{:S(2)}) %collective-permute-start.1) | collective-permute-done | bytes 524320 | tf_op jit(solution)/shard_map/ppermute | solution.py:619
  38.1 6.4 all-to-all-done
  46.6 12.9 %all-to-all-start.1 = ((bf16[32,2,256]{2,1,0:T(2,128)(2,1)}), bf16[32,2,256]{2,1,0:T(2,128)(2,1)S(1)}, u32[]{:S(2)}, u32[]{:S(2)}) async-start(bf16[32,2,256]{2,1,0:T(2,128)(2,1)} %reshape.298), calls=%async_computation.1 | async-start | bytes 65536 | tf_op jit(solution)/shard_map/all_to_all | solution.py:594
  63.0 3.8 all-to-all-done.1
  70.0 5.2 collective-permute-done.9
  88.3 3.8 fusion.75
  92.3 18.6 %collective-permute-done.11 = bf16[512,1024]{1,0:T(8,128)(2,1)} collective-permute-done((bf16[512,1024]{1,0:T(8,128)(2,1)}, bf16[512,1024]{1,0:T(8,128)(2,1)}, u32[]{:S(2)}, u32[]{:S(2)}) %collective-permute-start.11) | collective-permute-done | bytes 1048608 | tf_op jit(solution)/shard_map/ppermute | solution.py:584
  118.4 16.1 %collective-permute-done.7.refs_5_ = bf16[3,24,16,256]{3,2,1,0:T(8,128)(2,1)S(1)} collective-permute-done((bf16[3,24,16,256]{3,2,1,0:T(8,128)(2,1)}, bf16[3,24,16,256]{3,2,1,0:T(8,128)(2,1)S(1)}, u32[]{:S(2)}, u32[]{:S(2)}) %collective-permute-start.7) | collective-permute-done | bytes 589856 | tf_op jit(solution)/shard_map/ppermute | solution.py:584
  140.7 3.5 fusion.128.proj_ref
  144.2 7.7 %attend.5 = (bf16[1024,256]{1,0:T(8,128)(2,1)S(1)}, bf16[1024,768]{1,0:T(8,128)(2,1)S(1)}, f32[8,1024]{1,0:T(8,128)S(1)}) custom-call(s32[1]{0:T(128)} %bitcast.1.flip_ref, f32[1024,768]{1,0:T(8,128)} %fusion.128.proj_ref, f32[3,1024,128]{2,1,0:T(8,128)} %get-tuple-element.224.tab_ref, bf16[1024,256]{1,0:T(8,128)(2,1)S(1)} %copy-done.6, ...), custom_call_target="tpu_custom_call" | custom-call | flops 2147483648 | bytes 6291456 | tf_op jit(solution)/shard_map/attend/pallas_call | solution.py:200
  153.1 18.7 %all-gather.5.cloned.1.call-done = bf16[576,16,256]{2,1,0:T(8,128)(2,1)} async-done(((bf16[72,16,256]{2,1,0:T(8,128)(2,1)}), bf16[576,16,256]{2,1,0:T(8,128)(2,1)}) %all-gather.5.cloned.1.call-update) | async-done | bytes 4718608 | tf_op jit(solution)/shard_map/all_gather | solution.py:689
  171.8 4.0 assemble.4
  178.3 10.3 %multiply_convert_fusion.6 = (bf16[1024,1024]{1,0:T(8,128)(2,1)}, bf16[1024,1024]{1,0:T(8,128)(2,1)S(1)}, f32[1024,1024]{1,0:T(8,128)}) fusion(f32[1024]{0:T(1024)S(1)} %bitcast.180, f32[1024,1024]{1,0:T(8,128)S(1)} %fusion.129, bf16[1024,1024]{1,0:T(8,128)(2,1)S(1)} %get-tuple-element.120, bf16[512,1024]{1,0:T(8,128)(2,1)} %collective-permute-done.2, ...), kind=kOutput, calls=%fused_computation.48 | convolution fusion | flops 2172649472 | bytes 16781312 | tf_op jit(solution)/shard_map/dot_general | solution.py:37
  192.0 5.1 fusion.114.proj_ref
  197.1 7.9 %attend.4 = (bf16[1024,256]{1,0:T(8,128)(2,1)S(1)}, bf16[1024,768]{1,0:T(8,128)(2,1)S(1)}, f32[8,1024]{1,0:T(8,128)S(1)}) custom-call(s32[1]{0:T(128)} %bitcast.1.flip_ref, f32[1024,768]{1,0:T(8,128)} %fusion.114.proj_ref, f32[3,1024,128]{2,1,0:T(8,128)} %get-tuple-element.223.tab_ref, bf16[1024,256]{1,0:T(8,128)(2,1)S(1)} %copy-done.9, ...), custom_call_target="tpu_custom_call" | custom-call | flops 2147483648 | bytes 6291456 | tf_op jit(solution)/shard_map/attend/pallas_call | solution.py:200
  205.1 3.4 fusion.53
  219.6 22.8 %collective-permute-done.17 = bf16[512,1024]{1,0:T(8,128)(2,1)} collective-permute-done((bf16[512,1024]{1,0:T(8,128)(2,1)}, bf16[512,1024]{1,0:T(8,128)(2,1)}, u32[]{:S(2)}, u32[]{:S(2)}) %collective-permute-start.17) | collective-permute-done | bytes 1048608 | tf_op jit(solution)/shard_map/ppermute | solution.py:584
  252.4 29.0 %collective-permute-done.15 = bf16[1,256,1024]{2,1,0:T(8,128)(2,1)} collective-permute-done((bf16[1,256,1024]{2,1,0:T(8,128)(2,1)S(1)}, bf16[1,256,1024]{2,1,0:T(8,128)(2,1)}, u32[]{:S(2)}, u32[]{:S(2)}) %collective-permute-start.15) | collective-permute-done | bytes 524320 | tf_op jit(solution)/shard_map/ppermute | solution.py:619
  284.6 6.3 assemble.5
  290.8 7.2 collective-permute-start.20
  298.1 3.6 fusion.109
  301.7 5.6 fusion.110.proj_ref
  308.6 4.8 fusion.56
  313.5 3.5 fusion.130.proj_ref
  324.7 8.2 %attend.7 = (bf16[1024,256]{1,0:T(8,128)(2,1)S(1)}, bf16[1024,768]{1,0:T(8,128)(2,1)S(1)}, f32[8,1024]{1,0:T(8,128)S(1)}) custom-call(s32[1]{0:T(128)} %bitcast.1.flip_ref, f32[1024,768]{1,0:T(8,128)} %fusion.130.proj_ref, f32[3,1024,128]{2,1,0:T(8,128)} %get-tuple-element.224.tab_ref, bf16[1024,256]{1,0:T(8,128)(2,1)S(1)} %copy-done.6, ...), custom_call_target="tpu_custom_call" | custom-call | flops 2147483648 | bytes 6291456 | tf_op jit(solution)/shard_map/attend/pallas_call | solution.py:200
  337.8 7.8 %attend.6 = (bf16[1024,256]{1,0:T(8,128)(2,1)S(1)}, bf16[1024,768]{1,0:T(8,128)(2,1)S(1)}, f32[8,1024]{1,0:T(8,128)S(1)}) custom-call(s32[1]{0:T(128)} %bitcast.1.flip_ref, f32[1024,768]{1,0:T(8,128)} %fusion.110.proj_ref, f32[3,1024,128]{2,1,0:T(8,128)} %get-tuple-element.223.tab_ref, bf16[1024,256]{1,0:T(8,128)(2,1)S(1)} %copy-done.10, ...), custom_call_target="tpu_custom_call" | custom-call | flops 2147483648 | bytes 6291456 | tf_op jit(solution)/shard_map/attend/pallas_call | solution.py:200
  349.3 7.1 multiply_convert_fusion.5
  356.4 3.4 fusion.52
  359.8 3.8 fusion.108
  367.6 4.7 multiply_convert_fusion.4
  372.4 5.3 convolution_add_fusion.9.refs_2_
  381.8 5.7 disassemble.5
  397.4 12.6 %attend_back.4 = bf16[1024,768]{1,0:T(8,128)(2,1)S(1)} custom-call(s32[1]{0:T(128)} %bitcast.1.flip_ref, bf16[1024,768]{1,0:T(8,128)(2,1)} %copy-done.28, bf16[1024,256]{1,0:T(8,128)(2,1)S(1)} %convolution_convert_fusion.3.dctx_ref, f32[8,1024]{1,0:T(8,128)S(1)} %get-tuple-element.139.lse_ref, f32[3,1024,128]{2,1,0:T(8,128)} %get-tuple-element.224.tab_ref, ...), custom_call_target="tpu_custom_call" | custom-call | flops 5368709120 | bytes 6291456 | tf_op jit(solution)/shard_map/attend_back/pallas_call | solution.py:223
  426.0 12.9 %attend_back.5 = bf16[1024,768]{1,0:T(8,128)(2,1)S(1)} custom-call(s32[1]{0:T(128)} %bitcast.1.flip_ref, bf16[1024,768]{1,0:T(8,128)(2,1)} %copy-done.27, bf16[1024,256]{1,0:T(8,128)(2,1)S(1)} %convolution_convert_fusion.2.dctx_ref, f32[8,1024]{1,0:T(8,128)S(1)} %get-tuple-element.145.lse_ref, f32[3,1024,128]{2,1,0:T(8,128)} %get-tuple-element.223.tab_ref, ...), custom_call_target="tpu_custom_call" | custom-call | flops 5368709120 | bytes 6291456 | tf_op jit(solution)/shard_map/attend_back/pallas_call | solution.py:223
  438.9 8.6 %collective-permute-done.28 = bf16[512,1024]{1,0:T(8,128)(2,1)} collective-permute-done((bf16[512,1024]{1,0:T(8,128)(2,1)S(1)}, bf16[512,1024]{1,0:T(8,128)(2,1)}, u32[]{:S(2)}, u32[]{:S(2)}) %collective-permute-start.28) | collective-permute-done | bytes 1048608 | tf_op jit(solution)/shard_map/ppermute | solution.py:584
  472.6 13.5 %reduce-scatter.3.cloned.1.call-done = bf16[1,72,16,256]{3,2,1,0:T(8,128)(2,1)} async-done(((bf16[8,72,16,256]{3,2,1,0:T(8,128)(2,1)}), bf16[1,72,16,256]{3,2,1,0:T(8,128)(2,1)}) %reduce-scatter.3.cloned.1.call-update) | async-done | bytes 589840 | tf_op jit(solution)/shard_map/reduce_scatter | solution.py:912
  491.9 8.0 %multiply_convert_fusion.1 = bf16[1024,1024]{1,0:T(8,128)(2,1)} fusion(f32[1024,1024]{1,0:T(8,128)} %get-tuple-element.276, f32[1024]{0:T(1024)S(1)} %bitcast.181, bf16[1024,1024]{1,0:T(8,128)(2,1)S(1)} %copy-done.37, bf16[1280,1024]{1,0:T(8,128)(2,1)} %copy-done.11), kind=kOutput, calls=%fused_computation.43 | convolution fusion | flops 2170552320 | bytes 10489856 | tf_op jit(solution)/shard_map/dot_general | solution.py:41
  501.7 12.5 %attend_back.6 = bf16[1024,768]{1,0:T(8,128)(2,1)S(1)} custom-call(s32[1]{0:T(128)} %bitcast.1.flip_ref, bf16[1024,768]{1,0:T(8,128)(2,1)} %copy-done.26, bf16[1024,256]{1,0:T(8,128)(2,1)S(1)} %convolution_convert_fusion.1.dctx_ref, f32[8,1024]{1,0:T(8,128)S(1)} %get-tuple-element.157.lse_ref, f32[3,1024,128]{2,1,0:T(8,128)} %get-tuple-element.223.tab_ref, ...), custom_call_target="tpu_custom_call" | custom-call | flops 5368709120 | bytes 6291456 | tf_op jit(solution)/shard_map/attend_back/pallas_call | solution.py:223
  520.1 5.7 fusion.111
  525.8 5.9 fusion.112
  537.6 4.5 convolution_add_fusion.6.refs_1_
  547.1 6.6 multiply_convert_fusion
  553.7 4.5 convolution_add_fusion.5.refs_0_
  558.2 3.3 disassemble.8
  561.5 16.9 %collective-permute-done.35 = bf16[4,40,16,256]{3,2,1,0:T(8,128)(2,1)S(1)} collective-permute-done((bf16[4,40,16,256]{3,2,1,0:T(8,128)(2,1)S(1)}, bf16[4,40,16,256]{3,2,1,0:T(8,128)(2,1)S(1)}, u32[]{:S(2)}, u32[]{:S(2)}) %collective-permute-start.35) | collective-permute-done | bytes 1310752 | tf_op jit(solution)/shard_map/ppermute | solution.py:584
  579.9 9.2 %all-to-all-start.2 = ((bf16[4,40,16,256]{3,2,1,0:T(8,128)(2,1)}), bf16[4,40,16,256]{3,2,1,0:T(8,128)(2,1)}, u32[]{:S(2)}, u32[]{:S(2)}) async-start(bf16[4,40,16,256]{3,2,1,0:T(8,128)(2,1)} %add_convert_fusion), calls=%async_computation.3 | async-start | bytes 2621440 | tf_op jit(solution)/shard_map/all_to_all | solution.py:926
  589.1 6.8 fusion.137
  599.3 12.8 %attend_back.7 = bf16[1024,768]{1,0:T(8,128)(2,1)S(1)} custom-call(s32[1]{0:T(128)} %bitcast.1.flip_ref, bf16[1024,768]{1,0:T(8,128)(2,1)} %copy-done.25, bf16[1024,256]{1,0:T(8,128)(2,1)S(1)} %convolution_convert_fusion.dctx_ref, f32[8,1024]{1,0:T(8,128)S(1)} %get-tuple-element.174.lse_ref, f32[3,1024,128]{2,1,0:T(8,128)} %get-tuple-element.224.tab_ref, ...), custom_call_target="tpu_custom_call" | custom-call | flops 5368709120 | bytes 6291456 | tf_op jit(solution)/shard_map/attend_back/pallas_call | solution.py:223
  612.1 4.3 convolution_add_fusion.11.refs_0_
  624.1 4.8 all-to-all-start.3
  628.9 4.5 convolution_add_fusion.4
  637.6 15.8 %all-to-all-done.3 = bf16[4,32,16,256]{3,2,1,0:T(8,128)(2,1)S(1)} async-done(((bf16[4,32,16,256]{3,2,1,0:T(8,128)(2,1)}), bf16[4,32,16,256]{3,2,1,0:T(8,128)(2,1)S(1)}, u32[]{:S(2)}, u32[]{:S(2)}) %all-to-all-start.3) | async-done | bytes 1048608 | tf_op jit(solution)/shard_map/all_to_all | solution.py:926
  655.8 5.2 fusion.138
  663.4 3.7 all-to-all-start.4
  667.2 5.3 fusion.127
  672.6 6.2 collective-permute-done.38
  694.0 4.4 place.1
  698.4 4.5 all-to-all-start.5
  706.1 12.6 %collective-permute-done.42 = bf16[256,1024]{1,0:T(8,128)(2,1)S(1)} collective-permute-done((bf16[256,1024]{1,0:T(8,128)(2,1)S(1)}, bf16[256,1024]{1,0:T(8,128)(2,1)S(1)}, u32[]{:S(2)}, u32[]{:S(2)}) %collective-permute-start.42) | collective-permute-done | bytes 524320 | tf_op jit(solution)/shard_map/ppermute | solution.py:634
  718.8 11.7 %all-to-all-done.5.from_ref = bf16[8,528,256]{2,1,0:T(8,128)(2,1)} async-done(((bf16[8,528,256]{2,1,0:T(8,128)(2,1)}), bf16[8,528,256]{2,1,0:T(8,128)(2,1)}, u32[]{:S(2)}, u32[]{:S(2)}) %all-to-all-start.5) | async-done | bytes 2162720 | tf_op jit(solution)/shard_map/all_to_all | solution.py:1069
  732.0 4.3 all-to-all-start.6
  737.3 14.0 %adam.1 = (f32[32,32768]{1,0:T(8,128)}, f32[32,32768]{1,0:T(8,128)}, f32[32,32768]{1,0:T(8,128)}, bf16[32,32768]{1,0:T(8,128)(2,1)}) custom-call(bf16[8,528,256]{2,1,0:T(8,128)(2,1)} %all-to-all-done.5.from_ref, f32[32,32768]{1,0:T(8,128)} %w_ref.1, f32[32,32768]{1,0:T(8,128)} %one_ref.1, f32[32,32768]{1,0:T(8,128)} %two_ref.1), custom_call_target="tpu_custom_call" | custom-call | flops 20971520 | bytes 29360128 | tf_op jit(solution)/shard_map/adam/pallas_call | solution.py:500
  (496 shorter events, 215.1 us)
Async XLA Ops:
  12.5 32.1 %all-to-all-start = ((bf16[8,512,256]{2,1,0:T(8,128)(2,1)}), bf16[8,512,256]{2,1,0:T(8,128)(2,1)}, u32[]{:S(2)}, u32[]{:S(2)}) async-start(bf16[8,512,256]{2,1,0:T(8,128)(2,1)} %pack.1), calls=%async_computation | async-start | bytes 4194304 | tf_op jit(solution)/shard_map/all_to_all | solution.py:672
  23.0 4.7 collective-permute-start
  23.7 14.2 %collective-permute-start.1 = (bf16[1,256,1024]{2,1,0:T(8,128)(2,1)S(1)}, bf16[1,256,1024]{2,1,0:T(8,128)(2,1)S(1)}, u32[]{:S(2)}, u32[]{:S(2)}) collective-permute-start(bf16[1,256,1024]{2,1,0:T(8,128)(2,1)S(1)} %get-tuple-element.243), channel_id=1, source_target_pairs={{0,1},{16,17},{1,0},{17,16},{2,5},{18,21},{3,4},{19,20},{4,3},{20,... | collective-permute-start | bytes 1572872 | tf_op jit(solution)/shard_map/ppermute | solution.py:619
  38.1 46.8 %copy-start.32 = (bf16[512,1024]{1,0:T(8,128)(2,1)}, bf16[512,1024]{1,0:T(8,128)(2,1)S(1)}, u32[]{:S(2)}) copy-start(bf16[512,1024]{1,0:T(8,128)(2,1)S(1)} %maximum_bitcast_fusion) | copy-start | bytes 3145732
  46.6 20.2 %all-to-all-start.1 = ((bf16[32,2,256]{2,1,0:T(2,128)(2,1)}), bf16[32,2,256]{2,1,0:T(2,128)(2,1)S(1)}, u32[]{:S(2)}, u32[]{:S(2)}) async-start(bf16[32,2,256]{2,1,0:T(2,128)(2,1)} %reshape.298), calls=%async_computation.1 | async-start | bytes 65536 | tf_op jit(solution)/shard_map/all_to_all | solution.py:594
  59.5 112.3 %all-gather.5.cloned.1.call-start = ((), (), s32[]{:S(2)}) async-start(), calls=%async_computation.11 | async-start | bytes 5308416 | tf_op jit(solution)/shard_map/all_gather | solution.py:689
  68.1 2.0 collective-permute-start.8
  68.1 7.1 collective-permute-start.9
  68.8 9.0 %collective-permute-start.10 = (bf16[20,16,256]{2,1,0:T(8,128)(2,1)S(1)}, bf16[20,16,256]{2,1,0:T(8,128)(2,1)S(1)}, u32[]{:S(2)}, u32[]{:S(2)}) collective-permute-start(bf16[20,16,256]{2,1,0:T(8,128)(2,1)S(1)} %get-tuple-element.252), channel_id=1, source_target_pairs={{0,12},{4,8},{8,4},{12,0},{16,28},{20,24},{24,20},{28,16},{1,13},{... | collective-permute-start | bytes 491528 | tf_op jit(solution)/shard_map/ppermute | solution.py:584
  79.5 205.1 %all-gather.7.cloned.1.call-start = ((), (), s32[]{:S(2)}) async-start(), calls=%async_computation.12 | async-start | bytes 7077888 | tf_op jit(solution)/shard_map/all_gather | solution.py:689
  80.6 32.1 %collective-permute-start.5 = (bf16[24,16,256]{2,1,0:T(8,128)(2,1)S(1)}, bf16[24,16,256]{2,1,0:T(8,128)(2,1)S(1)}, u32[]{:S(2)}, u32[]{:S(2)}) collective-permute-start(bf16[24,16,256]{2,1,0:T(8,128)(2,1)S(1)} %copy-done.13), channel_id=1, source_target_pairs={{0,3},{1,0},{2,1},{3,2},{4,7},{5,4},{6,5},{7,6},{8,11},{9,8},{10,9... | collective-permute-start | bytes 589832 | tf_op jit(solution)/shard_map/ppermute | solution.py:744
  81.2 32.0 %collective-permute-start.3 = (bf16[24,16,256]{2,1,0:T(8,128)(2,1)S(1)}, bf16[24,16,256]{2,1,0:T(8,128)(2,1)S(1)}, u32[]{:S(2)}, u32[]{:S(2)}) collective-permute-start(bf16[24,16,256]{2,1,0:T(8,128)(2,1)S(1)} %copy-done.13), channel_id=1, source_target_pairs={{0,1},{1,2},{2,3},{3,0},{4,5},{5,6},{6,7},{7,4},{8,9},{9,10},{10,1... | collective-permute-start | bytes 589832 | tf_op jit(solution)/shard_map/ppermute | solution.py:744
  82.7 30.8 %collective-permute-start.4 = (bf16[24,16,256]{2,1,0:T(8,128)(2,1)S(1)}, bf16[24,16,256]{2,1,0:T(8,128)(2,1)S(1)}, u32[]{:S(2)}, u32[]{:S(2)}) collective-permute-start(bf16[24,16,256]{2,1,0:T(8,128)(2,1)S(1)} %copy-done.13), channel_id=1, source_target_pairs={{0,2},{1,3},{2,0},{3,1},{4,6},{5,7},{6,4},{7,5},{8,10},{9,11},{10,... | collective-permute-start | bytes 589832 | tf_op jit(solution)/shard_map/ppermute | solution.py:744
  83.2 34.6 %collective-permute-start.6 = (bf16[24,16,256]{2,1,0:T(8,128)(2,1)S(1)}, bf16[24,16,256]{2,1,0:T(8,128)(2,1)S(1)}, u32[]{:S(2)}, u32[]{:S(2)}) collective-permute-start(bf16[24,16,256]{2,1,0:T(8,128)(2,1)S(1)} %copy-done.13), channel_id=1, source_target_pairs={{0,16},{4,20},{8,24},{12,28},{16,0},{20,4},{24,8},{28,12},{1,17},{... | collective-permute-start | bytes 589832 | tf_op jit(solution)/shard_map/ppermute | solution.py:584
  86.3 24.5 %collective-permute-start.11 = (bf16[512,1024]{1,0:T(8,128)(2,1)}, bf16[512,1024]{1,0:T(8,128)(2,1)}, u32[]{:S(2)}, u32[]{:S(2)}) collective-permute-start(bf16[512,1024]{1,0:T(8,128)(2,1)} %fusion.35), channel_id=1, source_target_pairs={{0,8},{4,12},{8,0},{12,4},{16,24},{20,28},{24,16},{28,20},{1,9},{5... | collective-permute-start | bytes 3145736 | tf_op jit(solution)/shard_map/ppermute | solution.py:584
  88.2 397.9 %reduce-scatter.3.cloned.1.call-start = ((), (), s32[]{:S(2)}) async-start(), calls=%async_computation.9 | async-start | bytes 5308416 | tf_op jit(solution)/shard_map/reduce_scatter | solution.py:912
  110.9 28.5 %collective-permute-start.12 = (bf16[512,1024]{1,0:T(8,128)(2,1)}, bf16[512,1024]{1,0:T(8,128)(2,1)}, u32[]{:S(2)}, u32[]{:S(2)}) collective-permute-start(bf16[512,1024]{1,0:T(8,128)(2,1)} %collective-permute-done.11), channel_id=1, source_target_pairs={{0,4},{4,0},{8,12},{12,8},{16,20},{20,16},{24,28},{28,24},{1,5},{5... | collective-permute-start | bytes 3145736 | tf_op jit(solution)/shard_map/ppermute | solution.py:584
  112.7 65.5 %collective-permute-start.2 = (bf16[512,1024]{1,0:T(8,128)(2,1)}, bf16[512,1024]{1,0:T(8,128)(2,1)}, u32[]{:S(2)}, u32[]{:S(2)}) collective-permute-start(bf16[512,1024]{1,0:T(8,128)(2,1)} %fusion.35), channel_id=1, source_target_pairs={{0,4},{4,0},{8,12},{12,8},{16,20},{20,16},{24,28},{28,24},{1,5},{5... | collective-permute-start | bytes 3145736 | tf_op jit(solution)/shard_map/ppermute | solution.py:584
  114.4 20.1 %collective-permute-start.7 = (bf16[3,24,16,256]{3,2,1,0:T(8,128)(2,1)}, bf16[3,24,16,256]{3,2,1,0:T(8,128)(2,1)S(1)}, u32[]{:S(2)}, u32[]{:S(2)}) collective-permute-start(bf16[3,24,16,256]{3,2,1,0:T(8,128)(2,1)} %pad_maximum_fusion.8), channel_id=1, source_target_pairs={{0,16},{4,20},{8,24},{12,28},{16,0},{20,4},{24,8},{28,12},{1,17},{... | collective-permute-start | bytes 1769480 | tf_op jit(solution)/shard_map/ppermute | solution.py:584
  117.7 60.5 %copy-start.92 = (f32[4,1,256]{2,1,0:T(1,128)}, f32[4,1,256]{2,1,0:T(1,128)S(1)}, u32[]{:S(2)}) copy-start(f32[4,1,256]{2,1,0:T(1,128)S(1)} %fusion.95) | copy-start | bytes 12292
  137.5 54.5 %copy-start.4 = (bf16[1024,768]{1,0:T(8,128)(2,1)}, bf16[1024,768]{1,0:T(8,128)(2,1)S(1)}, u32[]{:S(2)}) copy-start(bf16[1024,768]{1,0:T(8,128)(2,1)S(1)} %assemble.3) | copy-start | bytes 4718596
  153.1 37.8 %copy-start = (bf16[1024,256]{1,0:T(8,128)(2,1)}, bf16[1024,256]{1,0:T(8,128)(2,1)S(1)}, u32[]{:S(2)}) copy-start(bf16[1024,256]{1,0:T(8,128)(2,1)S(1)} %get-tuple-element.119) | copy-start | bytes 1572868
  175.9 34.9 %copy-start.11 = (bf16[1280,1024]{1,0:T(8,128)(2,1)}, bf16[1280,1024]{1,0:T(8,128)(2,1)S(1)}, u32[]{:S(2)}) copy-start(bf16[1280,1024]{1,0:T(8,128)(2,1)S(1)} %get-tuple-element.118) | copy-start | bytes 7864324
  191.9 13.2 %collective-permute-start.13 = (bf16[512,1024]{1,0:T(8,128)(2,1)S(1)}, bf16[512,1024]{1,0:T(8,128)(2,1)}, u32[]{:S(2)}, u32[]{:S(2)}) collective-permute-start(bf16[512,1024]{1,0:T(8,128)(2,1)S(1)} %slice.354), channel_id=1, source_target_pairs={{0,4},{4,0},{8,12},{12,8},{16,20},{20,16},{24,28},{28,24},{1,5},{5... | collective-permute-start | bytes 3145736 | tf_op jit(solution)/shard_map/ppermute | solution.py:584
  213.5 28.8 %copy-start.33 = (bf16[512,1024]{1,0:T(8,128)(2,1)S(1)}, bf16[512,1024]{1,0:T(8,128)(2,1)}, u32[]{:S(2)}) copy-start(bf16[512,1024]{1,0:T(8,128)(2,1)} %copy-done.32) | copy-start | bytes 3145732
  216.4 3.2 collective-permute-start.16
  217.0 25.4 %collective-permute-start.17 = (bf16[512,1024]{1,0:T(8,128)(2,1)}, bf16[512,1024]{1,0:T(8,128)(2,1)}, u32[]{:S(2)}, u32[]{:S(2)}) collective-permute-start(bf16[512,1024]{1,0:T(8,128)(2,1)} %fusion.53), channel_id=1, source_target_pairs={{0,8},{4,12},{8,0},{12,4},{16,24},{20,28},{24,16},{28,20},{1,9},{5... | collective-permute-start | bytes 3145736 | tf_op jit(solution)/shard_map/ppermute | solution.py:584
  246.6 55.0 %copy-start.59 = (bf16[512,1024]{1,0:T(8,128)(2,1)}, bf16[512,1024]{1,0:T(8,128)(2,1)S(1)}, u32[]{:S(2)}) copy-start(bf16[512,1024]{1,0:T(8,128)(2,1)S(1)} %add_convert_fusion.2) | copy-start | bytes 3145732
  246.6 51.4 %collective-permute-start.18 = (bf16[512,1024]{1,0:T(8,128)(2,1)S(1)}, bf16[512,1024]{1,0:T(8,128)(2,1)}, u32[]{:S(2)}, u32[]{:S(2)}) collective-permute-start(bf16[512,1024]{1,0:T(8,128)(2,1)S(1)} %add_convert_fusion.2), channel_id=1, source_target_pairs={{0,4},{4,0},{8,12},{12,8},{16,20},{20,16},{24,28},{28,24},{1,5},{5... | collective-permute-start | bytes 3145736 | tf_op jit(solution)/shard_map/ppermute | solution.py:584
  246.6 44.2 %collective-permute-start.19 = (bf16[512,1024]{1,0:T(8,128)(2,1)S(1)}, bf16[512,1024]{1,0:T(8,128)(2,1)}, u32[]{:S(2)}, u32[]{:S(2)}) collective-permute-start(bf16[512,1024]{1,0:T(8,128)(2,1)S(1)} %add_convert_fusion.2), channel_id=1, source_target_pairs={{0,8},{4,12},{8,0},{12,4},{16,24},{20,28},{24,16},{28,20},{1,9},{5... | collective-permute-start | bytes 3145736 | tf_op jit(solution)/shard_map/ppermute | solution.py:584
  248.2 3.5 collective-permute-start.14
  249.8 31.5 %collective-permute-start.15 = (bf16[1,256,1024]{2,1,0:T(8,128)(2,1)S(1)}, bf16[1,256,1024]{2,1,0:T(8,128)(2,1)}, u32[]{:S(2)}, u32[]{:S(2)}) collective-permute-start(bf16[1,256,1024]{2,1,0:T(8,128)(2,1)S(1)} %get-tuple-element.235), channel_id=1, source_target_pairs={{0,1},{16,17},{1,0},{17,16},{2,5},{18,21},{3,4},{19,20},{4,3},{20,... | collective-permute-start | bytes 1572872 | tf_op jit(solution)/shard_map/ppermute | solution.py:619
  290.8 22.5 %collective-permute-start.20 = (bf16[512,1024]{1,0:T(8,128)(2,1)}, bf16[512,1024]{1,0:T(8,128)(2,1)S(1)}, u32[]{:S(2)}, u32[]{:S(2)}) collective-permute-start(bf16[512,1024]{1,0:T(8,128)(2,1)} %collective-permute-done.19), channel_id=1, source_target_pairs={{0,4},{4,0},{8,12},{12,8},{16,20},{20,16},{24,28},{28,24},{1,5},{5... | collective-permute-start | bytes 3145736 | tf_op jit(solution)/shard_map/ppermute | solution.py:584
  319.3 28.7 %collective-permute-start.21 = (bf16[512,1024]{1,0:T(8,128)(2,1)}, bf16[512,1024]{1,0:T(8,128)(2,1)}, u32[]{:S(2)}, u32[]{:S(2)}) collective-permute-start(bf16[512,1024]{1,0:T(8,128)(2,1)} %maximum_bitcast_fusion.1), channel_id=1, source_target_pairs={{0,4},{4,0},{8,12},{12,8},{16,20},{20,16},{24,28},{28,24},{1,5},{5... | collective-permute-start | bytes 3145736 | tf_op jit(solution)/shard_map/ppermute | solution.py:584
  320.2 25.5 %collective-permute-start.22 = (bf16[512,1024]{1,0:T(8,128)(2,1)}, bf16[512,1024]{1,0:T(8,128)(2,1)}, u32[]{:S(2)}, u32[]{:S(2)}) collective-permute-start(bf16[512,1024]{1,0:T(8,128)(2,1)} %maximum_bitcast_fusion.1), channel_id=1, source_target_pairs={{0,8},{4,12},{8,0},{12,4},{16,24},{20,28},{24,16},{28,20},{1,9},{5... | collective-permute-start | bytes 3145736 | tf_op jit(solution)/shard_map/ppermute | solution.py:584
  336.2 20.2 %collective-permute-start.24 = (bf16[512,1024]{1,0:T(8,128)(2,1)}, bf16[512,1024]{1,0:T(8,128)(2,1)}, u32[]{:S(2)}, u32[]{:S(2)}) collective-permute-start(bf16[512,1024]{1,0:T(8,128)(2,1)} %slice.352), channel_id=1, source_target_pairs={{0,4},{4,0},{8,12},{12,8},{16,20},{20,16},{24,28},{28,24},{1,5},{5... | collective-permute-start | bytes 3145736 | tf_op jit(solution)/shard_map/ppermute | solution.py:584
  345.6 21.9 %collective-permute-start.23 = (bf16[512,1024]{1,0:T(8,128)(2,1)}, bf16[512,1024]{1,0:T(8,128)(2,1)S(1)}, u32[]{:S(2)}, u32[]{:S(2)}) collective-permute-start(bf16[512,1024]{1,0:T(8,128)(2,1)} %collective-permute-done.22), channel_id=1, source_target_pairs={{0,4},{4,0},{8,12},{12,8},{16,20},{20,16},{24,28},{28,24},{1,5},{5... | collective-permute-start | bytes 3145736 | tf_op jit(solution)/shard_map/ppermute | solution.py:584
  387.5 25.6 %collective-permute-start.25 = (bf16[512,1024]{1,0:T(8,128)(2,1)}, bf16[512,1024]{1,0:T(8,128)(2,1)}, u32[]{:S(2)}, u32[]{:S(2)}) collective-permute-start(bf16[512,1024]{1,0:T(8,128)(2,1)} %fusion.52), channel_id=1, source_target_pairs={{0,8},{4,12},{8,0},{12,4},{16,24},{20,28},{24,16},{28,20},{1,9},{5... | collective-permute-start | bytes 3145736 | tf_op jit(solution)/shard_map/ppermute | solution.py:584
  388.8 235.3 %reduce-scatter.5.cloned.1.call-start = ((), (), s32[]{:S(2)}) async-start(), calls=%async_computation.10 | async-start | bytes 1769472 | tf_op jit(solution)/shard_map/reduce_scatter | solution.py:912
  393.6 24.2 %collective-permute-start.27 = (bf16[512,1024]{1,0:T(8,128)(2,1)}, bf16[512,1024]{1,0:T(8,128)(2,1)S(1)}, u32[]{:S(2)}, u32[]{:S(2)}) collective-permute-start(bf16[512,1024]{1,0:T(8,128)(2,1)} %slice.350), channel_id=1, source_target_pairs={{0,4},{4,0},{8,12},{12,8},{16,20},{20,16},{24,28},{28,24},{1,5},{5... | collective-permute-start | bytes 3145736 | tf_op jit(solution)/shard_map/ppermute | solution.py:584
  417.7 4.5 collective-permute-start.26
  422.5 25.0 %collective-permute-start.28 = (bf16[512,1024]{1,0:T(8,128)(2,1)S(1)}, bf16[512,1024]{1,0:T(8,128)(2,1)}, u32[]{:S(2)}, u32[]{:S(2)}) collective-permute-start(bf16[512,1024]{1,0:T(8,128)(2,1)S(1)} %fusion.51), channel_id=1, source_target_pairs={{0,8},{4,12},{8,0},{12,4},{16,24},{20,28},{24,16},{28,20},{1,9},{5... | collective-permute-start | bytes 3145736 | tf_op jit(solution)/shard_map/ppermute | solution.py:584
  451.9 2.7 collective-permute-start.29
  460.1 9.4 %collective-permute-start.30 = (bf16[512,1024]{1,0:T(8,128)(2,1)}, bf16[512,1024]{1,0:T(8,128)(2,1)}, u32[]{:S(2)}, u32[]{:S(2)}) collective-permute-start(bf16[512,1024]{1,0:T(8,128)(2,1)} %get-tuple-element.150), channel_id=1, source_target_pairs={{0,4},{4,0},{8,12},{12,8},{16,20},{20,16},{24,28},{28,24},{1,5},{5... | collective-permute-start | bytes 3145736 | tf_op jit(solution)/shard_map/ppermute | solution.py:584
  460.3 56.4 %collective-permute-start.31 = (bf16[512,1024]{1,0:T(8,128)(2,1)}, bf16[512,1024]{1,0:T(8,128)(2,1)}, u32[]{:S(2)}, u32[]{:S(2)}) collective-permute-start(bf16[512,1024]{1,0:T(8,128)(2,1)} %get-tuple-element.150), channel_id=1, source_target_pairs={{0,8},{4,12},{8,0},{12,4},{16,24},{20,28},{24,16},{28,20},{1,9},{5... | collective-permute-start | bytes 3145736 | tf_op jit(solution)/shard_map/ppermute | solution.py:584
  488.5 25.7 %collective-permute-start.32 = (bf16[256,1024]{1,0:T(8,128)(2,1)}, bf16[256,1024]{1,0:T(8,128)(2,1)S(1)}, u32[]{:S(2)}, u32[]{:S(2)}) collective-permute-start(bf16[256,1024]{1,0:T(8,128)(2,1)} %get-tuple-element.232), channel_id=1, source_target_pairs={{0,0},{16,16},{1,1},{17,17},{4,2},{20,18},{5,3},{21,19},{2,4},{18,... | collective-permute-start | bytes 1572872 | tf_op jit(solution)/shard_map/ppermute | solution.py:634
  490.2 24.0 %collective-permute-start.33 = (bf16[256,1024]{1,0:T(8,128)(2,1)}, bf16[256,1024]{1,0:T(8,128)(2,1)}, u32[]{:S(2)}, u32[]{:S(2)}) collective-permute-start(bf16[256,1024]{1,0:T(8,128)(2,1)} %get-tuple-element.231), channel_id=1, source_target_pairs={{1,0},{17,16},{0,1},{16,17},{5,2},{21,18},{4,3},{20,19},{3,4},{19,... | collective-permute-start | bytes 1572872 | tf_op jit(solution)/shard_map/ppermute | solution.py:634
  516.8 15.0 %collective-permute-start.34 = (bf16[512,1024]{1,0:T(8,128)(2,1)}, bf16[512,1024]{1,0:T(8,128)(2,1)S(1)}, u32[]{:S(2)}, u32[]{:S(2)}) collective-permute-start(bf16[512,1024]{1,0:T(8,128)(2,1)} %collective-permute-done.31), channel_id=1, source_target_pairs={{0,4},{4,0},{8,12},{12,8},{16,20},{20,16},{24,28},{28,24},{1,5},{5... | collective-permute-start | bytes 3145736 | tf_op jit(solution)/shard_map/ppermute | solution.py:584
  545.6 32.8 %collective-permute-start.35 = (bf16[4,40,16,256]{3,2,1,0:T(8,128)(2,1)S(1)}, bf16[4,40,16,256]{3,2,1,0:T(8,128)(2,1)S(1)}, u32[]{:S(2)}, u32[]{:S(2)}) collective-permute-start(bf16[4,40,16,256]{3,2,1,0:T(8,128)(2,1)S(1)} %get-tuple-element.172), channel_id=1, source_target_pairs={{0,16},{4,20},{8,24},{12,28},{16,0},{20,4},{24,8},{28,12},{1,17},{... | collective-permute-start | bytes 3932168 | tf_op jit(solution)/shard_map/ppermute | solution.py:584
  579.9 41.7 %all-to-all-start.2 = ((bf16[4,40,16,256]{3,2,1,0:T(8,128)(2,1)}), bf16[4,40,16,256]{3,2,1,0:T(8,128)(2,1)}, u32[]{:S(2)}, u32[]{:S(2)}) async-start(bf16[4,40,16,256]{3,2,1,0:T(8,128)(2,1)} %add_convert_fusion), calls=%async_computation.3 | async-start | bytes 2621440 | tf_op jit(solution)/shard_map/all_to_all | solution.py:926
  595.9 24.5 %collective-permute-start.36 = (bf16[4,32,16,256]{3,2,1,0:T(8,128)(2,1)S(1)}, bf16[4,32,16,256]{3,2,1,0:T(8,128)(2,1)S(1)}, u32[]{:S(2)}, u32[]{:S(2)}) collective-permute-start(bf16[4,32,16,256]{3,2,1,0:T(8,128)(2,1)S(1)} %get-tuple-element.178), channel_id=1, source_target_pairs={{0,16},{4,20},{8,24},{12,28},{16,0},{20,4},{24,8},{28,12},{1,17},{... | collective-permute-start | bytes 3145736 | tf_op jit(solution)/shard_map/ppermute | solution.py:584
  624.1 29.3 %all-to-all-start.3 = ((bf16[4,32,16,256]{3,2,1,0:T(8,128)(2,1)}), bf16[4,32,16,256]{3,2,1,0:T(8,128)(2,1)S(1)}, u32[]{:S(2)}, u32[]{:S(2)}) async-start(bf16[4,32,16,256]{3,2,1,0:T(8,128)(2,1)} %add_convert_fusion.1), calls=%async_computation.5 | async-start | bytes 2097152 | tf_op jit(solution)/shard_map/all_to_all | solution.py:926
  633.5 2.7 collective-permute-start.37
  633.6 27.4 %collective-permute-start.40 = (bf16[4,24,16,256]{3,2,1,0:T(8,128)(2,1)}, bf16[4,24,16,256]{3,2,1,0:T(8,128)(2,1)}, u32[]{:S(2)}, u32[]{:S(2)}) collective-permute-start(bf16[4,24,16,256]{3,2,1,0:T(8,128)(2,1)} %get-tuple-element.189), channel_id=1, source_target_pairs={{0,16},{4,20},{8,24},{12,28},{16,0},{20,4},{24,8},{28,12},{1,17},{... | collective-permute-start | bytes 2359304 | tf_op jit(solution)/shard_map/ppermute | solution.py:584
  654.3 24.4 %collective-permute-start.38 = (bf16[512,1024]{1,0:T(8,128)(2,1)}, bf16[512,1024]{1,0:T(8,128)(2,1)}, u32[]{:S(2)}, u32[]{:S(2)}) collective-permute-start(bf16[512,1024]{1,0:T(8,128)(2,1)} %fusion.45), channel_id=1, source_target_pairs={{0,8},{4,12},{8,0},{12,4},{16,24},{20,28},{24,16},{28,20},{1,9},{5... | collective-permute-start | bytes 3145736 | tf_op jit(solution)/shard_map/ppermute | solution.py:584
  663.4 23.8 %all-to-all-start.4 = ((bf16[4,24,16,256]{3,2,1,0:T(8,128)(2,1)}), bf16[4,24,16,256]{3,2,1,0:T(8,128)(2,1)S(1)}, u32[]{:S(2)}, u32[]{:S(2)}) async-start(bf16[4,24,16,256]{3,2,1,0:T(8,128)(2,1)} %add_convert_fusion.3), calls=%async_computation.6 | async-start | bytes 1572864 | tf_op jit(solution)/shard_map/all_to_all | solution.py:926
  679.9 8.2 %collective-permute-start.39 = (bf16[512,1024]{1,0:T(8,128)(2,1)}, bf16[512,1024]{1,0:T(8,128)(2,1)}, u32[]{:S(2)}, u32[]{:S(2)}) collective-permute-start(bf16[512,1024]{1,0:T(8,128)(2,1)} %slice.347), channel_id=1, source_target_pairs={{0,4},{4,0},{8,12},{12,8},{16,20},{20,16},{24,28},{28,24},{1,5},{5... | collective-permute-start | bytes 3145736 | tf_op jit(solution)/shard_map/ppermute | solution.py:584
  684.3 8.9 %collective-permute-start.43 = (bf16[20,16,256]{2,1,0:T(8,128)(2,1)}, bf16[20,16,256]{2,1,0:T(8,128)(2,1)S(1)}, u32[]{:S(2)}, u32[]{:S(2)}) collective-permute-start(bf16[20,16,256]{2,1,0:T(8,128)(2,1)} %get-tuple-element.247), channel_id=1, source_target_pairs={{0,4},{4,0},{8,12},{12,8},{16,20},{20,16},{24,28},{28,24},{1,5},{5... | collective-permute-start | bytes 491528 | tf_op jit(solution)/shard_map/ppermute | solution.py:584
  684.9 8.4 %collective-permute-start.44 = (bf16[20,16,256]{2,1,0:T(8,128)(2,1)}, bf16[20,16,256]{2,1,0:T(8,128)(2,1)S(1)}, u32[]{:S(2)}, u32[]{:S(2)}) collective-permute-start(bf16[20,16,256]{2,1,0:T(8,128)(2,1)} %get-tuple-element.248), channel_id=1, source_target_pairs={{0,8},{4,12},{8,0},{12,4},{16,24},{20,28},{24,16},{28,20},{1,9},{5... | collective-permute-start | bytes 491528 | tf_op jit(solution)/shard_map/ppermute | solution.py:584
  686.4 7.5 collective-permute-start.45
  698.4 32.1 %all-to-all-start.5 = ((bf16[8,528,256]{2,1,0:T(8,128)(2,1)}), bf16[8,528,256]{2,1,0:T(8,128)(2,1)}, u32[]{:S(2)}, u32[]{:S(2)}) async-start(bf16[8,528,256]{2,1,0:T(8,128)(2,1)} %place.1), calls=%async_computation.7 | async-start | bytes 4325376 | tf_op jit(solution)/shard_map/all_to_all | solution.py:1069
  705.4 0.8 collective-permute-start.41
  706.1 12.6 %collective-permute-start.42 = (bf16[256,1024]{1,0:T(8,128)(2,1)S(1)}, bf16[256,1024]{1,0:T(8,128)(2,1)S(1)}, u32[]{:S(2)}, u32[]{:S(2)}) collective-permute-start(bf16[256,1024]{1,0:T(8,128)(2,1)S(1)} %get-tuple-element.227), channel_id=1, source_target_pairs={{1,0},{17,16},{0,1},{16,17},{5,2},{21,18},{4,3},{20,19},{3,4},{19,... | collective-permute-start | bytes 1572872 | tf_op jit(solution)/shard_map/ppermute | solution.py:634
  732.0 19.3 %all-to-all-start.6 = ((f32[4,1,512]{2,1,0:T(1,128)}), f32[4,1,512]{2,1,0:T(1,128)S(1)}, u32[]{:S(2)}, u32[]{:S(2)}) async-start(f32[4,1,512]{2,1,0:T(1,128)} %all_to_all.34), calls=%async_computation.8 | async-start | bytes 16384 | tf_op jit(solution)/shard_map/all_to_all | solution.py:1072
  (102 other events, 611.0 us)
Sparse Core Ops, SparseCore 0:
  79.6 92.1 all-gather.4
  173.9 109.4 all-gather.6
  388.9 97.1 reduce-scatter.2
  501.8 69.3 reduce-scatter.4

commit v5 on v4

--- a/solution.py
+++ b/solution.py
@@ -479,10 +479,10 @@
                     place, :, side * 128 : side * 128 + 128
                 ].astype(F32)
 
-    for c in range(8):
+    for c in range(4):
         for lane in range(8):
             at = slice(c * 1024 + lane * 128, c * 1024 + lane * 128 + 128)
-            row = ((part // 2) * TP + lane // 2) * slots * 16 + (part % 2) * 8 + c
+            row = ((part // 4) * TP + lane // 2) * slots * 16 + (part % 4) * 4 + c
             grads = flat[lane % 2, pl.ds(row, slots, 16)]
             new, one, two = adam_update(
                 w_ref[:, at], grads, one_ref[:, at], two_ref[:, at], learn_rate, decay_rate
@@ -495,11 +495,11 @@
 
 def adam(received, masters, first_moment, second_moment):
     slots, piece = masters.shape
-    block = pl.BlockSpec((16, piece // 4), lambda i, j: (i, j))
+    block = pl.BlockSpec((16, piece // 8), lambda i, j: (i, j))
     whole = jax.ShapeDtypeStruct(masters.shape, F32)
     return pl.pallas_call(
         adam_kernel,
-        grid=(slots // 16, 4),
+        grid=(slots // 16, 8),
         in_specs=[pl.BlockSpec((8, 256, 256), lambda i, j: (0, i, 0))] + [block] * 3,
         out_specs=[block] * 4,
         out_shape=[whole, whole, whole, jax.ShapeDtypeStruct(masters.shape, BF)],

time: 768 us -> 772 us (level)
  no operation moved by 1% of the time
where the time goes in v5:
time: 772 us; the launch traced here: 762 us
  waiting for transfers between devices  230 us (30%)
  matrix products  171 us (22%)
  Pallas kernels  140 us (18%)
  starting transfers between devices  90.6 us (12%)
  other arithmetic  65.3 us (8%)
  local copies, waits for them, and re-layouts  43.6 us (6%)
  between operations  21.5 us (3%)
    ppermute x35, waiting for transfers between devices, swap(): return lax.ppermute(value, DP, [(i, i ^ bit) for i in range(n_dp)])  108 us
    dot_general x16, matrix products, dot_nt(): lax.dot_general(left, right, (((1,), (1,)), ((), ())), preferred_element_...  63.9 us
    dot_general x16, matrix products, dot(): return jnp.dot(left, right, preferred_element_type=F32)  57.2 us
    pallas_call x4, Pallas kernels, attend_back(): pl.pallas_call(functools.partial(attend_back_kernel, half), in_specs=[pl....  50.8 us
    dot_general x16, matrix products, dot_tn(): lax.dot_general(left, right, (((0,), (0,)), ((), ())), preferred_element_...  50.1 us
    ppermute x4, waiting for transfers between devices, to_rows(): parts.append(lax.ppermute(send, ALL, row_pairs(pairs, False)))  39.2 us
    ppermute x35, starting transfers between devices, swap(): return lax.ppermute(value, DP, [(i, i ^ bit) for i in range(n_dp)])  32.3 us
    pallas_call x4, Pallas kernels, attend(): pl.pallas_call(functools.partial(attend_kernel, half), in_specs=[pl.Block...  31.6 us
  transfers between devices with their start and end apart: 57, of which 25 were waited for; matrix products, arithmetic and copies ran while one was open for 32% of the time, Pallas kernels for 16%

profile of v5, /device:TPU:0, one launch (start us, length us, event | category | flops | bytes accessed | tf_op | source)
XLA Modules:
  0.0 762.5 jit_solution(14900651835442840599)
XLA Ops:
  7.2 5.3 pack.1
  12.5 5.3 all-to-all-start
  27.7 10.2 %collective-permute-done.1 = bf16[1,256,1024]{2,1,0:T(8,128)(2,1)S(1)} collective-permute-done((bf16[1,256,1024]{2,1,0:T(8,128)(2,1)S(1)}, bf16[1,256,1024]{2,1,0:T(8,128)(2,1)S(1)}, u32[]{:S(2)}, u32[]{:S(2)}) %collective-permute-start.1) | collective-permute-done | bytes 524320 | tf_op jit(solution)/shard_map/ppermute | solution.py:619
  38.1 6.4 all-to-all-done
  46.6 12.9 %all-to-all-start.1 = ((bf16[32,2,256]{2,1,0:T(2,128)(2,1)}), bf16[32,2,256]{2,1,0:T(2,128)(2,1)S(1)}, u32[]{:S(2)}, u32[]{:S(2)}) async-start(bf16[32,2,256]{2,1,0:T(2,128)(2,1)} %reshape.298), calls=%async_computation.1 | async-start | bytes 65536 | tf_op jit(solution)/shard_map/all_to_all | solution.py:594
  63.0 3.8 all-to-all-done.1
  70.0 5.2 collective-permute-done.9
  88.3 3.8 fusion.75
  92.3 18.6 %collective-permute-done.11 = bf16[512,1024]{1,0:T(8,128)(2,1)} collective-permute-done((bf16[512,1024]{1,0:T(8,128)(2,1)}, bf16[512,1024]{1,0:T(8,128)(2,1)}, u32[]{:S(2)}, u32[]{:S(2)}) %collective-permute-start.11) | collective-permute-done | bytes 1048608 | tf_op jit(solution)/shard_map/ppermute | solution.py:584
  118.4 16.1 %collective-permute-done.7.refs_5_ = bf16[3,24,16,256]{3,2,1,0:T(8,128)(2,1)S(1)} collective-permute-done((bf16[3,24,16,256]{3,2,1,0:T(8,128)(2,1)}, bf16[3,24,16,256]{3,2,1,0:T(8,128)(2,1)S(1)}, u32[]{:S(2)}, u32[]{:S(2)}) %collective-permute-start.7) | collective-permute-done | bytes 589856 | tf_op jit(solution)/shard_map/ppermute | solution.py:584
  140.7 3.5 fusion.128.proj_ref
  144.2 7.7 %attend.5 = (bf16[1024,256]{1,0:T(8,128)(2,1)S(1)}, bf16[1024,768]{1,0:T(8,128)(2,1)S(1)}, f32[8,1024]{1,0:T(8,128)S(1)}) custom-call(s32[1]{0:T(128)} %bitcast.1.flip_ref, f32[1024,768]{1,0:T(8,128)} %fusion.128.proj_ref, f32[3,1024,128]{2,1,0:T(8,128)} %get-tuple-element.224.tab_ref, bf16[1024,256]{1,0:T(8,128)(2,1)S(1)} %copy-done.6, ...), custom_call_target="tpu_custom_call" | custom-call | flops 2147483648 | bytes 6291456 | tf_op jit(solution)/shard_map/attend/pallas_call | solution.py:200
  153.1 18.7 %all-gather.5.cloned.1.call-done = bf16[576,16,256]{2,1,0:T(8,128)(2,1)} async-done(((bf16[72,16,256]{2,1,0:T(8,128)(2,1)}), bf16[576,16,256]{2,1,0:T(8,128)(2,1)}) %all-gather.5.cloned.1.call-update) | async-done | bytes 4718608 | tf_op jit(solution)/shard_map/all_gather | solution.py:689
  171.8 4.0 assemble.4
  178.3 10.3 %multiply_convert_fusion.6 = (bf16[1024,1024]{1,0:T(8,128)(2,1)}, bf16[1024,1024]{1,0:T(8,128)(2,1)S(1)}, f32[1024,1024]{1,0:T(8,128)}) fusion(f32[1024]{0:T(1024)S(1)} %bitcast.180, f32[1024,1024]{1,0:T(8,128)S(1)} %fusion.129, bf16[1024,1024]{1,0:T(8,128)(2,1)S(1)} %get-tuple-element.120, bf16[512,1024]{1,0:T(8,128)(2,1)} %collective-permute-done.2, ...), kind=kOutput, calls=%fused_computation.48 | convolution fusion | flops 2172649472 | bytes 16781312 | tf_op jit(solution)/shard_map/dot_general | solution.py:37
  192.0 5.1 fusion.114.proj_ref
  197.1 7.9 %attend.4 = (bf16[1024,256]{1,0:T(8,128)(2,1)S(1)}, bf16[1024,768]{1,0:T(8,128)(2,1)S(1)}, f32[8,1024]{1,0:T(8,128)S(1)}) custom-call(s32[1]{0:T(128)} %bitcast.1.flip_ref, f32[1024,768]{1,0:T(8,128)} %fusion.114.proj_ref, f32[3,1024,128]{2,1,0:T(8,128)} %get-tuple-element.223.tab_ref, bf16[1024,256]{1,0:T(8,128)(2,1)S(1)} %copy-done.9, ...), custom_call_target="tpu_custom_call" | custom-call | flops 2147483648 | bytes 6291456 | tf_op jit(solution)/shard_map/attend/pallas_call | solution.py:200
  205.1 3.4 fusion.53
  219.6 22.8 %collective-permute-done.17 = bf16[512,1024]{1,0:T(8,128)(2,1)} collective-permute-done((bf16[512,1024]{1,0:T(8,128)(2,1)}, bf16[512,1024]{1,0:T(8,128)(2,1)}, u32[]{:S(2)}, u32[]{:S(2)}) %collective-permute-start.17) | collective-permute-done | bytes 1048608 | tf_op jit(solution)/shard_map/ppermute | solution.py:584
  252.4 29.0 %collective-permute-done.15 = bf16[1,256,1024]{2,1,0:T(8,128)(2,1)} collective-permute-done((bf16[1,256,1024]{2,1,0:T(8,128)(2,1)S(1)}, bf16[1,256,1024]{2,1,0:T(8,128)(2,1)}, u32[]{:S(2)}, u32[]{:S(2)}) %collective-permute-start.15) | collective-permute-done | bytes 524320 | tf_op jit(solution)/shard_map/ppermute | solution.py:619
  284.6 6.3 assemble.5
  290.8 7.2 collective-permute-start.20
  298.1 3.6 fusion.109
  301.7 5.6 fusion.110.proj_ref
  308.6 4.8 fusion.56
  313.5 3.5 fusion.130.proj_ref
  324.7 8.2 %attend.7 = (bf16[1024,256]{1,0:T(8,128)(2,1)S(1)}, bf16[1024,768]{1,0:T(8,128)(2,1)S(1)}, f32[8,1024]{1,0:T(8,128)S(1)}) custom-call(s32[1]{0:T(128)} %bitcast.1.flip_ref, f32[1024,768]{1,0:T(8,128)} %fusion.130.proj_ref, f32[3,1024,128]{2,1,0:T(8,128)} %get-tuple-element.224.tab_ref, bf16[1024,256]{1,0:T(8,128)(2,1)S(1)} %copy-done.6, ...), custom_call_target="tpu_custom_call" | custom-call | flops 2147483648 | bytes 6291456 | tf_op jit(solution)/shard_map/attend/pallas_call | solution.py:200
  337.8 7.8 %attend.6 = (bf16[1024,256]{1,0:T(8,128)(2,1)S(1)}, bf16[1024,768]{1,0:T(8,128)(2,1)S(1)}, f32[8,1024]{1,0:T(8,128)S(1)}) custom-call(s32[1]{0:T(128)} %bitcast.1.flip_ref, f32[1024,768]{1,0:T(8,128)} %fusion.110.proj_ref, f32[3,1024,128]{2,1,0:T(8,128)} %get-tuple-element.223.tab_ref, bf16[1024,256]{1,0:T(8,128)(2,1)S(1)} %copy-done.10, ...), custom_call_target="tpu_custom_call" | custom-call | flops 2147483648 | bytes 6291456 | tf_op jit(solution)/shard_map/attend/pallas_call | solution.py:200
  349.3 7.1 multiply_convert_fusion.5
  356.4 3.4 fusion.52
  359.8 3.8 fusion.108
  367.6 4.7 multiply_convert_fusion.4
  372.4 5.3 convolution_add_fusion.9.refs_2_
  381.8 5.7 disassemble.5
  397.4 12.6 %attend_back.4 = bf16[1024,768]{1,0:T(8,128)(2,1)S(1)} custom-call(s32[1]{0:T(128)} %bitcast.1.flip_ref, bf16[1024,768]{1,0:T(8,128)(2,1)} %copy-done.28, bf16[1024,256]{1,0:T(8,128)(2,1)S(1)} %convolution_convert_fusion.3.dctx_ref, f32[8,1024]{1,0:T(8,128)S(1)} %get-tuple-element.139.lse_ref, f32[3,1024,128]{2,1,0:T(8,128)} %get-tuple-element.224.tab_ref, ...), custom_call_target="tpu_custom_call" | custom-call | flops 5368709120 | bytes 6291456 | tf_op jit(solution)/shard_map/attend_back/pallas_call | solution.py:223
  426.0 12.9 %attend_back.5 = bf16[1024,768]{1,0:T(8,128)(2,1)S(1)} custom-call(s32[1]{0:T(128)} %bitcast.1.flip_ref, bf16[1024,768]{1,0:T(8,128)(2,1)} %copy-done.27, bf16[1024,256]{1,0:T(8,128)(2,1)S(1)} %convolution_convert_fusion.2.dctx_ref, f32[8,1024]{1,0:T(8,128)S(1)} %get-tuple-element.145.lse_ref, f32[3,1024,128]{2,1,0:T(8,128)} %get-tuple-element.223.tab_ref, ...), custom_call_target="tpu_custom_call" | custom-call | flops 5368709120 | bytes 6291456 | tf_op jit(solution)/shard_map/attend_back/pallas_call | solution.py:223
  438.9 8.6 %collective-permute-done.28 = bf16[512,1024]{1,0:T(8,128)(2,1)} collective-permute-done((bf16[512,1024]{1,0:T(8,128)(2,1)S(1)}, bf16[512,1024]{1,0:T(8,128)(2,1)}, u32[]{:S(2)}, u32[]{:S(2)}) %collective-permute-start.28) | collective-permute-done | bytes 1048608 | tf_op jit(solution)/shard_map/ppermute | solution.py:584
  472.6 13.5 %reduce-scatter.3.cloned.1.call-done = bf16[1,72,16,256]{3,2,1,0:T(8,128)(2,1)} async-done(((bf16[8,72,16,256]{3,2,1,0:T(8,128)(2,1)}), bf16[1,72,16,256]{3,2,1,0:T(8,128)(2,1)}) %reduce-scatter.3.cloned.1.call-update) | async-done | bytes 589840 | tf_op jit(solution)/shard_map/reduce_scatter | solution.py:912
  491.9 8.0 %multiply_convert_fusion.1 = bf16[1024,1024]{1,0:T(8,128)(2,1)} fusion(f32[1024,1024]{1,0:T(8,128)} %get-tuple-element.276, f32[1024]{0:T(1024)S(1)} %bitcast.181, bf16[1024,1024]{1,0:T(8,128)(2,1)S(1)} %copy-done.37, bf16[1280,1024]{1,0:T(8,128)(2,1)} %copy-done.11), kind=kOutput, calls=%fused_computation.43 | convolution fusion | flops 2170552320 | bytes 10489856 | tf_op jit(solution)/shard_map/dot_general | solution.py:41
  501.7 12.5 %attend_back.6 = bf16[1024,768]{1,0:T(8,128)(2,1)S(1)} custom-call(s32[1]{0:T(128)} %bitcast.1.flip_ref, bf16[1024,768]{1,0:T(8,128)(2,1)} %copy-done.26, bf16[1024,256]{1,0:T(8,128)(2,1)S(1)} %convolution_convert_fusion.1.dctx_ref, f32[8,1024]{1,0:T(8,128)S(1)} %get-tuple-element.157.lse_ref, f32[3,1024,128]{2,1,0:T(8,128)} %get-tuple-element.223.tab_ref, ...), custom_call_target="tpu_custom_call" | custom-call | flops 5368709120 | bytes 6291456 | tf_op jit(solution)/shard_map/attend_back/pallas_call | solution.py:223
  520.1 5.7 fusion.111
  525.8 5.9 fusion.112
  537.6 4.5 convolution_add_fusion.6.refs_1_
  547.1 6.6 multiply_convert_fusion
  553.7 4.5 convolution_add_fusion.5.refs_0_
  558.2 3.3 disassemble.8
  561.5 16.9 %collective-permute-done.35 = bf16[4,40,16,256]{3,2,1,0:T(8,128)(2,1)S(1)} collective-permute-done((bf16[4,40,16,256]{3,2,1,0:T(8,128)(2,1)S(1)}, bf16[4,40,16,256]{3,2,1,0:T(8,128)(2,1)S(1)}, u32[]{:S(2)}, u32[]{:S(2)}) %collective-permute-start.35) | collective-permute-done | bytes 1310752 | tf_op jit(solution)/shard_map/ppermute | solution.py:584
  579.9 9.2 %all-to-all-start.2 = ((bf16[4,40,16,256]{3,2,1,0:T(8,128)(2,1)}), bf16[4,40,16,256]{3,2,1,0:T(8,128)(2,1)}, u32[]{:S(2)}, u32[]{:S(2)}) async-start(bf16[4,40,16,256]{3,2,1,0:T(8,128)(2,1)} %add_convert_fusion), calls=%async_computation.3 | async-start | bytes 2621440 | tf_op jit(solution)/shard_map/all_to_all | solution.py:926
  589.1 6.8 fusion.137
  599.3 12.8 %attend_back.7 = bf16[1024,768]{1,0:T(8,128)(2,1)S(1)} custom-call(s32[1]{0:T(128)} %bitcast.1.flip_ref, bf16[1024,768]{1,0:T(8,128)(2,1)} %copy-done.25, bf16[1024,256]{1,0:T(8,128)(2,1)S(1)} %convolution_convert_fusion.dctx_ref, f32[8,1024]{1,0:T(8,128)S(1)} %get-tuple-element.174.lse_ref, f32[3,1024,128]{2,1,0:T(8,128)} %get-tuple-element.224.tab_ref, ...), custom_call_target="tpu_custom_call" | custom-call | flops 5368709120 | bytes 6291456 | tf_op jit(solution)/shard_map/attend_back/pallas_call | solution.py:223
  612.1 4.3 convolution_add_fusion.11.refs_0_
  624.1 4.8 all-to-all-start.3
  628.9 4.5 convolution_add_fusion.4
  637.6 15.8 %all-to-all-done.3 = bf16[4,32,16,256]{3,2,1,0:T(8,128)(2,1)S(1)} async-done(((bf16[4,32,16,256]{3,2,1,0:T(8,128)(2,1)}), bf16[4,32,16,256]{3,2,1,0:T(8,128)(2,1)S(1)}, u32[]{:S(2)}, u32[]{:S(2)}) %all-to-all-start.3) | async-done | bytes 1048608 | tf_op jit(solution)/shard_map/all_to_all | solution.py:926
  655.8 5.2 fusion.138
  663.4 3.7 all-to-all-start.4
  667.2 5.3 fusion.127
  672.6 6.2 collective-permute-done.38
  694.0 4.4 place.1
  698.4 4.5 all-to-all-start.5
  706.1 12.6 %collective-permute-done.42 = bf16[256,1024]{1,0:T(8,128)(2,1)S(1)} collective-permute-done((bf16[256,1024]{1,0:T(8,128)(2,1)S(1)}, bf16[256,1024]{1,0:T(8,128)(2,1)S(1)}, u32[]{:S(2)}, u32[]{:S(2)}) %collective-permute-start.42) | collective-permute-done | bytes 524320 | tf_op jit(solution)/shard_map/ppermute | solution.py:634
  718.8 11.7 %all-to-all-done.5.from_ref = bf16[8,528,256]{2,1,0:T(8,128)(2,1)} async-done(((bf16[8,528,256]{2,1,0:T(8,128)(2,1)}), bf16[8,528,256]{2,1,0:T(8,128)(2,1)}, u32[]{:S(2)}, u32[]{:S(2)}) %all-to-all-start.5) | async-done | bytes 2162720 | tf_op jit(solution)/shard_map/all_to_all | solution.py:1069
  732.0 4.3 all-to-all-start.6
  737.3 17.6 %adam.1 = (f32[32,32768]{1,0:T(8,128)}, f32[32,32768]{1,0:T(8,128)}, f32[32,32768]{1,0:T(8,128)}, bf16[32,32768]{1,0:T(8,128)(2,1)}) custom-call(bf16[8,528,256]{2,1,0:T(8,128)(2,1)} %all-to-all-done.5.from_ref, f32[32,32768]{1,0:T(8,128)} %w_ref.1, f32[32,32768]{1,0:T(8,128)} %one_ref.1, f32[32,32768]{1,0:T(8,128)} %two_ref.1), custom_call_target="tpu_custom_call" | custom-call | flops 20971520 | bytes 29360128 | tf_op jit(solution)/shard_map/adam/pallas_call | solution.py:500
  (496 shorter events, 215.1 us)
Async XLA Ops:
  12.5 32.1 %all-to-all-start = ((bf16[8,512,256]{2,1,0:T(8,128)(2,1)}), bf16[8,512,256]{2,1,0:T(8,128)(2,1)}, u32[]{:S(2)}, u32[]{:S(2)}) async-start(bf16[8,512,256]{2,1,0:T(8,128)(2,1)} %pack.1), calls=%async_computation | async-start | bytes 4194304 | tf_op jit(solution)/shard_map/all_to_all | solution.py:672
  23.0 4.7 collective-permute-start
  23.7 14.2 %collective-permute-start.1 = (bf16[1,256,1024]{2,1,0:T(8,128)(2,1)S(1)}, bf16[1,256,1024]{2,1,0:T(8,128)(2,1)S(1)}, u32[]{:S(2)}, u32[]{:S(2)}) collective-permute-start(bf16[1,256,1024]{2,1,0:T(8,128)(2,1)S(1)} %get-tuple-element.243), channel_id=1, source_target_pairs={{0,1},{16,17},{1,0},{17,16},{2,5},{18,21},{3,4},{19,20},{4,3},{20,... | collective-permute-start | bytes 1572872 | tf_op jit(solution)/shard_map/ppermute | solution.py:619
  38.1 46.8 %copy-start.32 = (bf16[512,1024]{1,0:T(8,128)(2,1)}, bf16[512,1024]{1,0:T(8,128)(2,1)S(1)}, u32[]{:S(2)}) copy-start(bf16[512,1024]{1,0:T(8,128)(2,1)S(1)} %maximum_bitcast_fusion) | copy-start | bytes 3145732
  46.6 20.2 %all-to-all-start.1 = ((bf16[32,2,256]{2,1,0:T(2,128)(2,1)}), bf16[32,2,256]{2,1,0:T(2,128)(2,1)S(1)}, u32[]{:S(2)}, u32[]{:S(2)}) async-start(bf16[32,2,256]{2,1,0:T(2,128)(2,1)} %reshape.298), calls=%async_computation.1 | async-start | bytes 65536 | tf_op jit(solution)/shard_map/all_to_all | solution.py:594
  59.5 112.3 %all-gather.5.cloned.1.call-start = ((), (), s32[]{:S(2)}) async-start(), calls=%async_computation.11 | async-start | bytes 5308416 | tf_op jit(solution)/shard_map/all_gather | solution.py:689
  68.1 2.0 collective-permute-start.8
  68.1 7.1 collective-permute-start.9
  68.8 9.0 %collective-permute-start.10 = (bf16[20,16,256]{2,1,0:T(8,128)(2,1)S(1)}, bf16[20,16,256]{2,1,0:T(8,128)(2,1)S(1)}, u32[]{:S(2)}, u32[]{:S(2)}) collective-permute-start(bf16[20,16,256]{2,1,0:T(8,128)(2,1)S(1)} %get-tuple-element.252), channel_id=1, source_target_pairs={{0,12},{4,8},{8,4},{12,0},{16,28},{20,24},{24,20},{28,16},{1,13},{... | collective-permute-start | bytes 491528 | tf_op jit(solution)/shard_map/ppermute | solution.py:584
  79.5 205.1 %all-gather.7.cloned.1.call-start = ((), (), s32[]{:S(2)}) async-start(), calls=%async_computation.12 | async-start | bytes 7077888 | tf_op jit(solution)/shard_map/all_gather | solution.py:689
  80.6 32.1 %collective-permute-start.5 = (bf16[24,16,256]{2,1,0:T(8,128)(2,1)S(1)}, bf16[24,16,256]{2,1,0:T(8,128)(2,1)S(1)}, u32[]{:S(2)}, u32[]{:S(2)}) collective-permute-start(bf16[24,16,256]{2,1,0:T(8,128)(2,1)S(1)} %copy-done.13), channel_id=1, source_target_pairs={{0,3},{1,0},{2,1},{3,2},{4,7},{5,4},{6,5},{7,6},{8,11},{9,8},{10,9... | collective-permute-start | bytes 589832 | tf_op jit(solution)/shard_map/ppermute | solution.py:744
  81.2 32.0 %collective-permute-start.3 = (bf16[24,16,256]{2,1,0:T(8,128)(2,1)S(1)}, bf16[24,16,256]{2,1,0:T(8,128)(2,1)S(1)}, u32[]{:S(2)}, u32[]{:S(2)}) collective-permute-start(bf16[24,16,256]{2,1,0:T(8,128)(2,1)S(1)} %copy-done.13), channel_id=1, source_target_pairs={{0,1},{1,2},{2,3},{3,0},{4,5},{5,6},{6,7},{7,4},{8,9},{9,10},{10,1... | collective-permute-start | bytes 589832 | tf_op jit(solution)/shard_map/ppermute | solution.py:744
  82.7 30.8 %collective-permute-start.4 = (bf16[24,16,256]{2,1,0:T(8,128)(2,1)S(1)}, bf16[24,16,256]{2,1,0:T(8,128)(2,1)S(1)}, u32[]{:S(2)}, u32[]{:S(2)}) collective-permute-start(bf16[24,16,256]{2,1,0:T(8,128)(2,1)S(1)} %copy-done.13), channel_id=1, source_target_pairs={{0,2},{1,3},{2,0},{3,1},{4,6},{5,7},{6,4},{7,5},{8,10},{9,11},{10,... | collective-permute-start | bytes 589832 | tf_op jit(solution)/shard_map/ppermute | solution.py:744
  83.2 34.6 %collective-permute-start.6 = (bf16[24,16,256]{2,1,0:T(8,128)(2,1)S(1)}, bf16[24,16,256]{2,1,0:T(8,128)(2,1)S(1)}, u32[]{:S(2)}, u32[]{:S(2)}) collective-permute-start(bf16[24,16,256]{2,1,0:T(8,128)(2,1)S(1)} %copy-done.13), channel_id=1, source_target_pairs={{0,16},{4,20},{8,24},{12,28},{16,0},{20,4},{24,8},{28,12},{1,17},{... | collective-permute-start | bytes 589832 | tf_op jit(solution)/shard_map/ppermute | solution.py:584
  86.3 24.5 %collective-permute-start.11 = (bf16[512,1024]{1,0:T(8,128)(2,1)}, bf16[512,1024]{1,0:T(8,128)(2,1)}, u32[]{:S(2)}, u32[]{:S(2)}) collective-permute-start(bf16[512,1024]{1,0:T(8,128)(2,1)} %fusion.35), channel_id=1, source_target_pairs={{0,8},{4,12},{8,0},{12,4},{16,24},{20,28},{24,16},{28,20},{1,9},{5... | collective-permute-start | bytes 3145736 | tf_op jit(solution)/shard_map/ppermute | solution.py:584
  88.2 397.9 %reduce-scatter.3.cloned.1.call-start = ((), (), s32[]{:S(2)}) async-start(), calls=%async_computation.9 | async-start | bytes 5308416 | tf_op jit(solution)/shard_map/reduce_scatter | solution.py:912
  110.9 28.5 %collective-permute-start.12 = (bf16[512,1024]{1,0:T(8,128)(2,1)}, bf16[512,1024]{1,0:T(8,128)(2,1)}, u32[]{:S(2)}, u32[]{:S(2)}) collective-permute-start(bf16[512,1024]{1,0:T(8,128)(2,1)} %collective-permute-done.11), channel_id=1, source_target_pairs={{0,4},{4,0},{8,12},{12,8},{16,20},{20,16},{24,28},{28,24},{1,5},{5... | collective-permute-start | bytes 3145736 | tf_op jit(solution)/shard_map/ppermute | solution.py:584
  112.7 65.5 %collective-permute-start.2 = (bf16[512,1024]{1,0:T(8,128)(2,1)}, bf16[512,1024]{1,0:T(8,128)(2,1)}, u32[]{:S(2)}, u32[]{:S(2)}) collective-permute-start(bf16[512,1024]{1,0:T(8,128)(2,1)} %fusion.35), channel_id=1, source_target_pairs={{0,4},{4,0},{8,12},{12,8},{16,20},{20,16},{24,28},{28,24},{1,5},{5... | collective-permute-start | bytes 3145736 | tf_op jit(solution)/shard_map/ppermute | solution.py:584
  114.4 20.1 %collective-permute-start.7 = (bf16[3,24,16,256]{3,2,1,0:T(8,128)(2,1)}, bf16[3,24,16,256]{3,2,1,0:T(8,128)(2,1)S(1)}, u32[]{:S(2)}, u32[]{:S(2)}) collective-permute-start(bf16[3,24,16,256]{3,2,1,0:T(8,128)(2,1)} %pad_maximum_fusion.8), channel_id=1, source_target_pairs={{0,16},{4,20},{8,24},{12,28},{16,0},{20,4},{24,8},{28,12},{1,17},{... | collective-permute-start | bytes 1769480 | tf_op jit(solution)/shard_map/ppermute | solution.py:584
  117.7 60.5 %copy-start.92 = (f32[4,1,256]{2,1,0:T(1,128)}, f32[4,1,256]{2,1,0:T(1,128)S(1)}, u32[]{:S(2)}) copy-start(f32[4,1,256]{2,1,0:T(1,128)S(1)} %fusion.95) | copy-start | bytes 12292
  137.5 54.5 %copy-start.4 = (bf16[1024,768]{1,0:T(8,128)(2,1)}, bf16[1024,768]{1,0:T(8,128)(2,1)S(1)}, u32[]{:S(2)}) copy-start(bf16[1024,768]{1,0:T(8,128)(2,1)S(1)} %assemble.3) | copy-start | bytes 4718596
  153.1 37.8 %copy-start = (bf16[1024,256]{1,0:T(8,128)(2,1)}, bf16[1024,256]{1,0:T(8,128)(2,1)S(1)}, u32[]{:S(2)}) copy-start(bf16[1024,256]{1,0:T(8,128)(2,1)S(1)} %get-tuple-element.119) | copy-start | bytes 1572868
  175.9 34.9 %copy-start.11 = (bf16[1280,1024]{1,0:T(8,128)(2,1)}, bf16[1280,1024]{1,0:T(8,128)(2,1)S(1)}, u32[]{:S(2)}) copy-start(bf16[1280,1024]{1,0:T(8,128)(2,1)S(1)} %get-tuple-element.118) | copy-start | bytes 7864324
  191.9 13.2 %collective-permute-start.13 = (bf16[512,1024]{1,0:T(8,128)(2,1)S(1)}, bf16[512,1024]{1,0:T(8,128)(2,1)}, u32[]{:S(2)}, u32[]{:S(2)}) collective-permute-start(bf16[512,1024]{1,0:T(8,128)(2,1)S(1)} %slice.354), channel_id=1, source_target_pairs={{0,4},{4,0},{8,12},{12,8},{16,20},{20,16},{24,28},{28,24},{1,5},{5... | collective-permute-start | bytes 3145736 | tf_op jit(solution)/shard_map/ppermute | solution.py:584
  213.5 28.8 %copy-start.33 = (bf16[512,1024]{1,0:T(8,128)(2,1)S(1)}, bf16[512,1024]{1,0:T(8,128)(2,1)}, u32[]{:S(2)}) copy-start(bf16[512,1024]{1,0:T(8,128)(2,1)} %copy-done.32) | copy-start | bytes 3145732
  216.4 3.2 collective-permute-start.16
  217.0 25.4 %collective-permute-start.17 = (bf16[512,1024]{1,0:T(8,128)(2,1)}, bf16[512,1024]{1,0:T(8,128)(2,1)}, u32[]{:S(2)}, u32[]{:S(2)}) collective-permute-start(bf16[512,1024]{1,0:T(8,128)(2,1)} %fusion.53), channel_id=1, source_target_pairs={{0,8},{4,12},{8,0},{12,4},{16,24},{20,28},{24,16},{28,20},{1,9},{5... | collective-permute-start | bytes 3145736 | tf_op jit(solution)/shard_map/ppermute | solution.py:584
  246.6 55.0 %copy-start.59 = (bf16[512,1024]{1,0:T(8,128)(2,1)}, bf16[512,1024]{1,0:T(8,128)(2,1)S(1)}, u32[]{:S(2)}) copy-start(bf16[512,1024]{1,0:T(8,128)(2,1)S(1)} %add_convert_fusion.2) | copy-start | bytes 3145732
  246.6 51.4 %collective-permute-start.18 = (bf16[512,1024]{1,0:T(8,128)(2,1)S(1)}, bf16[512,1024]{1,0:T(8,128)(2,1)}, u32[]{:S(2)}, u32[]{:S(2)}) collective-permute-start(bf16[512,1024]{1,0:T(8,128)(2,1)S(1)} %add_convert_fusion.2), channel_id=1, source_target_pairs={{0,4},{4,0},{8,12},{12,8},{16,20},{20,16},{24,28},{28,24},{1,5},{5... | collective-permute-start | bytes 3145736 | tf_op jit(solution)/shard_map/ppermute | solution.py:584
  246.6 44.2 %collective-permute-start.19 = (bf16[512,1024]{1,0:T(8,128)(2,1)S(1)}, bf16[512,1024]{1,0:T(8,128)(2,1)}, u32[]{:S(2)}, u32[]{:S(2)}) collective-permute-start(bf16[512,1024]{1,0:T(8,128)(2,1)S(1)} %add_convert_fusion.2), channel_id=1, source_target_pairs={{0,8},{4,12},{8,0},{12,4},{16,24},{20,28},{24,16},{28,20},{1,9},{5... | collective-permute-start | bytes 3145736 | tf_op jit(solution)/shard_map/ppermute | solution.py:584
  248.2 3.5 collective-permute-start.14
  249.8 31.5 %collective-permute-start.15 = (bf16[1,256,1024]{2,1,0:T(8,128)(2,1)S(1)}, bf16[1,256,1024]{2,1,0:T(8,128)(2,1)}, u32[]{:S(2)}, u32[]{:S(2)}) collective-permute-start(bf16[1,256,1024]{2,1,0:T(8,128)(2,1)S(1)} %get-tuple-element.235), channel_id=1, source_target_pairs={{0,1},{16,17},{1,0},{17,16},{2,5},{18,21},{3,4},{19,20},{4,3},{20,... | collective-permute-start | bytes 1572872 | tf_op jit(solution)/shard_map/ppermute | solution.py:619
  290.8 22.5 %collective-permute-start.20 = (bf16[512,1024]{1,0:T(8,128)(2,1)}, bf16[512,1024]{1,0:T(8,128)(2,1)S(1)}, u32[]{:S(2)}, u32[]{:S(2)}) collective-permute-start(bf16[512,1024]{1,0:T(8,128)(2,1)} %collective-permute-done.19), channel_id=1, source_target_pairs={{0,4},{4,0},{8,12},{12,8},{16,20},{20,16},{24,28},{28,24},{1,5},{5... | collective-permute-start | bytes 3145736 | tf_op jit(solution)/shard_map/ppermute | solution.py:584
  319.3 28.7 %collective-permute-start.21 = (bf16[512,1024]{1,0:T(8,128)(2,1)}, bf16[512,1024]{1,0:T(8,128)(2,1)}, u32[]{:S(2)}, u32[]{:S(2)}) collective-permute-start(bf16[512,1024]{1,0:T(8,128)(2,1)} %maximum_bitcast_fusion.1), channel_id=1, source_target_pairs={{0,4},{4,0},{8,12},{12,8},{16,20},{20,16},{24,28},{28,24},{1,5},{5... | collective-permute-start | bytes 3145736 | tf_op jit(solution)/shard_map/ppermute | solution.py:584
  320.2 25.5 %collective-permute-start.22 = (bf16[512,1024]{1,0:T(8,128)(2,1)}, bf16[512,1024]{1,0:T(8,128)(2,1)}, u32[]{:S(2)}, u32[]{:S(2)}) collective-permute-start(bf16[512,1024]{1,0:T(8,128)(2,1)} %maximum_bitcast_fusion.1), channel_id=1, source_target_pairs={{0,8},{4,12},{8,0},{12,4},{16,24},{20,28},{24,16},{28,20},{1,9},{5... | collective-permute-start | bytes 3145736 | tf_op jit(solution)/shard_map/ppermute | solution.py:584
  336.2 20.2 %collective-permute-start.24 = (bf16[512,1024]{1,0:T(8,128)(2,1)}, bf16[512,1024]{1,0:T(8,128)(2,1)}, u32[]{:S(2)}, u32[]{:S(2)}) collective-permute-start(bf16[512,1024]{1,0:T(8,128)(2,1)} %slice.352), channel_id=1, source_target_pairs={{0,4},{4,0},{8,12},{12,8},{16,20},{20,16},{24,28},{28,24},{1,5},{5... | collective-permute-start | bytes 3145736 | tf_op jit(solution)/shard_map/ppermute | solution.py:584
  345.6 21.9 %collective-permute-start.23 = (bf16[512,1024]{1,0:T(8,128)(2,1)}, bf16[512,1024]{1,0:T(8,128)(2,1)S(1)}, u32[]{:S(2)}, u32[]{:S(2)}) collective-permute-start(bf16[512,1024]{1,0:T(8,128)(2,1)} %collective-permute-done.22), channel_id=1, source_target_pairs={{0,4},{4,0},{8,12},{12,8},{16,20},{20,16},{24,28},{28,24},{1,5},{5... | collective-permute-start | bytes 3145736 | tf_op jit(solution)/shard_map/ppermute | solution.py:584
  387.5 25.6 %collective-permute-start.25 = (bf16[512,1024]{1,0:T(8,128)(2,1)}, bf16[512,1024]{1,0:T(8,128)(2,1)}, u32[]{:S(2)}, u32[]{:S(2)}) collective-permute-start(bf16[512,1024]{1,0:T(8,128)(2,1)} %fusion.52), channel_id=1, source_target_pairs={{0,8},{4,12},{8,0},{12,4},{16,24},{20,28},{24,16},{28,20},{1,9},{5... | collective-permute-start | bytes 3145736 | tf_op jit(solution)/shard_map/ppermute | solution.py:584
  388.8 235.3 %reduce-scatter.5.cloned.1.call-start = ((), (), s32[]{:S(2)}) async-start(), calls=%async_computation.10 | async-start | bytes 1769472 | tf_op jit(solution)/shard_map/reduce_scatter | solution.py:912
  393.6 24.2 %collective-permute-start.27 = (bf16[512,1024]{1,0:T(8,128)(2,1)}, bf16[512,1024]{1,0:T(8,128)(2,1)S(1)}, u32[]{:S(2)}, u32[]{:S(2)}) collective-permute-start(bf16[512,1024]{1,0:T(8,128)(2,1)} %slice.350), channel_id=1, source_target_pairs={{0,4},{4,0},{8,12},{12,8},{16,20},{20,16},{24,28},{28,24},{1,5},{5... | collective-permute-start | bytes 3145736 | tf_op jit(solution)/shard_map/ppermute | solution.py:584
  417.7 4.5 collective-permute-start.26
  422.5 25.0 %collective-permute-start.28 = (bf16[512,1024]{1,0:T(8,128)(2,1)S(1)}, bf16[512,1024]{1,0:T(8,128)(2,1)}, u32[]{:S(2)}, u32[]{:S(2)}) collective-permute-start(bf16[512,1024]{1,0:T(8,128)(2,1)S(1)} %fusion.51), channel_id=1, source_target_pairs={{0,8},{4,12},{8,0},{12,4},{16,24},{20,28},{24,16},{28,20},{1,9},{5... | collective-permute-start | bytes 3145736 | tf_op jit(solution)/shard_map/ppermute | solution.py:584
  451.9 2.7 collective-permute-start.29
  460.1 9.4 %collective-permute-start.30 = (bf16[512,1024]{1,0:T(8,128)(2,1)}, bf16[512,1024]{1,0:T(8,128)(2,1)}, u32[]{:S(2)}, u32[]{:S(2)}) collective-permute-start(bf16[512,1024]{1,0:T(8,128)(2,1)} %get-tuple-element.150), channel_id=1, source_target_pairs={{0,4},{4,0},{8,12},{12,8},{16,20},{20,16},{24,28},{28,24},{1,5},{5... | collective-permute-start | bytes 3145736 | tf_op jit(solution)/shard_map/ppermute | solution.py:584
  460.3 56.4 %collective-permute-start.31 = (bf16[512,1024]{1,0:T(8,128)(2,1)}, bf16[512,1024]{1,0:T(8,128)(2,1)}, u32[]{:S(2)}, u32[]{:S(2)}) collective-permute-start(bf16[512,1024]{1,0:T(8,128)(2,1)} %get-tuple-element.150), channel_id=1, source_target_pairs={{0,8},{4,12},{8,0},{12,4},{16,24},{20,28},{24,16},{28,20},{1,9},{5... | collective-permute-start | bytes 3145736 | tf_op jit(solution)/shard_map/ppermute | solution.py:584
  488.5 25.7 %collective-permute-start.32 = (bf16[256,1024]{1,0:T(8,128)(2,1)}, bf16[256,1024]{1,0:T(8,128)(2,1)S(1)}, u32[]{:S(2)}, u32[]{:S(2)}) collective-permute-start(bf16[256,1024]{1,0:T(8,128)(2,1)} %get-tuple-element.232), channel_id=1, source_target_pairs={{0,0},{16,16},{1,1},{17,17},{4,2},{20,18},{5,3},{21,19},{2,4},{18,... | collective-permute-start | bytes 1572872 | tf_op jit(solution)/shard_map/ppermute | solution.py:634
  490.2 24.0 %collective-permute-start.33 = (bf16[256,1024]{1,0:T(8,128)(2,1)}, bf16[256,1024]{1,0:T(8,128)(2,1)}, u32[]{:S(2)}, u32[]{:S(2)}) collective-permute-start(bf16[256,1024]{1,0:T(8,128)(2,1)} %get-tuple-element.231), channel_id=1, source_target_pairs={{1,0},{17,16},{0,1},{16,17},{5,2},{21,18},{4,3},{20,19},{3,4},{19,... | collective-permute-start | bytes 1572872 | tf_op jit(solution)/shard_map/ppermute | solution.py:634
  516.8 15.0 %collective-permute-start.34 = (bf16[512,1024]{1,0:T(8,128)(2,1)}, bf16[512,1024]{1,0:T(8,128)(2,1)S(1)}, u32[]{:S(2)}, u32[]{:S(2)}) collective-permute-start(bf16[512,1024]{1,0:T(8,128)(2,1)} %collective-permute-done.31), channel_id=1, source_target_pairs={{0,4},{4,0},{8,12},{12,8},{16,20},{20,16},{24,28},{28,24},{1,5},{5... | collective-permute-start | bytes 3145736 | tf_op jit(solution)/shard_map/ppermute | solution.py:584
  545.6 32.8 %collective-permute-start.35 = (bf16[4,40,16,256]{3,2,1,0:T(8,128)(2,1)S(1)}, bf16[4,40,16,256]{3,2,1,0:T(8,128)(2,1)S(1)}, u32[]{:S(2)}, u32[]{:S(2)}) collective-permute-start(bf16[4,40,16,256]{3,2,1,0:T(8,128)(2,1)S(1)} %get-tuple-element.172), channel_id=1, source_target_pairs={{0,16},{4,20},{8,24},{12,28},{16,0},{20,4},{24,8},{28,12},{1,17},{... | collective-permute-start | bytes 3932168 | tf_op jit(solution)/shard_map/ppermute | solution.py:584
  579.9 41.7 %all-to-all-start.2 = ((bf16[4,40,16,256]{3,2,1,0:T(8,128)(2,1)}), bf16[4,40,16,256]{3,2,1,0:T(8,128)(2,1)}, u32[]{:S(2)}, u32[]{:S(2)}) async-start(bf16[4,40,16,256]{3,2,1,0:T(8,128)(2,1)} %add_convert_fusion), calls=%async_computation.3 | async-start | bytes 2621440 | tf_op jit(solution)/shard_map/all_to_all | solution.py:926
  595.9 24.5 %collective-permute-start.36 = (bf16[4,32,16,256]{3,2,1,0:T(8,128)(2,1)S(1)}, bf16[4,32,16,256]{3,2,1,0:T(8,128)(2,1)S(1)}, u32[]{:S(2)}, u32[]{:S(2)}) collective-permute-start(bf16[4,32,16,256]{3,2,1,0:T(8,128)(2,1)S(1)} %get-tuple-element.178), channel_id=1, source_target_pairs={{0,16},{4,20},{8,24},{12,28},{16,0},{20,4},{24,8},{28,12},{1,17},{... | collective-permute-start | bytes 3145736 | tf_op jit(solution)/shard_map/ppermute | solution.py:584
  624.1 29.3 %all-to-all-start.3 = ((bf16[4,32,16,256]{3,2,1,0:T(8,128)(2,1)}), bf16[4,32,16,256]{3,2,1,0:T(8,128)(2,1)S(1)}, u32[]{:S(2)}, u32[]{:S(2)}) async-start(bf16[4,32,16,256]{3,2,1,0:T(8,128)(2,1)} %add_convert_fusion.1), calls=%async_computation.5 | async-start | bytes 2097152 | tf_op jit(solution)/shard_map/all_to_all | solution.py:926
  633.5 2.7 collective-permute-start.37
  633.6 27.4 %collective-permute-start.40 = (bf16[4,24,16,256]{3,2,1,0:T(8,128)(2,1)}, bf16[4,24,16,256]{3,2,1,0:T(8,128)(2,1)}, u32[]{:S(2)}, u32[]{:S(2)}) collective-permute-start(bf16[4,24,16,256]{3,2,1,0:T(8,128)(2,1)} %get-tuple-element.189), channel_id=1, source_target_pairs={{0,16},{4,20},{8,24},{12,28},{16,0},{20,4},{24,8},{28,12},{1,17},{... | collective-permute-start | bytes 2359304 | tf_op jit(solution)/shard_map/ppermute | solution.py:584
  654.3 24.4 %collective-permute-start.38 = (bf16[512,1024]{1,0:T(8,128)(2,1)}, bf16[512,1024]{1,0:T(8,128)(2,1)}, u32[]{:S(2)}, u32[]{:S(2)}) collective-permute-start(bf16[512,1024]{1,0:T(8,128)(2,1)} %fusion.45), channel_id=1, source_target_pairs={{0,8},{4,12},{8,0},{12,4},{16,24},{20,28},{24,16},{28,20},{1,9},{5... | collective-permute-start | bytes 3145736 | tf_op jit(solution)/shard_map/ppermute | solution.py:584
  663.4 23.8 %all-to-all-start.4 = ((bf16[4,24,16,256]{3,2,1,0:T(8,128)(2,1)}), bf16[4,24,16,256]{3,2,1,0:T(8,128)(2,1)S(1)}, u32[]{:S(2)}, u32[]{:S(2)}) async-start(bf16[4,24,16,256]{3,2,1,0:T(8,128)(2,1)} %add_convert_fusion.3), calls=%async_computation.6 | async-start | bytes 1572864 | tf_op jit(solution)/shard_map/all_to_all | solution.py:926
  679.9 8.2 %collective-permute-start.39 = (bf16[512,1024]{1,0:T(8,128)(2,1)}, bf16[512,1024]{1,0:T(8,128)(2,1)}, u32[]{:S(2)}, u32[]{:S(2)}) collective-permute-start(bf16[512,1024]{1,0:T(8,128)(2,1)} %slice.347), channel_id=1, source_target_pairs={{0,4},{4,0},{8,12},{12,8},{16,20},{20,16},{24,28},{28,24},{1,5},{5... | collective-permute-start | bytes 3145736 | tf_op jit(solution)/shard_map/ppermute | solution.py:584
  684.3 8.9 %collective-permute-start.43 = (bf16[20,16,256]{2,1,0:T(8,128)(2,1)}, bf16[20,16,256]{2,1,0:T(8,128)(2,1)S(1)}, u32[]{:S(2)}, u32[]{:S(2)}) collective-permute-start(bf16[20,16,256]{2,1,0:T(8,128)(2,1)} %get-tuple-element.247), channel_id=1, source_target_pairs={{0,4},{4,0},{8,12},{12,8},{16,20},{20,16},{24,28},{28,24},{1,5},{5... | collective-permute-start | bytes 491528 | tf_op jit(solution)/shard_map/ppermute | solution.py:584
  684.9 8.4 %collective-permute-start.44 = (bf16[20,16,256]{2,1,0:T(8,128)(2,1)}, bf16[20,16,256]{2,1,0:T(8,128)(2,1)S(1)}, u32[]{:S(2)}, u32[]{:S(2)}) collective-permute-start(bf16[20,16,256]{2,1,0:T(8,128)(2,1)} %get-tuple-element.248), channel_id=1, source_target_pairs={{0,8},{4,12},{8,0},{12,4},{16,24},{20,28},{24,16},{28,20},{1,9},{5... | collective-permute-start | bytes 491528 | tf_op jit(solution)/shard_map/ppermute | solution.py:584
  686.4 7.5 collective-permute-start.45
  698.4 32.1 %all-to-all-start.5 = ((bf16[8,528,256]{2,1,0:T(8,128)(2,1)}), bf16[8,528,256]{2,1,0:T(8,128)(2,1)}, u32[]{:S(2)}, u32[]{:S(2)}) async-start(bf16[8,528,256]{2,1,0:T(8,128)(2,1)} %place.1), calls=%async_computation.7 | async-start | bytes 4325376 | tf_op jit(solution)/shard_map/all_to_all | solution.py:1069
  705.4 0.8 collective-permute-start.41
  706.1 12.6 %collective-permute-start.42 = (bf16[256,1024]{1,0:T(8,128)(2,1)S(1)}, bf16[256,1024]{1,0:T(8,128)(2,1)S(1)}, u32[]{:S(2)}, u32[]{:S(2)}) collective-permute-start(bf16[256,1024]{1,0:T(8,128)(2,1)S(1)} %get-tuple-element.227), channel_id=1, source_target_pairs={{1,0},{17,16},{0,1},{16,17},{5,2},{21,18},{4,3},{20,19},{3,4},{19,... | collective-permute-start | bytes 1572872 | tf_op jit(solution)/shard_map/ppermute | solution.py:634
  732.0 22.9 %all-to-all-start.6 = ((f32[4,1,512]{2,1,0:T(1,128)}), f32[4,1,512]{2,1,0:T(1,128)S(1)}, u32[]{:S(2)}, u32[]{:S(2)}) async-start(f32[4,1,512]{2,1,0:T(1,128)} %all_to_all.34), calls=%async_computation.8 | async-start | bytes 16384 | tf_op jit(solution)/shard_map/all_to_all | solution.py:1072
  (102 other events, 621.8 us)
Sparse Core Ops, SparseCore 0:
  79.6 92.1 all-gather.4
  173.9 109.4 all-gather.6
  388.9 97.1 reduce-scatter.2
  501.8 69.3 reduce-scatter.4
